TPU v7x, 32 devices: a whole 2x2x4 slice. The times are simulated.
32 devices in a mesh: dp: 8 (over y, x, core), tensor: 4 (over z).
Axes of the slice: x: 2, y: 2, z: 4, core: 2. Of those that a mesh axis runs over, the one named last changes fastest.
Arguments:
- tokens: bfloat16 [15872, 768], P('dp'), may hold values from -6 to 6
- slot_kind: int32 [32], P('dp'), may hold values from 0 to 1
- offset_bucket: int32 [991], replicated, may hold values from 0 to 319
- w_query: bfloat16 [768, 768], P(None, 'tensor'), may hold values from -0.21875 to 0.21875
- b_query: bfloat16 [768], P('tensor'), may hold values from -2 to 2
- w_key: bfloat16 [768, 768], P(None, 'tensor'), may hold values from -0.21875 to 0.21875
- w_value: bfloat16 [768, 768], P(None, 'tensor'), may hold values from -0.21875 to 0.21875
- b_value: bfloat16 [768], P('tensor'), may hold values from -2 to 2
- w_out: bfloat16 [768, 768], P('tensor'), may hold values from -1.25 to 1.25
- b_out: bfloat16 [768], replicated, may hold values from -2 to 2
- gate_weight: bfloat16 [64, 8], replicated, may hold values from -0.75 to 0.75
- gate_bias: bfloat16 [8], replicated, may hold values from -2 to 2
- gate_scale: bfloat16 [12], P('tensor'), may hold values from 0.5 to 2
- rel_table: bfloat16 [320, 12], P(None, 'tensor'), may hold values from -4 to 4
- norm1_gain: bfloat16 [768], replicated, may hold values from 0.099609375 to 1.8984375
- norm1_bias: bfloat16 [768], replicated, may hold values from -2 to 2
- w_inner: bfloat16 [768, 3072], P(None, 'tensor'), may hold values from -0.21875 to 0.21875
- b_inner: bfloat16 [3072], P('tensor'), may hold values from -2 to 2
- w_outer: bfloat16 [3072, 768], P('tensor'), may hold values from -0.15625 to 0.15625
- b_outer: bfloat16 [768], replicated, may hold values from -2 to 2
- norm2_gain: bfloat16 [768], replicated, may hold values from 0.099609375 to 1.8984375
- norm2_bias: bfloat16 [768], replicated, may hold values from -2 to 2
- cotangent: bfloat16 [15872, 768], P('dp'), may hold values from -6 to 6
Outputs:
- output: bfloat16 [15872, 768], P('dp')
- grad_tokens: bfloat16 [15872, 768], P('dp')
- grad_w_query: float32 [768, 768], P(None, 'tensor')
- grad_b_query: float32 [768], P('tensor')
- grad_w_key: float32 [768, 768], P(None, 'tensor')
- grad_w_value: float32 [768, 768], P(None, 'tensor')
- grad_b_value: float32 [768], P('tensor')
- grad_w_out: float32 [768, 768], P('tensor')
- grad_b_out: float32 [768], replicated
- grad_gate_weight: float32 [64, 8], replicated
- grad_gate_bias: float32 [8], replicated
- grad_gate_scale: float32 [12], P('tensor')
- grad_rel_table: float32 [320, 12], P(None, 'tensor')
- grad_norm1_gain: float32 [768], replicated
- grad_norm1_bias: float32 [768], replicated
- grad_w_inner: float32 [768, 3072], P(None, 'tensor')
- grad_b_inner: float32 [3072], P('tensor')
- grad_w_outer: float32 [3072, 768], P('tensor')
- grad_b_outer: float32 [768], replicated
- grad_norm2_gain: float32 [768], replicated
- grad_norm2_bias: float32 [768], replicated
Inputs may be any that keep to these rules, and one draw needn't show every extreme that they name: `slot_kind`: 0: the slot holds one clip of 496 patches; 1: it holds two clips of 248 patches, each attending only within itself. `offset_bucket`: entry d + 495 is the bucket of a key d positions after its query.
All inputs are finite; a program needn't handle non-finite values.
Results may differ from a plain program's by a relative error of at most 0.035.
Values may be sent and summed in bfloat16 or wider, within the bound.
A program may use at most 192 MiB of HBM per device.

v0:
```python
import math

import jax
import jax.numpy as jnp
from jax import lax
from jax.sharding import PartitionSpec as P

HEAD = 64
SEQ = 496


highest = lax.Precision.HIGHEST
residual_scale = 24.0**0.25
norm_epsilon = 1e-05


def matmul(left, right):
    return jnp.dot(left, right, preferred_element_type=jnp.float32)


def left_product(left, right):
    return lax.dot_general(
        left, right, (((0,), (0,)), ((), ())), preferred_element_type=jnp.float32
    )


def right_product(left, right):
    return lax.dot_general(
        left, right, (((1,), (1,)), ((), ())), preferred_element_type=jnp.float32
    )


def layer_stats(values):
    centered = values - jnp.mean(values, -1, keepdims=True)
    inverse = lax.rsqrt(jnp.mean(centered * centered, -1, keepdims=True) + norm_epsilon)
    return (centered * inverse, inverse)


def norm_back(grad_normed, normed, inverse):
    return inverse * (
        grad_normed
        - jnp.mean(grad_normed, -1, keepdims=True)
        - normed * jnp.mean(grad_normed * normed, -1, keepdims=True)
    )


def gelu_exact(values):
    return jax.nn.gelu(values, approximate=False)


def keep_same(values):
    return values


def expand(offset_values):
    head_rows = jnp.transpose(offset_values)
    padded = jnp.pad(head_rows, ((0, 0), (0, 1)))
    tiled = jnp.tile(padded, (1, SEQ))
    stride = 2 * SEQ - 1
    skewed = tiled[:, : SEQ * stride].reshape(head_rows.shape[0], SEQ, stride)
    return skewed[:, :, SEQ - 1 :]


def layer(tok, kinds, upstream_in, offset_bucket, weights, shared, hooks):
    (
        w_query,
        b_query,
        w_key,
        w_value,
        b_value,
        w_out,
        gate_scale,
        rel_table,
        w_inner,
        b_inner,
        w_outer,
    ) = weights
    b_out, gate_weight, gate_bias, norm1_gain, norm1_bias, b_outer, norm2_gain, norm2_bias = shared
    sum_attention, sum_ffn, sum_ffn_back, sum_input, finish_ffn = hooks
    rows = tok.shape[0]
    slots = rows // SEQ
    local_heads = gate_scale.shape[0]
    local_width = local_heads * HEAD
    shape_four = (slots, SEQ, local_heads, HEAD)
    scaling = 1.0 / math.sqrt(HEAD)
    query_rows = ((matmul(tok, w_query) + b_query.astype(jnp.float32)) * scaling).astype(
        jnp.bfloat16
    )
    key_rows = matmul(tok, w_key).astype(jnp.bfloat16)
    value_rows = (matmul(tok, w_value) + b_value.astype(jnp.float32)).astype(jnp.bfloat16)
    query_four = query_rows.reshape(shape_four)
    key_four = key_rows.reshape(shape_four)
    value_four = value_rows.reshape(shape_four)
    own_columns = tok.astype(jnp.float32).reshape(shape_four)
    gate_matrix = gate_weight.astype(jnp.float32)
    gate_logits = jnp.einsum(
        "sihd,de->sihe", own_columns, gate_matrix, precision=highest
    ) + gate_bias.astype(jnp.float32)
    first_gate = jax.nn.sigmoid(jnp.sum(gate_logits[..., :4], -1))
    second_gate = jax.nn.sigmoid(jnp.sum(gate_logits[..., 4:], -1))
    head_factor = gate_scale.astype(jnp.float32)
    gate_value = first_gate * (second_gate * head_factor - 1.0) + 2.0
    gate_heads = jnp.transpose(gate_value, (0, 2, 1))[..., None]
    position = lax.iota(jnp.int32, SEQ)
    bucket_onehot = (
        offset_bucket[:, None] == lax.iota(jnp.int32, rel_table.shape[0])[None, :]
    ).astype(jnp.float32)
    offset_bias = jnp.dot(bucket_onehot, rel_table.astype(jnp.float32), precision=highest)
    position_bias, expand_pull = jax.vjp(expand, offset_bias)
    half_length = SEQ // 2
    same_half = position[:, None] // half_length == position[None, :] // half_length
    allowed = (kinds[:, None, None] == 0) | same_half[None]
    scores = jnp.einsum("sihd,sjhd->shij", query_four, key_four, preferred_element_type=jnp.float32)
    scores = scores + gate_heads * position_bias[None]
    scores = jnp.where(allowed[:, None], scores, -1e30)
    probs = jax.nn.softmax(scores, axis=-1)
    probs_low = probs.astype(jnp.bfloat16)
    mixed = jnp.einsum("shij,sjhd->sihd", probs_low, value_four, preferred_element_type=jnp.float32)
    mixed = mixed.reshape(rows, local_width).astype(jnp.bfloat16)
    attention = sum_attention(matmul(mixed, w_out)) + b_out.astype(jnp.float32)
    gain_one = norm1_gain.astype(jnp.float32)
    normed_one, inverse_one = layer_stats(residual_scale * tok.astype(jnp.float32) + attention)
    hidden_one = normed_one * gain_one + norm1_bias.astype(jnp.float32)
    hidden_low = hidden_one.astype(jnp.bfloat16)
    inner = matmul(hidden_low, w_inner) + b_inner.astype(jnp.float32)
    activated = gelu_exact(inner).astype(jnp.bfloat16)
    branch = sum_ffn(matmul(activated, w_outer)) + b_outer.astype(jnp.float32)
    gain_two = norm2_gain.astype(jnp.float32)
    normed_two, inverse_two = layer_stats(residual_scale * hidden_one + branch)
    output = (normed_two * gain_two + norm2_bias.astype(jnp.float32)).astype(jnp.bfloat16)
    upstream = upstream_in.astype(jnp.float32)
    grad_norm2_gain = jnp.sum(upstream * normed_two, 0)
    grad_norm2_bias = jnp.sum(upstream, 0)
    grad_two = norm_back(upstream * gain_two, normed_two, inverse_two)
    grad_branch = grad_two.astype(jnp.bfloat16)
    grad_b_outer = jnp.sum(grad_branch.astype(jnp.float32), 0)
    grad_w_outer = left_product(activated, grad_branch)
    grad_activated = right_product(grad_branch, w_outer)
    gelu_pull = jax.vjp(gelu_exact, inner)[1]
    grad_inner = gelu_pull(grad_activated)[0].astype(jnp.bfloat16)
    grad_b_inner = jnp.sum(grad_inner.astype(jnp.float32), 0)
    grad_w_inner = left_product(hidden_low, grad_inner)
    ffn_done = finish_ffn(
        (grad_w_inner, grad_b_inner, grad_w_outer, grad_b_outer, grad_norm2_gain, grad_norm2_bias)
    )
    grad_hidden = residual_scale * grad_two + sum_ffn_back(right_product(grad_inner, w_inner))
    grad_norm1_gain = jnp.sum(grad_hidden * normed_one, 0)
    grad_norm1_bias = jnp.sum(grad_hidden, 0)
    grad_one = norm_back(grad_hidden * gain_one, normed_one, inverse_one)
    grad_attention = grad_one.astype(jnp.bfloat16)
    grad_b_out = jnp.sum(grad_attention.astype(jnp.float32), 0)
    grad_w_out = left_product(mixed, grad_attention)
    grad_mixed = right_product(grad_attention, w_out).astype(jnp.bfloat16).reshape(shape_four)
    grad_values = jnp.einsum(
        "shij,sihd->sjhd", probs_low, grad_mixed, preferred_element_type=jnp.float32
    ).astype(jnp.bfloat16)
    grad_probs = jnp.einsum(
        "sihd,sjhd->shij", grad_mixed, value_four, preferred_element_type=jnp.float32
    )
    grad_scores = probs * (grad_probs - jnp.sum(grad_probs * probs, -1, keepdims=True))
    grad_scores_low = grad_scores.astype(jnp.bfloat16)
    grad_query = jnp.einsum(
        "shij,sjhd->sihd", grad_scores_low, key_four, preferred_element_type=jnp.float32
    ).astype(jnp.bfloat16)
    grad_keys = jnp.einsum(
        "shij,sihd->sjhd", grad_scores_low, query_four, preferred_element_type=jnp.float32
    ).astype(jnp.bfloat16)
    grad_bias = grad_scores_low.astype(jnp.float32)
    grad_gate = jnp.transpose(jnp.sum(grad_bias * position_bias[None], -1), (0, 2, 1))
    grad_position = jnp.sum(grad_bias * gate_heads, 0)
    grad_offset = expand_pull(grad_position)[0]
    grad_rel_table = jnp.dot(bucket_onehot.T, grad_offset, precision=highest)
    grad_gate_scale = jnp.sum(grad_gate * first_gate * second_gate, (0, 1))
    grad_first_logit = (
        grad_gate * (second_gate * head_factor - 1.0) * first_gate * (1.0 - first_gate)
    )
    grad_second_logit = grad_gate * first_gate * head_factor * second_gate * (1.0 - second_gate)
    wide_shape = grad_gate.shape + (4,)
    grad_logits = jnp.concatenate(
        [
            jnp.broadcast_to(grad_first_logit[..., None], wide_shape),
            jnp.broadcast_to(grad_second_logit[..., None], wide_shape),
        ],
        -1,
    )
    grad_gate_weight = jnp.einsum("sihd,sihe->de", own_columns, grad_logits, precision=highest)
    grad_gate_bias = jnp.sum(grad_logits, (0, 1, 2))
    grad_own = jnp.einsum("sihe,de->sihd", grad_logits, gate_matrix, precision=highest).reshape(
        rows, local_width
    )
    grad_pre = (grad_query * scaling).reshape(rows, local_width)
    grad_key_flat = grad_keys.reshape(rows, local_width)
    grad_value_flat = grad_values.reshape(rows, local_width)
    grad_b_query = jnp.sum(grad_pre.astype(jnp.float32), 0)
    grad_w_query = left_product(tok, grad_pre)
    grad_w_key = left_product(tok, grad_key_flat)
    grad_w_value = left_product(tok, grad_value_flat)
    grad_b_value = jnp.sum(grad_value_flat.astype(jnp.float32), 0)
    input_part = (
        right_product(grad_pre, w_query)
        + right_product(grad_key_flat, w_key)
        + right_product(grad_value_flat, w_value)
    )
    own_slice = input_part + grad_own
    input_part = own_slice
    input_summed, gate_weight_summed, gate_bias_summed = sum_input(
        (input_part, grad_gate_weight, grad_gate_bias)
    )
    grad_tokens = (residual_scale * grad_one + input_summed).astype(jnp.bfloat16)
    attn_parts = (
        grad_w_query,
        grad_b_query,
        grad_w_key,
        grad_w_value,
        grad_b_value,
        grad_w_out,
        grad_b_out,
        gate_weight_summed,
        gate_bias_summed,
        grad_gate_scale,
        grad_rel_table,
        grad_norm1_gain,
        grad_norm1_bias,
    )
    return (output, grad_tokens, ffn_done, attn_parts)


def body(
    tokens,
    slot_kind,
    offset_bucket,
    w_query,
    b_query,
    w_key,
    w_value,
    b_value,
    w_out,
    b_out,
    gate_weight,
    gate_bias,
    gate_scale,
    rel_table,
    norm1_gain,
    norm1_bias,
    w_inner,
    b_inner,
    w_outer,
    b_outer,
    norm2_gain,
    norm2_bias,
    cotangent,
):
    shared = (
        b_out,
        gate_weight,
        gate_bias,
        norm1_gain,
        norm1_bias,
        b_outer,
        norm2_gain,
        norm2_bias,
    )
    weights = (
        lax.all_gather(w_query, "tensor", axis=1, tiled=True),
        lax.all_gather(b_query, "tensor", axis=0, tiled=True),
        lax.all_gather(w_key, "tensor", axis=1, tiled=True),
        lax.all_gather(w_value, "tensor", axis=1, tiled=True),
        lax.all_gather(b_value, "tensor", axis=0, tiled=True),
        lax.all_gather(w_out, "tensor", axis=0, tiled=True),
        lax.all_gather(gate_scale, "tensor", axis=0, tiled=True),
        lax.all_gather(rel_table, "tensor", axis=1, tiled=True),
        lax.all_gather(w_inner, "tensor", axis=1, tiled=True),
        lax.all_gather(b_inner, "tensor", axis=0, tiled=True),
        lax.all_gather(w_outer, "tensor", axis=0, tiled=True),
    )
    share_rows = tokens.shape[0] // lax.axis_size("tensor")
    share_slots = share_rows // SEQ
    member = lax.axis_index("tensor")
    local_tokens = lax.dynamic_slice_in_dim(tokens, member * share_rows, share_rows, 0)
    local_upstream = lax.dynamic_slice_in_dim(cotangent, member * share_rows, share_rows, 0)
    local_kinds = lax.dynamic_slice_in_dim(slot_kind, member * share_slots, share_slots, 0)

    def ffn_local(grads):
        sharded = (
            lax.psum_scatter(
                grads[0].astype(jnp.bfloat16), "tensor", scatter_dimension=1, tiled=True
            ).astype(jnp.float32),
            lax.psum_scatter(
                grads[1].astype(jnp.bfloat16), "tensor", scatter_dimension=0, tiled=True
            ).astype(jnp.float32),
            lax.psum_scatter(
                grads[2].astype(jnp.bfloat16), "tensor", scatter_dimension=0, tiled=True
            ).astype(jnp.float32),
        )
        common = lax.psum((grads[3], grads[4], grads[5]), "tensor")
        return (sharded[0], sharded[1], sharded[2], common[0], common[1], common[2])

    def finish_ffn(grads):
        reduced = ffn_local(grads)
        return reduced

    hooks = (keep_same, keep_same, keep_same, keep_same, finish_ffn)
    output, grad_tokens, ffn_done, attn_parts = layer(
        local_tokens, local_kinds, local_upstream, offset_bucket, weights, shared, hooks
    )
    output, grad_tokens = (
        lax.all_gather(output, "tensor", axis=0, tiled=True),
        lax.all_gather(grad_tokens, "tensor", axis=0, tiled=True),
    )
    sharded = (
        lax.psum_scatter(attn_parts[0], "tensor", scatter_dimension=1, tiled=True),
        lax.psum_scatter(attn_parts[1], "tensor", scatter_dimension=0, tiled=True),
        lax.psum_scatter(attn_parts[2], "tensor", scatter_dimension=1, tiled=True),
        lax.psum_scatter(attn_parts[3], "tensor", scatter_dimension=1, tiled=True),
        lax.psum_scatter(attn_parts[4], "tensor", scatter_dimension=0, tiled=True),
        lax.psum_scatter(attn_parts[5], "tensor", scatter_dimension=0, tiled=True),
        lax.psum_scatter(attn_parts[9], "tensor", scatter_dimension=0, tiled=True),
        lax.psum_scatter(attn_parts[10], "tensor", scatter_dimension=1, tiled=True),
    )
    common = lax.psum(
        (attn_parts[6], attn_parts[7], attn_parts[8], attn_parts[11], attn_parts[12]), "tensor"
    )
    summed = lax.psum(
        (
            sharded[0],
            sharded[1],
            sharded[2],
            sharded[3],
            sharded[4],
            sharded[5],
            common[0],
            common[1],
            common[2],
            sharded[6],
            sharded[7],
            common[3],
            common[4],
            ffn_done[0],
            ffn_done[1],
            ffn_done[2],
            ffn_done[3],
            ffn_done[4],
            ffn_done[5],
        ),
        "dp",
    )
    a_sum = summed[:13]
    f_sum = summed[13:]
    return (
        output,
        grad_tokens,
        a_sum[0],
        a_sum[1],
        a_sum[2],
        a_sum[3],
        a_sum[4],
        a_sum[5],
        a_sum[6],
        a_sum[7],
        a_sum[8],
        a_sum[9],
        a_sum[10],
        a_sum[11],
        a_sum[12],
        f_sum[0],
        f_sum[1],
        f_sum[2],
        f_sum[3],
        f_sum[4],
        f_sum[5],
    )


def solution(mesh):
    in_specs = (
        P("dp", None),
        P("dp"),
        P(),
        P(None, "tensor"),
        P("tensor"),
        P(None, "tensor"),
        P(None, "tensor"),
        P("tensor"),
        P("tensor", None),
        P(),
        P(),
        P(),
        P("tensor"),
        P(None, "tensor"),
        P(),
        P(),
        P(None, "tensor"),
        P("tensor"),
        P("tensor", None),
        P(),
        P(),
        P(),
        P("dp", None),
    )
    out_specs = (
        P("dp", None),
        P("dp", None),
        P(None, "tensor"),
        P("tensor"),
        P(None, "tensor"),
        P(None, "tensor"),
        P("tensor"),
        P("tensor", None),
        P(),
        P(),
        P(),
        P("tensor"),
        P(None, "tensor"),
        P(),
        P(),
        P(None, "tensor"),
        P("tensor"),
        P("tensor", None),
        P(),
        P(),
        P(),
    )
    return jax.shard_map(body, mesh=mesh, in_specs=in_specs, out_specs=out_specs, check_vma=False)
```

profile of v0, /device:TPU:0, one launch (start us, length us, event | category | flops | bytes accessed | tf_op | source)
XLA Modules:
  0.0 982.2 jit_solution(13247593238140962737)
XLA Ops:
  14.1 13.9 %all-reduce.14 = (bf16[768]{0:T(1024)(128)(2,1)S(1)}, bf16[12]{0:T(256)(128)(2,1)S(1)}, bf16[768]{0:T(1024)(128)(2,1)S(1)}) all-reduce(bf16[768]{0:T(1024)(128)(2,1)S(1)} %dynamic-update-slice, bf16[12]{0:T(256)(128)(2,1)S(1)} %dynamic-update-slice.2, bf16[768]{0:T(1024)(128)(2,1)S(1)} %dynamic-update-slice.1), channel_id=1, replica_groups=mesh['dp'=8,'tensor'=4] {'tensor'}, use_global_device_ids=true, to_apply=%add.3 | all-reduce | flops 1548 | bytes 6192
  29.3 13.2 %all-gather.1 = bf16[4,1,768]{2,1,0:T(2,128)(2,1)S(1)} all-gather(bf16[1,1,768]{2,1,0:T(2,128)(2,1)S(1)} %reshape.478), channel_id=1, replica_groups=mesh['dp'=8,'tensor'=4] {'tensor'}, dimensions={0}, use_global_device_ids=true | all-gather | bytes 7680 | tf_op jit(solution)/shard_map/all_gather | solution.py:273
  42.5 13.2 %all-gather = bf16[4,3,320]{2,1,0:T(4,128)(2,1)S(1)} all-gather(bf16[1,3,320]{2,1,0:T(4,128)(2,1)S(1)} %bitcast.177), channel_id=1, replica_groups=mesh['dp'=8,'tensor'=4] {'tensor'}, dimensions={0}, use_global_device_ids=true | all-gather | bytes 9600 | tf_op jit(solution)/shard_map/all_gather | solution.py:271
  58.9 11.3 %tile.4 = f32[12,496,992]{2,1,0:T(8,128)} broadcast(f32[12,992]{1,0:T(8,128)S(1)} %pad.15), dimensions={0,2} | broadcast | bytes 23665152 | tf_op jit(solution)/shard_map/jvp()/tile | solution.py:58
  70.2 41.4 %tile.10 = f32[12,492032]{1,0:T(8,128)} reshape(f32[12,496,992]{2,1,0:T(8,128)} %tile.4) | data formatting | bytes 47235072 | tf_op jit(solution)/shard_map/jvp()/tile | solution.py:58
  111.5 21.8 %slice.19 = f32[12,491536]{1,0:T(8,128)} slice(f32[12,492032]{1,0:T(8,128)} %tile.10), slice={[0:12], [0:491536]} | slice | bytes 47187456 | tf_op jit(solution)/shard_map/jvp()/slice | solution.py:60
  133.3 40.9 %reshape.458 = f32[12,496,991]{2,1,0:T(8,128)} reshape(f32[12,491536]{1,0:T(8,128)} %slice.19) | data formatting | bytes 47187456 | tf_op jit(solution)/shard_map/jvp()/reshape | solution.py:60
  174.2 13.0 %slice.20 = f32[12,496,496]{2,1,0:T(8,128)} slice(f32[12,496,991]{2,1,0:T(8,128)} %reshape.458), slice={[0:12], [0:496], [495:991]} | slice | bytes 23617536 | tf_op jit(solution)/shard_map/jvp()/slice | solution.py:61
  187.2 12.5 %copy.86 = f32[12,496,496]{1,2,0:T(8,128)} copy(f32[12,496,496]{2,1,0:T(8,128)} %slice.20) | data formatting | bytes 23617536
  213.6 11.2 %add_select_fusion = f32[12,496,496]{1,2,0:T(8,128)} fusion(f32[12,496,496]{1,2,0:T(8,128)} %copy.86, f32[12,496]{1,0:T(8,128)S(1)} %fusion.47, pred[496,496]{0,1:T(8,128)(4,1)S(1)} %compare_or_fusion, bf16[496,12,64]{0,2,1:T(8,128)(2,1)S(1)} %bitcast.160, bf16[496,12,64]{0,2,1:T(8,128)(2,1)S(1)} %bitcast.156), kind=kOutput, calls=%fused_computation.7 | convolution fusion | flops 386737152 | bytes 25411072 | tf_op jit(solution)/shard_map/sihd,sjhd->shij/dot_general | solution.py:113
  224.9 14.8 %fusion.69 = (f32[12,496]{1,0:T(8,128)S(1)}, f32[12,496,496]{1,2,0:T(8,128)}) fusion(f32[12,496,496]{1,2,0:T(8,128)} %add_select_fusion), kind=kOutput, calls=%fused_computation.136 | output fusion | flops 5904879 | bytes 23641344 | tf_op jit(solution)/shard_map/sub | solution.py:116
  239.6 12.1 %fusion.21 = bf16[12,64,496]{2,1,0:T(8,128)(2,1)} fusion(bf16[496,12,64]{0,2,1:T(8,128)(2,1)} %bitcast.171, f32[12,496]{1,0:T(8,128)S(1)} %get-tuple-element.79, f32[12,496,496]{1,2,0:T(8,128)} %add_select_fusion), kind=kOutput, calls=%fused_computation.64 | convolution fusion | flops 387124512 | bytes 13356288 | tf_op jit(solution)/shard_map/shij,sjhd->sihd/dot_general | solution.py:118
  254.6 19.4 %multiply_convert_fusion.1 = (bf16[496,3072]{1,0:T(8,128)(2,1)}, f32[496,3072]{1,0:T(8,128)}, f32[496,3072]{1,0:T(8,128)}) fusion(f32[3072]{0:T(1024)S(1)} %bitcast.175, bf16[768,3072]{1,0:T(8,128)(2,1)} %all-gather.19.cloned.1.call-done, f32[496,768]{1,0:T(8,128)S(1)} %get-tuple-element.82, f32[768]{0:T(1024)S(1)} %convert_element_type.171, ...), kind=kOutput, calls=%fused_computation.11 | convolution fusion | flops 2442891264 | bytes 21501824 | tf_op jit(solution)/shard_map/dot_general | solution.py:18
  273.9 42.0 %all-gather.21.cloned.1.call-done = bf16[3072,768]{1,0:T(8,128)(2,1)} async-done(((bf16[768,768]{1,0:T(8,128)(2,1)}), bf16[3072,768]{1,0:T(8,128)(2,1)}) %all-gather.21.cloned.1.call-update) | async-done | bytes 4718608 | tf_op jit(solution)/shard_map/all_gather | solution.py:274
  326.3 9.0 fusion.72
  345.6 12.6 %convert_reduce_fusion.1 = (f32[12,64]{1,0:T(8,128)S(1)}, bf16[12,64,496]{2,1,0:T(8,128)(2,1)}) fusion(bf16[496,12,64]{0,2,1:T(8,128)(2,1)} %bitcast.173, f32[12,496]{1,0:T(8,128)S(1)} %get-tuple-element.79, f32[12,496,496]{1,2,0:T(8,128)} %add_select_fusion), kind=kOutput, calls=%fused_computation.38 | convolution fusion | flops 387885600 | bytes 13359360 | tf_op jit(solution)/shard_map/shij,sihd->sjhd/dot_general | solution.py:154
  361.6 11.8 %multiply_reduce_fusion = (f32[12,496]{1,0:T(8,128)S(1)}, f32[12,496,496]{1,2,0:T(8,128)}) fusion(f32[12,496,496]{1,2,0:T(8,128)} %get-tuple-element.80, f32[12,496]{1,0:T(8,128)S(1)} %get-tuple-element.79, bf16[496,12,64]{0,2,1:T(8,128)(2,1)} %bitcast.174, bf16[496,12,64]{0,2,1:T(8,128)(2,1)} %bitcast.172), kind=kOutput, calls=%fused_computation.5 | convolution fusion | flops 386731200 | bytes 25188864 | tf_op jit(solution)/shard_map/sihd,sjhd->shij/dot_general | solution.py:157
  373.4 12.0 %convert_multiply_fusion = (f32[12,496,496]{1,2,0:T(8,128)}, bf16[12,496,496]{1,2,0:T(8,128)(2,1)S(1)}) fusion(f32[12,496]{1,0:T(8,128)S(1)} %fusion.47, f32[12,496,496]{1,2,0:T(8,128)} %get-tuple-element.88, f32[12,496]{1,0:T(8,128)S(1)} %get-tuple-element.87, f32[12,496,496]{1,2,0:T(8,128)S(1)} %bitcast.155, f32[12,496]{1,0:T(8,128)S(1)} %get-tuple-element.79), kind=kLoop, calls=%fused_computation.1 | loop fusion | flops 17713152 | bytes 41402112 | tf_op jit(solution)/shard_map/mul | solution.py:170
  399.3 8.2 fusion.1
  438.8 50.4 %reduce-scatter.9.cloned.1.call-done = f32[768,192]{0,1:T(8,128)} async-done(((f32[768,768]{0,1:T(8,128)}), f32[768,192]{0,1:T(8,128)}) %reduce-scatter.9.cloned.1.call-update) | async-done | bytes 589840 | tf_op jit(solution)/shard_map/reduce_scatter | solution.py:313
  489.3 50.3 %reduce-scatter.7.cloned.1.call-done = f32[768,192]{0,1:T(8,128)} async-done(((f32[768,768]{0,1:T(8,128)}), f32[768,192]{0,1:T(8,128)}) %reduce-scatter.7.cloned.1.call-update) | async-done | bytes 589840 | tf_op jit(solution)/shard_map/reduce_scatter | solution.py:311
  541.6 12.5 %copy.87 = f32[12,496,496]{2,1,0:T(8,128)} copy(f32[12,496,496]{1,2,0:T(8,128)} %get-tuple-element.67) | data formatting | bytes 23617536
  554.2 15.3 %pad.16.clone = f32[12,496,991]{2,1,0:T(8,128)} pad(f32[12,496,496]{2,1,0:T(8,128)} %copy.87, f32[]{:T(128)} %constant.27.clone.1), padding=0_0x0_0x495_0 | pad | bytes 35402500 | tf_op jit(solution)/shard_map/transpose(jvp())/pad | solution.py:61
  569.5 36.8 %reshape.465 = f32[12,491536]{1,0:T(8,128)} reshape(f32[12,496,991]{2,1,0:T(8,128)} %pad.16.clone) | data formatting | bytes 47187456 | tf_op jit(solution)/shard_map/transpose(jvp())/reshape | solution.py:60
  606.3 23.2 %pad.17 = f32[12,492032]{1,0:T(8,128)} pad(f32[12,491536]{1,0:T(8,128)} %reshape.465, f32[]{:T(128)} %constant.27.clone.1), padding=0_0x0_496 | pad | bytes 47211268 | tf_op jit(solution)/shard_map/transpose(jvp())/pad | solution.py:60
  629.5 36.9 %reshape.466 = f32[12,496,992]{2,1,0:T(8,128)} reshape(f32[12,492032]{1,0:T(8,128)} %pad.17) | data formatting | bytes 47235072 | tf_op jit(solution)/shard_map/transpose(jvp())/reshape | solution.py:58
  666.4 9.8 reduce_sum.259
  677.9 20.8 %all-reduce.13 = (f32[768]{0:T(1024)S(1)}, f32[768]{0:T(1024)S(1)}, f32[768]{0:T(1024)S(1)}, f32[64,8]{0,1:T(8,128)S(1)}, f32[8]{0:T(128)S(1)}, /*index=5*/f32[1...) all-reduce(f32[768]{0:T(1024)S(1)} %reduce_sum.253, ...), channel_id=3, replica_groups=mesh['dp'=8,'tensor'=4] {'tensor'}, use_global_device_ids=true, to_apply=%region_17.18.clone | all-reduce | flops 10516 | bytes 84128
  698.9 13.4 %all-reduce.10 = bf16[3072]{0:T(1024)(128)(2,1)S(1)} all-reduce(bf16[3072]{0:T(1024)(128)(2,1)S(1)} %copy-done.38), channel_id=11, replica_groups=mesh['dp'=8,'tensor'=4] {'tensor'}, use_global_device_ids=true, to_apply=%region_51.52.clone | all-reduce | flops 3072 | bytes 12288
  712.5 41.0 %reduce-scatter.15.cloned.1.call-done = bf16[768,768]{1,0:T(8,128)(2,1)} async-done(((bf16[768,3072]{1,0:T(8,128)(2,1)}), bf16[768,768]{1,0:T(8,128)(2,1)}) %reduce-scatter.15.cloned.1.call-update) | async-done | bytes 1179664 | tf_op jit(solution)/shard_map/reduce_scatter | solution.py:285
  753.4 88.0 %reduce-scatter.17.cloned.1.call-done = bf16[768,768]{1,0:T(8,128)(2,1)} async-done(((bf16[3072,768]{1,0:T(8,128)(2,1)}), bf16[768,768]{1,0:T(8,128)(2,1)}) %reduce-scatter.17.cloned.1.call-update) | async-done | bytes 1179664 | tf_op jit(solution)/shard_map/reduce_scatter | solution.py:291
  841.4 125.3 %all-reduce.19 = (f32[192]{0:T(256)}, f32[192]{0:T(256)}, f32[768]{0:T(1024)}, f32[64,8]{0,1:T(8,128)}, f32[8]{0:T(128)}, /*index=5*/f32[3]{0:T(128)}, f32[320,3...) all-reduce(f32[192]{0:T(256)S(1)} %dynamic-slice.4, ...), channel_id=1, replica_groups=mesh['dp'=8,'tensor'=4] {'dp'}, use_global_device_ids=true, to_apply=%region_18.19 | all-reduce | flops 1186891 | bytes 7135832 | tf_op jit(solution)/shard_map/psum | solution.py:323
  (261 shorter events, 105.3 us)
Async XLA Ops:
  7.2 48.5 %copy-start = (bf16[1984,768]{1,0:T(8,128)(2,1)S(1)}, bf16[1984,768]{1,0:T(8,128)(2,1)}, u32[]{:S(2)}) copy-start(bf16[1984,768]{1,0:T(8,128)(2,1)} %param.23) | copy-start | bytes 9142276
  7.3 20.7 %copy-start.51 = (bf16[768]{0:T(1024)(128)(2,1)S(1)}, bf16[768]{0:T(1024)(128)(2,1)}, u32[]{:S(2)}) copy-start(bf16[768]{0:T(1024)(128)(2,1)} %param.40) | copy-start | bytes 4612
  7.3 20.7 %copy-start.44 = (bf16[768]{0:T(1024)(128)(2,1)S(1)}, bf16[768]{0:T(1024)(128)(2,1)}, u32[]{:S(2)}) copy-start(bf16[768]{0:T(1024)(128)(2,1)} %param.37) | copy-start | bytes 4612
  7.3 20.8 %copy-start.45 = (bf16[768]{0:T(1024)(128)(2,1)S(1)}, bf16[768]{0:T(1024)(128)(2,1)}, u32[]{:S(2)}) copy-start(bf16[768]{0:T(1024)(128)(2,1)} %param.38) | copy-start | bytes 4612
  7.3 20.8 %copy-start.46 = (bf16[768]{0:T(1024)(128)(2,1)S(1)}, bf16[768]{0:T(1024)(128)(2,1)}, u32[]{:S(2)}) copy-start(bf16[768]{0:T(1024)(128)(2,1)} %param.43) | copy-start | bytes 4612
  7.3 21.4 %copy-start.47 = (bf16[768]{0:T(1024)(128)(2,1)S(1)}, bf16[768]{0:T(1024)(128)(2,1)}, u32[]{:S(2)}) copy-start(bf16[768]{0:T(1024)(128)(2,1)} %param.32) | copy-start | bytes 4612
  7.3 21.4 %copy-start.48 = (bf16[768]{0:T(1024)(128)(2,1)S(1)}, bf16[768]{0:T(1024)(128)(2,1)}, u32[]{:S(2)}) copy-start(bf16[768]{0:T(1024)(128)(2,1)} %param.42) | copy-start | bytes 4612
  7.3 21.4 %copy-start.49 = (bf16[768]{0:T(1024)(128)(2,1)S(1)}, bf16[768]{0:T(1024)(128)(2,1)}, u32[]{:S(2)}) copy-start(bf16[768]{0:T(1024)(128)(2,1)} %param.44) | copy-start | bytes 4612
  7.3 35.1 %copy-start.41 = (bf16[320,3]{0,1:T(4,128)(2,1)S(1)}, bf16[320,3]{0,1:T(4,128)(2,1)}, u32[]{:S(2)}) copy-start(bf16[320,3]{0,1:T(4,128)(2,1)} %param.36) | copy-start | bytes 5764
  7.3 194.0 %all-gather.13.cloned.1.call-start = ((), (), s32[]{:S(2)}) async-start(), calls=%async_computation.7 | async-start | bytes 1474560 | tf_op jit(solution)/shard_map/all_gather | solution.py:264
  8.1 195.4 %all-gather.11.cloned.1.call-start = ((), (), s32[]{:S(2)}) async-start(), calls=%async_computation.6 | async-start | bytes 1474560 | tf_op jit(solution)/shard_map/all_gather | solution.py:267
  8.8 197.6 %all-gather.15.cloned.1.call-start = ((), (), s32[]{:S(2)}) async-start(), calls=%async_computation.8 | async-start | bytes 1474560 | tf_op jit(solution)/shard_map/all_gather | solution.py:266
  9.6 48.5 %copy-start.36 = (bf16[64,8]{0,1:T(8,128)(2,1)S(1)}, bf16[64,8]{0,1:T(8,128)(2,1)}, u32[]{:S(2)}) copy-start(bf16[64,8]{0,1:T(8,128)(2,1)} %param.33) | copy-start | bytes 3076
  9.6 242.2 %all-gather.17.cloned.1.call-start = ((), (), s32[]{:S(2)}) async-start(), calls=%async_computation.9 | async-start | bytes 1474560 | tf_op jit(solution)/shard_map/all_gather | solution.py:269
  10.2 244.4 %all-gather.19.cloned.1.call-start = ((), (), s32[]{:S(2)}) async-start(), calls=%async_computation.10 | async-start | bytes 5898240 | tf_op jit(solution)/shard_map/all_gather | solution.py:272
  10.7 47.6 %copy-start.54 = (s32[991]{0:T(1024)S(1)}, s32[991]{0:T(1024)}, u32[]{:S(2)}) copy-start(s32[991]{0:T(1024)} %param.25) | copy-start | bytes 11896
  10.8 305.2 %all-gather.21.cloned.1.call-start = ((), (), s32[]{:S(2)}) async-start(), calls=%async_computation.11 | async-start | bytes 5898240 | tf_op jit(solution)/shard_map/all_gather | solution.py:274
  11.3 424.2 %reduce-scatter.13.cloned.1.call-start = ((), (), s32[]{:S(2)}) async-start(), calls=%async_computation.17 | async-start | bytes 2949120 | tf_op jit(solution)/shard_map/reduce_scatter | solution.py:316
  28.0 173.3 %copy-start.42 = (f32[12]{0:T(128)}, f32[12]{0:T(128)S(1)}, u32[]{:S(2)}) copy-start(f32[12]{0:T(128)S(1)} %convert_element_type.163) | copy-start | bytes 148
  58.4 142.8 %copy-start.26 = (f32[496,12]{0,1:T(8,128)}, f32[496,12]{0,1:T(8,128)S(1)}, u32[]{:S(2)}) copy-start(f32[496,12]{0,1:T(8,128)S(1)} %get-tuple-element.29) | copy-start | bytes 71428
  58.4 142.8 %copy-start.28 = (f32[496,12]{0,1:T(8,128)}, f32[496,12]{0,1:T(8,128)S(1)}, u32[]{:S(2)}) copy-start(f32[496,12]{0,1:T(8,128)S(1)} %get-tuple-element.30) | copy-start | bytes 71428
  209.6 15.2 %copy-start.7 = (bf16[496,768]{0,1:T(8,128)(2,1)}, bf16[496,768]{0,1:T(8,128)(2,1)S(1)}, u32[]{:S(2)}) copy-start(bf16[496,768]{0,1:T(8,128)(2,1)S(1)} %copy.71) | copy-start | bytes 2285572
  254.2 19.7 %copy-start.10 = (f32[496,768]{1,0:T(8,128)}, f32[496,768]{1,0:T(8,128)S(1)}, u32[]{:S(2)}) copy-start(f32[496,768]{1,0:T(8,128)S(1)} %get-tuple-element.82) | copy-start | bytes 4571140
  342.3 96.5 %reduce-scatter.11.cloned.1.call-start = ((), (), s32[]{:S(2)}) async-start(), calls=%async_computation.16 | async-start | bytes 2949120 | tf_op jit(solution)/shard_map/reduce_scatter | solution.py:314
  361.5 127.8 %reduce-scatter.9.cloned.1.call-start = ((), (), s32[]{:S(2)}) async-start(), calls=%async_computation.15 | async-start | bytes 2949120 | tf_op jit(solution)/shard_map/reduce_scatter | solution.py:313
  391.2 148.4 %reduce-scatter.7.cloned.1.call-start = ((), (), s32[]{:S(2)}) async-start(), calls=%async_computation.14 | async-start | bytes 2949120 | tf_op jit(solution)/shard_map/reduce_scatter | solution.py:311
  398.5 313.9 %all-gather.23.cloned.1.call-start = ((), (), s32[]{:S(2)}) async-start(), calls=%async_computation.12 | async-start | bytes 3809280 | tf_op jit(solution)/shard_map/all_gather | solution.py:307
  399.3 313.2 %all-gather.25.cloned.1.call-start = ((), (), s32[]{:S(2)}) async-start(), calls=%async_computation.13 | async-start | bytes 3809280 | tf_op jit(solution)/shard_map/all_gather | solution.py:308
  419.4 334.0 %reduce-scatter.15.cloned.1.call-start = ((), (), s32[]{:S(2)}) async-start(), calls=%async_computation.18 | async-start | bytes 5898240 | tf_op jit(solution)/shard_map/reduce_scatter | solution.py:285
  426.8 414.6 %reduce-scatter.17.cloned.1.call-start = ((), (), s32[]{:S(2)}) async-start(), calls=%async_computation.19 | async-start | bytes 5898240 | tf_op jit(solution)/shard_map/reduce_scatter | solution.py:291
  435.0 531.7 %all-reduce.18.cloned.1.call-start = ((), (), s32[]{:S(2)}) async-start(), calls=%async_computation.20 | async-start | bytes 4718592 | tf_op jit(solution)/shard_map/psum | solution.py:323
  666.4 32.5 %copy-start.38 = (bf16[3072]{0:T(1024)(128)(2,1)S(1)}, bf16[3072]{0:T(1024)(128)(2,1)}, u32[]{:S(2)}) copy-start(bf16[3072]{0:T(1024)(128)(2,1)} %get-tuple-element.93) | copy-start | bytes 18436
  (50 other events, 346.2 us)
Sparse Core Ops, SparseCore 0:
  9.7 33.5 all-gather.12
  44.9 29.6 all-gather.10
  76.1 29.5 all-gather.14
  107.1 29.5 all-gather.16
  138.1 88.5 all-gather.18
  228.1 87.8 all-gather.20
  342.4 46.4 reduce-scatter.12
  391.3 47.5 reduce-scatter.10
  441.7 47.5 reduce-scatter.8
  492.0 47.5 reduce-scatter.6
  541.1 61.3 all-gather.22
  604.0 60.5 all-gather.24
  666.8 86.5 reduce-scatter.14
  755.6 85.7 reduce-scatter.16
  844.7 87.7 all-reduce.17
where the time goes:
time: 988 us; the launch traced here: 982 us
  local copies, waits for them, and re-layouts  293 us (30%)
  waiting for transfers between devices  280 us (28%)
  blocking collectives  200 us (20%)
  matrix products  138 us (14%)
  other arithmetic  52 us (5%)
  between operations  19.1 us (2%)
    psum x1, blocking collectives, body(): lax.psum((sharded[0], sharded[1], sharded[2], sharded[3], sharded[4], sha...  125 us
    reduce_scatter x1, waiting for transfers between devices, ffn_local(): lax.psum_scatter(grads[2].astype(jnp.bfloat16), 'tensor', scatter_dimensi...  88 us
    reshape x2, local copies, waits for them, and re-layouts, expand(): skewed = tiled[:, :SEQ * stride].reshape(head_rows.shape[0], SEQ, stride)  77.7 us
    another operation x2, local copies, waits for them, and re-layouts, expand(): tiled = jnp.tile(padded, (1, SEQ))  52.6 us
    reduce_scatter x1, waiting for transfers between devices, body(): lax.psum_scatter(attn_parts[2], 'tensor', scatter_dimension=1, tiled=True)  50.4 us
    reduce_scatter x1, waiting for transfers between devices, body(): lax.psum_scatter(attn_parts[0], 'tensor', scatter_dimension=1, tiled=True)  50.3 us
    unnamed x3, blocking collectives  48.1 us
    all_gather x1, waiting for transfers between devices, body(): lax.all_gather(w_outer, 'tensor', axis=0, tiled=True)  42 us
  transfers between devices with their start and end apart: 15, of which 6 were waited for; matrix products, arithmetic and copies ran while one was open for 45% of the time, Pallas kernels for 0%

commit v1 on v0

v1 whole, which is shorter than its diff:
```python
import functools
import math

import jax
import jax.numpy as jnp
from jax import lax
from jax.experimental import pallas as pl
from jax.experimental.pallas import tpu as pltpu
from jax.sharding import PartitionSpec as P

HEAD = 64
SEQ = 496
PAD = 512
D = 768
PAIRS = 6
HEADS = 12
BIAS = 1024
NB = 320
VMEM_LIMIT = 64 * 2**20 - 2**16
HALF = SEQ // 2
f32 = jnp.float32
bf16 = jnp.bfloat16
residual_scale = 24.0**0.25
norm_epsilon = 1e-05
highest = lax.Precision.HIGHEST


def dot(a, b, precision=None):
    return lax.dot_general(a, b, (((1,), (0,)), ((), ())), preferred_element_type=f32, precision=precision)


def dot_t(a, b, precision=None):
    return lax.dot_general(a, b, (((1,), (1,)), ((), ())), preferred_element_type=f32, precision=precision)


def dot_l(a, b):
    return lax.dot_general(a, b, (((0,), (0,)), ((), ())), preferred_element_type=f32)


def fold(x):
    return jnp.sum(x.reshape(x.shape[0] // 8, 8, x.shape[1]), axis=0)


def stats(r):
    c = r - jnp.mean(r, -1, keepdims=True)
    inv = lax.rsqrt(jnp.mean(c * c, -1, keepdims=True) + norm_epsilon)
    return c * inv, inv


def norm_back(g, n, inv):
    return inv * (g - jnp.mean(g, -1, keepdims=True) - n * jnp.mean(g * n, -1, keepdims=True))


def wide(ref, i):
    return ref[i].reshape(D, D)


def rows_loop(step, body, carry):
    def go(c, carry):
        return body(pl.ds(pl.multiple_of(c * step, step), step), carry)
    return lax.fori_loop(0, PAD // step, go, carry)


class K:
    pass


def head_mask(hh):
    lane = lax.broadcasted_iota(jnp.int32, (1, 128), 1)
    return jnp.where((lane // HEAD) == hh, 1.0, 0.0).astype(bf16)


def onehot(k):
    return jnp.where(lax.broadcasted_iota(jnp.int32, (NB, BIAS), 0) == k.bucket[...], 1.0, 0.0)


def own_small(k, z):
    table = dot(k.small[0:16, 0:NB], onehot(k).astype(bf16))
    k.sm[z, 0:3, :] = table[0:3]
    k.sm[z, 3:8, :] = k.small[3:8, :].astype(f32)


def mask_build(k, z):
    kind = k.kinds[z].astype(f32)
    def go(rows, _):
        j = lax.broadcasted_iota(jnp.int32, (32, PAD), 0) + rows.start
        i = lax.broadcasted_iota(jnp.int32, (32, PAD), 1)
        far = jnp.where(j < HALF, 0, 1) != jnp.where(i < HALF, 0, 1)
        k.mask[rows, :] = jnp.where(j < SEQ, 0.0, -1e30) + jnp.where(far, -1e30, 0.0) * kind
        return 0
    rows_loop(32, go, 0)


def gate_weights(k):
    gw = k.small[16:24, :].astype(f32)
    first = jnp.sum(gw[0:4], axis=0, keepdims=True)
    second = jnp.sum(gw[4:8], axis=0, keepdims=True)
    own = (lax.broadcasted_iota(jnp.int32, (16, D), 1) // HEAD) == lax.broadcasted_iota(jnp.int32, (16, D), 0)
    wide_first = jnp.where(own, first[:, 0:D], 0.0)
    wide_second = jnp.where(own, second[:, 0:D], 0.0)
    return jnp.concatenate([wide_first, wide_second], axis=0), first[:, D:], second[:, D:], own


def gates(k):
    weights, first_bias, second_bias, _ = gate_weights(k)
    logits = dot_t(weights, k.tok[...].astype(f32), precision=highest)
    spread = lambda b: jnp.concatenate([b, b], axis=1)
    first = jax.nn.sigmoid(logits[0:16] + spread(first_bias))
    second = jax.nn.sigmoid(logits[16:32] + spread(second_bias))
    k.first[...] = first
    k.second[...] = second
    for h in range(HEADS):
        k.factor[h : h + 1, :] = k.sm[h // 3, 5 + h % 3 : 6 + h % 3, 0:PAD]
    value = first * (second * k.factor[...] - 1.0) + 2.0
    for h in range(HEADS):
        k.gate[h] = value[h : h + 1, :]


def bias_tables(k):
    def go(p, _):
        for i in range(3):
            row = jnp.broadcast_to(k.sm[p, i : i + 1, :], (128, BIAS))
            k.bias[p * 3 + i] = pltpu.roll(row, 0, 1, stride=1, stride_axis=0)[:, 0:896].astype(bf16)
        return 0
    lax.fori_loop(0, 4, go, 0)


def small_row(k, row, start):
    return jnp.concatenate([k.sm[p, row : row + 1, start : start + 192] for p in range(4)], axis=1)


def project(k):
    bq = small_row(k, 3, 0)
    bv = small_row(k, 3, 192)
    for t, dest, bias, scale in ((0, k.q, bq, 0.125), (1, k.k, None, None), (2, k.v, bv, None)):
        r = dot_t(k.tok[...], wide(k.wa, t))
        if bias is not None:
            r = r + bias
        if scale is not None:
            r = r * scale
        r = r.astype(bf16)
        for pr in range(PAIRS):
            dest[pr] = r[:, 128 * pr : 128 * pr + 128]


def attend(k, pr):
    qp, kp, vp = k.q[pr], k.k[pr], k.v[pr]
    total = None
    for hh in range(2):
        h = pr * 2 + hh
        hm = head_mask(hh)
        km = kp * hm
        gate = k.gate[h]
        m8 = jnp.full((8, PAD), -3e38, f32)
        for c in range(4):
            s = dot_t(km[128 * c : 128 * c + 128], qp)
            k.s[128 * c : 128 * c + 128, :] = s
        for c in range(16):
            rows = slice(32 * c, 32 * c + 32)
            lane = 384 - 128 * (c // 4)
            t = k.bias[h, 32 * (c % 4) : 32 * (c % 4) + 32, lane : lane + PAD].astype(f32)
            s = k.s[rows, :] + t * gate + k.mask[rows, :]
            k.s[rows, :] = s
            m8 = jnp.maximum(m8, jnp.max(s.reshape(4, 8, PAD), axis=0))
        m = jnp.max(m8, axis=0, keepdims=True)
        l8 = jnp.zeros((8, PAD), f32)
        for c in range(16):
            rows = slice(32 * c, 32 * c + 32)
            e = jnp.exp(k.s[rows, :] - m)
            k.s[rows, :] = e
            l8 = l8 + fold(e)
        inv = 1.0 / jnp.sum(l8, axis=0, keepdims=True)
        for c in range(16):
            rows = slice(32 * c, 32 * c + 32)
            k.p[h, rows, :] = (k.s[rows, :] * inv).astype(bf16)
        part = dot_l(k.p[h], vp * hm)
        total = part if total is None else total + part
    k.mixed[pr] = total.astype(bf16)


def mixed_all(ref):
    return jnp.concatenate([ref[pr] for pr in range(PAIRS)], axis=1)


def vec(k, row):
    return k.small[row : row + 1, 0:D].astype(f32)


def norm_one(k):
    k.fa[...] = dot(mixed_all(k.mixed), wide(k.wa, 3))
    b_out, gain, shift = vec(k, 8), vec(k, 9), vec(k, 10)
    def go(rows, _):
        r = residual_scale * k.tok[rows, :].astype(f32) + k.fa[rows, :] + b_out
        n, inv = stats(r)
        k.n1[rows, :] = n
        k.inv1[rows, :] = jnp.broadcast_to(inv, (32, 128))
        k.hid[rows, :] = (n * gain + shift).astype(bf16)
        return 0
    rows_loop(32, go, 0)


def feed(k, p):
    k.fa[...] = dot(k.hid[...], wide(k.wi, p))
    b = k.sm[p, 4:5, 0:D]
    def go(rows, _):
        x = k.fa[rows, :] + b
        half = 0.5 * (1.0 + lax.erf(x * (1.0 / math.sqrt(2.0))))
        k.act[p, rows, :] = (x * half).astype(bf16)
        k.dg[p, rows, :] = (half + x * (jnp.exp(-0.5 * x * x) * (1.0 / math.sqrt(2.0 * math.pi)))).astype(bf16)
        return 0
    rows_loop(16, go, 0)
    k.fb[...] += dot(k.act[p], wide(k.wo, p))


def feed_init(k):
    k.fb[...] = jnp.zeros((PAD, D), f32)


def norm_two(k):
    b_outer, gain1, shift1, gain2, shift2 = vec(k, 11), vec(k, 9), vec(k, 10), vec(k, 12), vec(k, 13)
    def go(rows, carry):
        g_gain, g_shift, g_b = carry
        r = residual_scale * (k.n1[rows, :] * gain1 + shift1) + k.fb[rows, :] + b_outer
        n, inv = stats(r)
        k.out[rows, :] = (n * gain2 + shift2).astype(bf16)
        up = k.cot[rows, :].astype(f32)
        g2 = norm_back(up * gain2, n, inv)
        low = g2.astype(bf16)
        k.gb[rows, :] = low
        k.fb[rows, :] = residual_scale * g2
        return g_gain + fold(up * n), g_shift + fold(up), g_b + fold(low.astype(f32))
    zero = jnp.zeros((8, D), f32)
    g_gain, g_shift, g_b = rows_loop(32, go, (zero, zero, zero))
    for row, v in ((3, g_b), (4, g_gain), (5, g_shift)):
        k.sg[row : row + 1, 0:D] = jnp.sum(v, axis=0, keepdims=True)


def feed_back(k, p):
    k.fa[...] = dot_t(k.gb[...], wide(k.wo, p))
    def go(rows, acc):
        gi = (k.fa[rows, :] * k.dg[p, rows, :].astype(f32)).astype(bf16)
        k.dg[p, rows, :] = gi
        return acc + fold(gi.astype(f32))
    acc = rows_loop(32, go, jnp.zeros((8, D), f32))
    k.sg[pl.ds(6 + p, 1), 0:D] = jnp.sum(acc, axis=0, keepdims=True)
    k.fb[...] += dot_t(k.dg[p], wide(k.wi, p))
    k.wo[p] = dot_l(k.act[p], k.gb[...]).astype(bf16).reshape(8, 96, D)
    k.wi[p] = dot_l(k.hid[...], k.dg[p]).astype(bf16).reshape(8, 96, D)


def norm_one_back(k):
    gain = vec(k, 9)
    def go(rows, carry):
        g_gain, g_shift, g_b = carry
        gh = k.fb[rows, :]
        n = k.n1[rows, :]
        g1 = norm_back(gh * gain, n, k.inv1[rows, 0:1])
        low = g1.astype(bf16)
        k.gb[rows, :] = low
        k.fb[rows, :] = residual_scale * g1
        return g_gain + fold(gh * n), g_shift + fold(gh), g_b + fold(low.astype(f32))
    zero = jnp.zeros((8, D), f32)
    g_gain, g_shift, g_b = rows_loop(32, go, (zero, zero, zero))
    for row, v in ((0, g_b), (1, g_gain), (2, g_shift)):
        k.sg[row : row + 1, 0:D] = jnp.sum(v, axis=0, keepdims=True)
    gm = dot_t(k.gb[...], wide(k.wa, 3)).astype(bf16)
    for pr in range(PAIRS):
        k.gm[pr] = gm[:, 128 * pr : 128 * pr + 128]


def attend_back(k, pr):
    qp, kp, vp, gm = k.q[pr], k.k[pr], k.v[pr], k.gm[pr]
    tq = tk = tv = None
    for hh in range(2):
        h = pr * 2 + hh
        hm = head_mask(hh)
        vm = vp * hm
        gate = k.gate[h]
        for c in range(4):
            k.s[128 * c : 128 * c + 128, :] = dot_t(vm[128 * c : 128 * c + 128], gm)
        d8 = jnp.zeros((8, PAD), f32)
        for c in range(16):
            rows = slice(32 * c, 32 * c + 32)
            d8 = d8 + fold(k.s[rows, :] * k.p[h, rows, :].astype(f32))
        total = jnp.sum(d8, axis=0, keepdims=True)
        gg = jnp.zeros((8, PAD), f32)
        k.a[...] = jnp.zeros((128, BIAS), f32)
        for c in range(16):
            rows = slice(32 * c, 32 * c + 32)
            part = slice(32 * (c % 4), 32 * (c % 4) + 32)
            lane = 384 - 128 * (c // 4)
            low = (k.p[h, rows, :].astype(f32) * (k.s[rows, :] - total)).astype(bf16)
            k.gs[rows, :] = low
            g = low.astype(f32)
            gg = gg + fold(g * k.bias[h, part, lane : lane + PAD].astype(f32))
            k.a[part, lane : lane + PAD] += g * gate
        k.ggate[h] = jnp.sum(gg, axis=0, keepdims=True)
        acc = k.a[0:8, :]
        for c in range(1, 16):
            acc = acc + pltpu.roll(k.a[8 * c : 8 * c + 8, :], BIAS - 8 * c, 1)
        flat = acc[0:1]
        for b in range(1, 8):
            flat = flat + pltpu.roll(acc, BIAS - b, 1)[b : b + 1]
        k.goff[h] = flat
        gs = k.gs[...]
        pv = dot(k.p[h], gm * hm)
        pq = dot_l(gs, kp * hm)
        pk = dot(gs, qp * hm)
        tv, tq, tk = (pv, pq, pk) if tv is None else (tv + pv, tq + pq, tk + pk)
    k.q[pr] = (tq.astype(bf16) * 0.125).astype(bf16)
    k.k[pr] = tk.astype(bf16)
    k.v[pr] = tv.astype(bf16)


def gate_back(k):
    weights, _, _, own = gate_weights(k)
    ggate = jnp.concatenate([k.ggate[h] for h in range(HEADS)] + [jnp.zeros((4, PAD), f32)], axis=0)
    first, second, factor = k.first[...], k.second[...], k.factor[...]
    df = ggate * (second * factor - 1.0) * first * (1.0 - first)
    ds = ggate * first * factor * second * (1.0 - second)
    dz = jnp.concatenate([df, ds], axis=0)
    gscale = jnp.sum(ggate * first * second, axis=1, keepdims=True)
    gw = dot(dz, k.tok[...].astype(f32), precision=highest)
    pick = lambda v: jnp.sum(jnp.where(own, v, 0.0), axis=0, keepdims=True)
    k.sg[24:25, 0:D] = pick(gw[0:16])
    k.sg[25:26, 0:D] = pick(gw[16:32])
    k.sg[24:25, D:] = jnp.broadcast_to(jnp.sum(jnp.sum(df, axis=0, keepdims=True), axis=1, keepdims=True), (1, 256))
    k.sg[25:26, D:] = jnp.broadcast_to(jnp.sum(jnp.sum(ds, axis=0, keepdims=True), axis=1, keepdims=True), (1, 256))
    goff = jnp.concatenate([k.goff[h] for h in range(HEADS)] + [jnp.zeros((4, BIAS), f32)], axis=0)
    rel = dot_t(goff, onehot(k), precision=highest)
    k.sg[12:24, 0:NB] = rel[0:HEADS]
    k.sg[12:24, 512:640] = jnp.broadcast_to(gscale, (16, 128))[0:HEADS]
    return dot(dz.T, weights)


def grad_input(k):
    k.fa[...] = gate_back(k)
    for t, src in ((0, k.q), (1, k.k), (2, k.v)):
        k.fa[...] += dot(mixed_all(src), wide(k.wa, t))
    def go(rows, _):
        k.gtok[rows, :] = (k.fb[rows, :] + k.fa[rows, :]).astype(bf16)
        return 0
    rows_loop(32, go, 0)


def grad_projections(k):
    for t, src in ((0, k.q), (1, k.k), (2, k.v)):
        g = mixed_all(src)
        if t != 1:
            row = jnp.sum(fold(g.astype(f32)), axis=0, keepdims=True)
            k.sg[10 + t // 2 : 11 + t // 2, 0:D] = row
        k.wa[t] = dot_l(g, k.tok[...]).astype(bf16).reshape(4, 2, 96, D)
    k.wa[3] = dot_l(mixed_all(k.mixed), k.gb[...]).astype(bf16).reshape(4, 2, 96, D)


def each(n, fn, k):
    def go(i, _):
        fn(k, i)
        return 0
    lax.fori_loop(0, n, go, 0)


COMPUTE_SCRATCH = dict(
    tok=((PAD, D), bf16), cot=((PAD, D), bf16), sm=((4, 8, BIAS), f32), mask=((PAD, PAD), f32),
    first=((16, PAD), f32), second=((16, PAD), f32), factor=((16, PAD), f32), gate=((HEADS, 1, PAD), f32),
    bias=((HEADS, 128, 896), bf16), q=((PAIRS, PAD, 128), bf16), k=((PAIRS, PAD, 128), bf16),
    v=((PAIRS, PAD, 128), bf16), s=((PAD, PAD), f32), p=((HEADS, PAD, PAD), bf16), mixed=((PAIRS, PAD, 128), bf16),
    fa=((PAD, D), f32), fb=((PAD, D), f32), n1=((PAD, D), f32), inv1=((PAD, 128), f32), hid=((PAD, D), bf16),
    act=((4, PAD, D), bf16), dg=((4, PAD, D), bf16), out=((PAD, D), bf16), gb=((PAD, D), bf16),
    gm=((PAIRS, PAD, 128), bf16), gs=((PAD, PAD), bf16), a=((128, BIAS), f32), ggate=((HEADS, 1, PAD), f32),
    goff=((HEADS, 1, BIAS), f32), gtok=((PAD, D), bf16), sg=((32, BIAS), f32),
    wa=((4, 4, 2, 96, D), bf16), wi=((4, 8, 96, D), bf16), wo=((4, 8, 96, D), bf16),
)


MESH = pl.DeviceIdType.MESH
BLOCKS = (0, 1, 2)
SEMS = dict(
    wz=(3, 3), w1=(3, 3), w2=(3, 3, 2), w3=(3, 3), sm=(3,), ot=(3,), gt=(3,), r1=(3,), r2=(3, 2), r3=(3,),
    r4=(3, 3), a1=(3,), a2=(3, 2), a3=(3,), sg=(5,),
)
COMM_SCRATCH = dict(
    stage=((3, D, 192), bf16), rb1a=((2, 4, 2, 96, D), bf16), rb1i=((4, 4, 96, D), bf16), rb1o=((4, 4, 96, D), bf16),
    rb2=((3, 2, 4, 96, D), bf16), rb3=((3, 4, 96, D), bf16), rb4=((3, 3, 96, D), bf16), sgr=((5, 32, BIAS), f32),
)


class Net:
    def __init__(self, k):
        self.k = k
        dp, z = lax.axis_index("dp"), lax.axis_index("tensor")
        self.dp, self.z = dp, z
        c, x, y = dp % 2, (dp // 2) % 2, (dp // 4) % 2
        self.c = c
        across_x, across_y = dp + 2 * (1 - 2 * x), dp + 4 * (1 - 2 * y)
        self.core = (dp + 1 - 2 * c, z)
        self.x, self.y = (across_x, z), (across_y, z)
        self.one = ((1 - c) * across_x + c * across_y, z)
        self.two = (c * across_x + (1 - c) * across_y, z)
        at = lambda cc, yy, xx: 4 * cc + 2 * yy + xx
        ex, ey = at(c, y, 1 - x), at(c, 1 - y, x)
        self.e = at(c, y, x)
        self.e1 = (1 - c) * ex + c * ey
        self.e2 = c * ex + (1 - c) * ey
        self.e12 = at(c, 1 - y, 1 - x)

    def ahead(self, dz):
        return (self.z + dz) % 4

    def behind(self, dz):
        return (self.z + 4 - dz) % 4

    def copy(self, name, index, src, dst, device):
        sems = getattr(self.k, "sem_" + name)
        return pltpu.make_async_remote_copy(
            src_ref=src, dst_ref=dst, send_sem=sems.at[(0, *index)], recv_sem=sems.at[(1, *index)],
            device_id=device, device_id_type=MESH,
        )

    def greet(self):
        barrier = pltpu.get_barrier_semaphore()
        peers = [self.core, self.one, self.two] + [(self.dp, self.ahead(dz)) for dz in (1, 2, 3)]
        for peer in peers:
            pl.semaphore_signal(barrier, inc=1, device_id=peer, device_id_type=MESH)
        pl.semaphore_wait(barrier, len(peers))

    def block(self, b):
        return (self.k.wa, self.k.wi, self.k.wo)[b]

    def chunk(self, b, p, e):
        return self.block(b).at[e // 2, p, e % 2] if b == 0 else self.block(b).at[p, e]

    def chunk_all(self, b, e):
        return self.block(b).at[e // 2, :, e % 2] if b == 0 else self.block(b).at[:, e]

    def side(self, b, p, c):
        return self.block(b).at[pl.ds(2 * c, 2), p] if b == 0 else self.block(b).at[p, pl.ds(4 * c, 4)]

    def side_all(self, b, c):
        return self.block(b).at[pl.ds(2 * c, 2)] if b == 0 else self.block(b).at[:, pl.ds(4 * c, 4)]

    def wz(self, b, d):
        ref = self.chunk(b, self.z, self.e)
        return self.copy("wz", (b, d - 1), ref, ref, (self.dp, self.ahead(d)))

    def w1(self, b, d):
        ref = self.chunk(b, self.behind(d), self.e)
        return self.copy("w1", (b, d - 1), ref, ref, self.one)

    def w2(self, b, d, i):
        ref = self.chunk(b, self.behind(d), (self.e, self.e1)[i])
        return self.copy("w2", (b, d - 1, i), ref, ref, self.two)

    def w3(self, b, d):
        ref = self.side(b, self.behind(d), self.c)
        return self.copy("w3", (b, d - 1), ref, ref, self.core)

    def sm(self, d):
        ref = self.k.sm.at[self.z]
        return self.copy("sm", (d - 1,), ref, ref, (self.dp, self.ahead(d)))

    def rows(self, name, d):
        src, dst = (self.k.out, self.k.out_hbm) if name == "ot" else (self.k.gtok, self.k.gtok_hbm)
        at = pl.ds(pl.multiple_of(self.z * SEQ, 16), SEQ)
        return self.copy(name, (d - 1,), src.at[pl.ds(0, SEQ)], dst.at[at], (self.dp, self.ahead(d)))

    def r1(self, b):
        dst = (self.k.rb1a, self.k.rb1i, self.k.rb1o)[b]
        return self.copy("r1", (b,), self.side_all(b, 1 - self.c), dst, self.core)

    def r2(self, b, i):
        return self.copy("r2", (b, i), self.chunk_all(b, (self.e1, self.e12)[i]), self.k.rb2.at[b, i], self.one)

    def r3(self, b):
        return self.copy("r3", (b,), self.chunk_all(b, self.e2), self.k.rb3.at[b], self.two)

    def r4(self, b, d):
        to = self.ahead(d)
        return self.copy("r4", (b, d - 1), self.chunk(b, to, self.e), self.k.rb4.at[b, d - 1], (self.dp, to))

    def result(self, b, e):
        return (self.k.ra, self.k.ri, self.k.ro)[b].at[e]

    def keep(self, b):
        return pltpu.make_async_copy(self.chunk(b, self.z, self.e), self.result(b, self.e), self.k.sem_keep.at[b])

    def a1(self, b):
        return self.copy("a1", (b,), self.chunk(b, self.z, self.e), self.result(b, self.e), self.one)

    def a2(self, b, i):
        src = (self.chunk(b, self.z, self.e), self.result(b, self.e1))[i]
        return self.copy("a2", (b, i), src, self.result(b, (self.e, self.e1)[i]), self.two)

    def a3(self, b):
        ref = self.result(b, pl.ds(4 * self.c, 4))
        return self.copy("a3", (b,), ref, ref, self.core)

    def sg(self, i):
        device = (self.core, self.x, self.y, (self.dp, self.flip(1)), (self.dp, self.flip(2)))[i]
        return self.copy("sg", (i,), self.k.sg if i == 0 else self.k.sgs.at[i - 1], self.k.sgr.at[i], device)

    def flip(self, bit):
        return self.z + bit * (1 - 2 * ((self.z // bit) % 2))


def loop(n, fn):
    def go(i, _):
        fn(i)
        return 0
    lax.fori_loop(0, n, go, 0)


def weight_stage(net, b, stage):
    for d in (1, 3, 2):
        if stage == 1:
            net.wz(b, d).wait_recv()
            net.w1(b, d).start()
        elif stage == 2:
            net.w1(b, d).wait_recv()
            net.w2(b, d, 0).start()
            net.w2(b, d, 1).start()
        elif stage == 3:
            net.w2(b, d, 0).wait_recv()
            net.w2(b, d, 1).wait_recv()
            net.w3(b, d).start()
        else:
            net.w3(b, d).wait_recv()


def weights_sent(net):
    for b in BLOCKS:
        for d in (1, 2, 3):
            net.wz(b, d).wait_send()
            net.w1(b, d).wait_send()
            net.w2(b, d, 0).wait_send()
            net.w2(b, d, 1).wait_send()
            net.w3(b, d).wait_send()


def add_all(net, b, e, ref):
    def go(p):
        if b == 0:
            net.k.wa[e // 2, p, e % 2] = net.k.wa[e // 2, p, e % 2] + ref[p]
        else:
            net.block(b)[p, e] = net.block(b)[p, e] + ref[p]
    loop(4, go)


def reduce_stage(net, b, stage):
    k, c = net.k, net.c
    if stage == 0:
        net.r1(b).start()
    elif stage == 1:
        net.r1(b).wait_recv()
        def go(i):
            if b == 0:
                t, p = i // 4, i % 4
                for half in range(2):
                    k.wa[2 * c + t, p, half] = k.wa[2 * c + t, p, half] + k.rb1a[t, p, half]
            else:
                ref, src = net.block(b), (k.rb1i, k.rb1o)[b - 1]
                p, j = i // 2, 2 * (i % 2)
                for h in range(2):
                    ref[p, 4 * c + j + h] = ref[p, 4 * c + j + h] + src[p, j + h]
        loop(8, go)
        net.r2(b, 0).start()
        net.r2(b, 1).start()
    elif stage == 2:
        net.r2(b, 1).wait_recv()
        add_all(net, b, net.e2, k.rb2.at[b, 1])
        net.r3(b).start()
        net.r2(b, 0).wait_recv()
        add_all(net, b, net.e, k.rb2.at[b, 0])
    elif stage == 3:
        net.r3(b).wait_recv()
        add_all(net, b, net.e, k.rb3.at[b])
        for d in (1, 3, 2):
            net.r4(b, d).start()
    elif stage == 4:
        for d in (1, 3, 2):
            net.r4(b, d).wait_recv()
        if b == 0:
            own = k.wa[net.e // 2, net.z, net.e % 2]
        else:
            own = net.block(b)[net.z, net.e]
        total = (own.astype(f32) + k.rb4[b, 0].astype(f32)) + (k.rb4[b, 1].astype(f32) + k.rb4[b, 2].astype(f32))
        if b == 0:
            k.wa[net.e // 2, net.z, net.e % 2] = total.astype(bf16)
        else:
            net.block(b)[net.z, net.e] = total.astype(bf16)
        net.keep(b).start()
        net.a1(b).start()
        net.a2(b, 0).start()
    elif stage == 5:
        net.a1(b).wait_recv()
        net.a2(b, 1).start()
    elif stage == 6:
        net.keep(b).wait()
        net.a2(b, 0).wait_recv()
        net.a2(b, 1).wait_recv()
        net.a3(b).start()
    else:
        net.a3(b).wait_recv()
        net.r1(b).wait_send()
        for i in (0, 1):
            net.r2(b, i).wait_send()
            net.a2(b, i).wait_send()
        net.r3(b).wait_send()
        for d in (1, 2, 3):
            net.r4(b, d).wait_send()
        net.a1(b).wait_send()
        net.a3(b).wait_send()


def small_stage(net, i):
    k = net.k
    if i > 0:
        net.sg(i - 1).wait_recv()
        mine = k.sg[...] if i == 1 else k.sgs[i - 2]
        k.sgs[i - 1] = mine + k.sgr[i - 1]
    if i < 5:
        net.sg(i).start()


def kernel(names, *refs):
    k = K()
    for name, ref in zip(names, refs):
        setattr(k, name, ref)
    net = Net(k)
    z = net.z
    own_rows = pl.ds(pl.multiple_of(z * SEQ, 16), SEQ)
    local = [
        pltpu.make_async_copy(k.wq_hbm, k.stage.at[0], k.sem_in.at[0]),
        pltpu.make_async_copy(k.wk_hbm, k.stage.at[1], k.sem_in.at[1]),
        pltpu.make_async_copy(k.wv_hbm, k.stage.at[2], k.sem_in.at[2]),
        pltpu.make_async_copy(k.wout_hbm, k.wa.at[3, z], k.sem_in.at[3]),
        pltpu.make_async_copy(k.wi_hbm, k.wi.at[z], k.sem_in.at[4]),
        pltpu.make_async_copy(k.wo_hbm, k.wo.at[z], k.sem_in.at[5]),
        pltpu.make_async_copy(k.tok_hbm.at[own_rows], k.tok.at[pl.ds(0, SEQ)], k.sem_in.at[6]),
        pltpu.make_async_copy(k.cot_hbm.at[own_rows], k.cot.at[pl.ds(0, SEQ)], k.sem_in.at[7]),
    ]
    for c in local:
        c.start()
    k.tok[SEQ:PAD] = jnp.zeros((PAD - SEQ, D), bf16)
    k.cot[SEQ:PAD] = jnp.zeros((PAD - SEQ, D), bf16)
    k.sg[...] = jnp.zeros((32, BIAS), f32)
    k.factor[...] = jnp.zeros((16, PAD), f32)
    own_small(k, z)
    for t in range(3):
        local[t].wait()
        k.wa[t, z] = k.stage[t].T.reshape(2, 96, D)
    net.greet()
    for d in (1, 3, 2):
        net.sm(d).start()
    local[3].wait()
    for d in (1, 3, 2):
        net.wz(0, d).start()
    local[4].wait()
    local[5].wait()
    for b in (1, 2):
        for d in (1, 3, 2):
            net.wz(b, d).start()
    local[6].wait()
    local[7].wait()
    mask_build(k, z)
    weight_stage(net, 0, 1)
    for d in (1, 2, 3):
        net.sm(d).wait_recv()
    gates(k)
    weight_stage(net, 0, 2)
    bias_tables(k)
    weight_stage(net, 1, 1)
    weight_stage(net, 0, 3)
    weight_stage(net, 1, 2)
    weight_stage(net, 2, 1)
    weight_stage(net, 0, 4)
    project(k)

    def forward(pr):
        attend(k, pr)
        @pl.when(pr == 0)
        def _():
            weight_stage(net, 1, 3)
            weight_stage(net, 2, 2)
        @pl.when(pr == 3)
        def _():
            weight_stage(net, 2, 3)
    loop(PAIRS, forward)
    norm_one(k)
    weight_stage(net, 1, 4)
    weight_stage(net, 2, 4)
    feed_init(k)
    loop(4, lambda p: feed(k, p))
    norm_two(k)
    here = [
        pltpu.make_async_copy(k.out.at[pl.ds(0, SEQ)], k.out_hbm.at[own_rows], k.sem_in.at[0]),
        pltpu.make_async_copy(k.gtok.at[pl.ds(0, SEQ)], k.gtok_hbm.at[own_rows], k.sem_in.at[1]),
    ]
    here[0].start()
    for d in (1, 3, 2):
        net.rows("ot", d).start()
    weights_sent(net)
    loop(4, lambda p: feed_back(k, p))
    reduce_stage(net, 2, 0)
    reduce_stage(net, 1, 0)
    norm_one_back(k)
    reduce_stage(net, 2, 1)
    reduce_stage(net, 1, 1)

    def backward(pr):
        attend_back(k, pr)
        for step, stage in ((1, 2), (3, 3), (4, 4), (5, 5)):
            @pl.when(pr == step)
            def _():
                reduce_stage(net, 2, stage)
                reduce_stage(net, 1, stage)
    loop(PAIRS, backward)
    grad_input(k)
    here[1].start()
    for d in (1, 3, 2):
        net.rows("gt", d).start()
    grad_projections(k)
    reduce_stage(net, 0, 0)
    small_stage(net, 0)
    reduce_stage(net, 2, 6)
    reduce_stage(net, 1, 6)
    reduce_stage(net, 0, 1)
    small_stage(net, 1)
    reduce_stage(net, 0, 2)
    small_stage(net, 2)
    reduce_stage(net, 0, 3)
    small_stage(net, 3)
    reduce_stage(net, 0, 4)
    small_stage(net, 4)
    reduce_stage(net, 0, 5)
    small_stage(net, 5)
    reduce_stage(net, 0, 6)
    finish = pltpu.make_async_copy(k.sgs.at[4], k.sg_hbm, k.sem_in.at[2])
    finish.start()
    for b in (2, 1, 0):
        reduce_stage(net, b, 7)
    for i in range(5):
        net.sg(i).wait_send()
    for d in (1, 2, 3):
        net.sm(d).wait_send()
        for name in ("ot", "gt"):
            net.rows(name, d).wait_send()
            net.rows(name, d).wait_recv()
    here[0].wait()
    here[1].wait()
    finish.wait()


def pack(offset_bucket, b_query, b_value, gate_scale, rel_table, b_inner, shared, gate_weight, gate_bias):
    def row(v):
        return jnp.pad(v, (0, BIAS - v.shape[0]))
    rows = [row(rel_table[:, i]) for i in range(3)]
    rows += [row(jnp.concatenate([b_query, b_value])), row(b_inner)]
    rows += [jnp.broadcast_to(gate_scale[i], (BIAS,)) for i in range(3)]
    rows += [row(v) for v in shared] + [jnp.zeros(BIAS, bf16)] * 2
    gw = jnp.concatenate([jnp.tile(gate_weight.T, (1, HEADS)), jnp.broadcast_to(gate_bias[:, None], (8, BIAS - D))], 1)
    small = jnp.concatenate([jnp.stack(rows), gw])
    rev = offset_bucket[::-1]
    bucket = jnp.concatenate([rev[111:991], jnp.full((33,), -1, jnp.int32), rev[0:111]])[None]
    return small, bucket


def body(
    tokens, slot_kind, offset_bucket, w_query, b_query, w_key, w_value, b_value, w_out, b_out, gate_weight, gate_bias,
    gate_scale, rel_table, norm1_gain, norm1_bias, w_inner, b_inner, w_outer, b_outer, norm2_gain, norm2_bias, cotangent,
):
    shared = (b_out, norm1_gain, norm1_bias, b_outer, norm2_gain, norm2_bias)
    small, bucket = pack(offset_bucket, b_query, b_value, gate_scale, rel_table, b_inner, shared, gate_weight, gate_bias)
    z = lax.axis_index("tensor")
    n_dp = lax.axis_size("dp")
    rows = tokens.shape[0]
    shape = jax.ShapeDtypeStruct
    names = ["kinds", "bucket", "small", "tok_hbm", "cot_hbm", "wq_hbm", "wk_hbm", "wv_hbm", "wout_hbm", "wi_hbm", "wo_hbm"]
    names += ["out_hbm", "gtok_hbm", "ra", "ri", "ro", "sg_hbm"]
    scratch = []
    for name, (dims, dtype) in (COMPUTE_SCRATCH | COMM_SCRATCH).items():
        names.append(name)
        scratch.append(pltpu.VMEM(dims, dtype))
    names.append("sgs")
    scratch.append(pltpu.VMEM((5, 32, BIAS), f32))
    for name, dims in SEMS.items():
        names.append("sem_" + name)
        scratch.append(pltpu.SemaphoreType.DMA((2, *dims)))
    for name, count in (("sem_in", 8), ("sem_keep", 3)):
        names.append(name)
        scratch.append(pltpu.SemaphoreType.DMA((count,)))
    anywhere = pl.BlockSpec(memory_space=pl.ANY)
    vmem = pl.BlockSpec(memory_space=pltpu.VMEM)
    smem = pl.BlockSpec(memory_space=pltpu.SMEM)
    out, gtok, ra, ri, ro, sg = pl.pallas_call(
        functools.partial(kernel, names),
        in_specs=[smem, vmem, vmem] + [anywhere] * 8,
        out_specs=[anywhere] * 6,
        out_shape=[
            shape((rows, D), bf16), shape((rows, D), bf16), shape((8, 96, D), bf16), shape((8, 96, D), bf16),
            shape((8, 96, D), bf16), shape((32, BIAS), f32),
        ],
        scratch_shapes=scratch,
        compiler_params=pltpu.CompilerParams(collective_id=0, has_side_effects=True, vmem_limit_bytes=VMEM_LIMIT),
    )(
        slot_kind, bucket, small, tokens, cotangent, w_query, w_key, w_value, w_out.reshape(2, 96, D),
        w_inner.reshape(8, 96, D), w_outer.reshape(8, 96, D),
    )
    if n_dp > 8:
        groups = [list(range(g, n_dp, 8)) for g in range(8)]
        ra, ri, ro, sg = lax.psum((ra.astype(f32), ri.astype(f32), ro.astype(f32), sg), "dp", axis_index_groups=groups)
    ra = ra.reshape(4, 192, D).astype(f32)
    pick = lambda v, size: lax.dynamic_slice_in_dim(v, z * size, size, 0)
    return (
        out,
        gtok,
        ra[0].T,
        pick(sg[10], 192),
        ra[1].T,
        ra[2].T,
        pick(sg[11], 192),
        ra[3],
        sg[0, :D],
        jnp.concatenate([jnp.broadcast_to(jnp.sum(sg[24 + i, :D].reshape(HEADS, HEAD), 0)[:, None], (HEAD, 4)) for i in (0, 1)], 1),
        jnp.concatenate([jnp.broadcast_to(sg[24 + i, D], (4,)) for i in (0, 1)]),
        pick(sg[12:24, 512], 3),
        pick(sg[12:24, :NB], 3).T,
        sg[1, :D],
        sg[2, :D],
        ri.reshape(D, D).astype(f32),
        lax.dynamic_index_in_dim(sg[6:10, :D], z, 0, False),
        ro.reshape(D, D).astype(f32),
        sg[3, :D],
        sg[4, :D],
        sg[5, :D],
    )


def solution(mesh):
    in_specs = (
        P("dp", None),
        P("dp"),
        P(),
        P(None, "tensor"),
        P("tensor"),
        P(None, "tensor"),
        P(None, "tensor"),
        P("tensor"),
        P("tensor", None),
        P(),
        P(),
        P(),
        P("tensor"),
        P(None, "tensor"),
        P(),
        P(),
        P(None, "tensor"),
        P("tensor"),
        P("tensor", None),
        P(),
        P(),
        P(),
        P("dp", None),
    )
    out_specs = (
        P("dp", None),
        P("dp", None),
        P(None, "tensor"),
        P("tensor"),
        P(None, "tensor"),
        P(None, "tensor"),
        P("tensor"),
        P("tensor", None),
        P(),
        P(),
        P(),
        P("tensor"),
        P(None, "tensor"),
        P(),
        P(),
        P(None, "tensor"),
        P("tensor"),
        P("tensor", None),
        P(),
        P(),
        P(),
    )
    return jax.shard_map(body, mesh=mesh, in_specs=in_specs, out_specs=out_specs, check_vma=False)
```

time: 988 us -> 330 us (0.33)
  Pallas kernels: 0 us -> 282 us
  waiting for transfers between devices: 280 us -> 0 us
  local copies, waits for them, and re-layouts: 293 us -> 37.2 us
  blocking collectives: 200 us -> 0 us
  matrix products: 138 us -> 0 us
  other arithmetic: 52 us -> 4.77 us
  between operations: 19.1 us -> 0.78 us
    pallas_call x0 -> x1, Pallas kernels: none -> 282 us  [body(): pl.pallas_call(functools.partial(kernel, names), in_specs=[smem, vmem, vm...]
    reduce_scatter x6 -> x0, waiting for transfers between devices: 233 us -> none  [the longest x1 88 us: ffn_local(): lax.psum_scatter(grads[2].astype(jnp.bfloat16), 'tensor', scatter_dimensi...]
    dot_general x29 -> x0, matrix products: 138 us -> none  [the longest x6 36.3 us: matmul(): return jnp.dot(left, right, preferred_element_type=jnp.float32)]
    psum x1 -> x0, blocking collectives: 125 us -> none  [body(): lax.psum((sharded[0], sharded[1], sharded[2], sharded[3], sharded[4], sha...]
    reshape x4 -> x0, local copies, waits for them, and re-layouts: 118 us -> none  [the longest x2 77.7 us: expand(): skewed = tiled[:, :SEQ * stride].reshape(head_rows.shape[0], SEQ, stride)]
    another operation x2 -> x18, local copies, waits for them, and re-layouts: 52.6 us -> 2.95 us  [the longest x14 2.03 us: pack(): small = jnp.concatenate([jnp.stack(rows), gw])]
    unnamed x3 -> x0, blocking collectives: 48.1 us -> none
    all_gather x8 -> x0, waiting for transfers between devices: 42.1 us -> none  [the longest x1 42 us: body(): lax.all_gather(w_outer, 'tensor', axis=0, tiled=True)]
  transfers between devices with their start and end apart: 15 -> 0, of which waited for: 6 -> 0; matrix products, arithmetic and copies ran while one was open for 45% -> 0% of each run, Pallas kernels for 0% -> 0%
where the time goes in v1:
time: 330 us; the launch traced here: 325 us
  Pallas kernels  282 us (85%)
  local copies, waits for them, and re-layouts  37.2 us (11%)
  other arithmetic  4.77 us (1%)
    pallas_call x1, Pallas kernels, body(): pl.pallas_call(functools.partial(kernel, names), in_specs=[smem, vmem, vm...  282 us
    unnamed x15, local copies, waits for them, and re-layouts  11.2 us

profile of v1, /device:TPU:0, one launch (start us, length us, event | category | flops | bytes accessed | tf_op | source)
XLA Modules:
  0.0 325.2 jit_solution(12990474850576010444)
XLA Ops:
  0.7 0.8 slice.93
  1.5 1.4 fusion.6
  2.9 0.7 fusion.2
  3.6 0.7 pad.42
  4.3 0.7 pad.43
  5.0 0.7 pad.44
  5.7 0.7 pad.41
  6.4 0.7 pad.45
  7.1 0.7 pad.46
  7.8 0.7 pad.47
  8.5 0.8 slice_reduce_fusion.8
  11.4 0.7 broadcast_in_dim.14
  12.1 0.8 reverse.2
  12.9 0.7 pad_add_fusion
  13.6 0.7 tile.4
  14.4 1.9 concatenate.25.refs_2_
  16.3 1.9 copy.47.refs_5_
  18.2 1.9 copy.48.refs_6_
  20.1 1.9 copy.49.refs_7_
  22.0 282.4 %shard_map.382 = (bf16[1984,768]{1,0:T(8,128)(2,1)}, bf16[1984,768]{1,0:T(8,128)(2,1)}, bf16[8,96,768]{2,1,0:T(8,128)(2,1)}, bf16[8,96,768]{2,1,0:T(8,128)(2,1)}...) custom-call(s32[4]{0:T(128)} %refs_0_.1, s32[1,1024]{1,0:T(1,128)} %bitcast.39, bf16[24,1024]{1,0:T(8,128)(2,1)} %concatenate.25.refs_2_, ...), custom_call_target="tpu_custom_call" | custom-call | tf_op jit(solution)/shard_map/pallas_call | solution.py:795
  304.4 1.3 fusion.4
  306.3 1.2 concatenate.27
  307.5 0.7 slice.112
  308.8 0.8 fusion.5
  310.3 0.8 slice.116
  311.1 1.6 slice_reduce_fusion
  312.8 0.8 slice.113
  314.9 2.8 fusion.3
  317.8 2.7 bitcast_convert_fusion
  320.6 1.6 copy.52
  322.2 1.3 copy-done
  323.5 1.6 copy.53
  (41 shorter events, 5.8 us)
Async XLA Ops:
  314.9 2.8 copy-start.2
  314.9 2.8 copy-start.3
  317.8 2.8 copy-start.1
  320.6 3.0 copy-start

commit v2 on v1

--- a/solution.py
+++ b/solution.py
@@ -17,6 +17,7 @@
 BIAS = 1024
 NB = 320
 VMEM_LIMIT = 64 * 2**20 - 2**16
+OFFSETS = 991
 HALF = SEQ // 2
 f32 = jnp.float32
 bf16 = jnp.bfloat16
@@ -70,14 +71,28 @@
     return jnp.where((lane // HEAD) == hh, 1.0, 0.0).astype(bf16)
 
 
-def onehot(k):
-    return jnp.where(lax.broadcasted_iota(jnp.int32, (NB, BIAS), 0) == k.bucket[...], 1.0, 0.0)
+def line(ref):
+    return ref[...].astype(f32).reshape(1, ref.shape[0])
+
+
+def one_hot(k):
+    k.row[...] = jnp.full((1, BIAS), -1, jnp.int32)
+    k.row[:, 0:OFFSETS] = k.bucket[...]
+    hot = jnp.where(lax.broadcasted_iota(jnp.int32, (NB, BIAS), 0) == k.row[...], 1.0, 0.0).astype(bf16)
+    for n in range(4):
+        m = lax.broadcasted_iota(jnp.int32, (BIAS, 256), 0) + lax.broadcasted_iota(jnp.int32, (BIAS, 256), 1) + 256 * n
+        turn = jnp.where((m == 879) | (m == 1903), 1.0, 0.0).astype(bf16)
+        k.hot[:, 256 * n : 256 * n + 256] = dot(hot, turn).astype(bf16)
 
 
 def own_small(k, z):
-    table = dot(k.small[0:16, 0:NB], onehot(k).astype(bf16))
-    k.sm[z, 0:3, :] = table[0:3]
-    k.sm[z, 3:8, :] = k.small[3:8, :].astype(f32)
+    one_hot(k)
+    k.sm[z, 0:3, :] = dot(k.rel[...], k.hot[...])
+    k.sm[z, 3:4, 0:192] = line(k.b_query)
+    k.sm[z, 3:4, 192:384] = line(k.b_value)
+    k.sm[z, 4:5, 0:D] = line(k.b_inner)
+    for i in range(3):
+        k.sm[z, 5 + i : 6 + i, :] = jnp.broadcast_to(k.scale[:, i : i + 1].astype(f32), (1, BIAS))
 
 
 def mask_build(k, z):
@@ -92,21 +107,22 @@
 
 
 def gate_weights(k):
-    gw = k.small[16:24, :].astype(f32)
-    first = jnp.sum(gw[0:4], axis=0, keepdims=True)
-    second = jnp.sum(gw[4:8], axis=0, keepdims=True)
+    gw = k.gw[...].astype(f32)
+    tile = lambda v: jnp.concatenate([jnp.concatenate([v, v], axis=1)] * PAIRS, axis=1)
+    first = tile(jnp.sum(gw[0:4], axis=0, keepdims=True))
+    second = tile(jnp.sum(gw[4:8], axis=0, keepdims=True))
+    bias = line(k.gate_bias)
     own = (lax.broadcasted_iota(jnp.int32, (16, D), 1) // HEAD) == lax.broadcasted_iota(jnp.int32, (16, D), 0)
-    wide_first = jnp.where(own, first[:, 0:D], 0.0)
-    wide_second = jnp.where(own, second[:, 0:D], 0.0)
-    return jnp.concatenate([wide_first, wide_second], axis=0), first[:, D:], second[:, D:], own
+    both = jnp.concatenate([jnp.where(own, first, 0.0), jnp.where(own, second, 0.0)], axis=0)
+    add = lambda v: jnp.sum(v, axis=1, keepdims=True)
+    return both, add(bias[:, 0:4]), add(bias[:, 4:8]), own
 
 
 def gates(k):
     weights, first_bias, second_bias, _ = gate_weights(k)
     logits = dot_t(weights, k.tok[...].astype(f32), precision=highest)
-    spread = lambda b: jnp.concatenate([b, b], axis=1)
-    first = jax.nn.sigmoid(logits[0:16] + spread(first_bias))
-    second = jax.nn.sigmoid(logits[16:32] + spread(second_bias))
+    first = jax.nn.sigmoid(logits[0:16] + first_bias)
+    second = jax.nn.sigmoid(logits[16:32] + second_bias)
     k.first[...] = first
     k.second[...] = second
     for h in range(HEADS):
@@ -182,13 +198,9 @@
     return jnp.concatenate([ref[pr] for pr in range(PAIRS)], axis=1)
 
 
-def vec(k, row):
-    return k.small[row : row + 1, 0:D].astype(f32)
-
-
 def norm_one(k):
     k.fa[...] = dot(mixed_all(k.mixed), wide(k.wa, 3))
-    b_out, gain, shift = vec(k, 8), vec(k, 9), vec(k, 10)
+    b_out, gain, shift = line(k.b_out), line(k.norm1_gain), line(k.norm1_bias)
     def go(rows, _):
         r = residual_scale * k.tok[rows, :].astype(f32) + k.fa[rows, :] + b_out
         n, inv = stats(r)
@@ -217,7 +229,8 @@
 
 
 def norm_two(k):
-    b_outer, gain1, shift1, gain2, shift2 = vec(k, 11), vec(k, 9), vec(k, 10), vec(k, 12), vec(k, 13)
+    b_outer, gain1, shift1 = line(k.b_outer), line(k.norm1_gain), line(k.norm1_bias)
+    gain2, shift2 = line(k.norm2_gain), line(k.norm2_bias)
     def go(rows, carry):
         g_gain, g_shift, g_b = carry
         r = residual_scale * (k.n1[rows, :] * gain1 + shift1) + k.fb[rows, :] + b_outer
@@ -249,7 +262,7 @@
 
 
 def norm_one_back(k):
-    gain = vec(k, 9)
+    gain = line(k.norm1_gain)
     def go(rows, carry):
         g_gain, g_shift, g_b = carry
         gh = k.fb[rows, :]
@@ -327,7 +340,7 @@
     k.sg[24:25, D:] = jnp.broadcast_to(jnp.sum(jnp.sum(df, axis=0, keepdims=True), axis=1, keepdims=True), (1, 256))
     k.sg[25:26, D:] = jnp.broadcast_to(jnp.sum(jnp.sum(ds, axis=0, keepdims=True), axis=1, keepdims=True), (1, 256))
     goff = jnp.concatenate([k.goff[h] for h in range(HEADS)] + [jnp.zeros((4, BIAS), f32)], axis=0)
-    rel = dot_t(goff, onehot(k), precision=highest)
+    rel = dot_t(goff, k.hot[...].astype(f32), precision=highest)
     k.sg[12:24, 0:NB] = rel[0:HEADS]
     k.sg[12:24, 512:640] = jnp.broadcast_to(gscale, (16, 128))[0:HEADS]
     return dot(dz.T, weights)
@@ -348,7 +361,9 @@
         g = mixed_all(src)
         if t != 1:
             row = jnp.sum(fold(g.astype(f32)), axis=0, keepdims=True)
-            k.sg[10 + t // 2 : 11 + t // 2, 0:D] = row
+            for p in range(4):
+                at, lane = (6 + p, D) if t == 0 else (12 + 3 * p, 640)
+                k.sg[at : at + 1, lane : lane + 192] = row[:, 192 * p : 192 * p + 192]
         k.wa[t] = dot_l(g, k.tok[...]).astype(bf16).reshape(4, 2, 96, D)
     k.wa[3] = dot_l(mixed_all(k.mixed), k.gb[...]).astype(bf16).reshape(4, 2, 96, D)
 
@@ -361,7 +376,7 @@
 
 
 COMPUTE_SCRATCH = dict(
-    tok=((PAD, D), bf16), cot=((PAD, D), bf16), sm=((4, 8, BIAS), f32), mask=((PAD, PAD), f32),
+    row=((1, BIAS), jnp.int32), hot=((NB, BIAS), bf16), tok=((PAD, D), bf16), cot=((PAD, D), bf16), sm=((4, 8, BIAS), f32), mask=((PAD, PAD), f32),
     first=((16, PAD), f32), second=((16, PAD), f32), factor=((16, PAD), f32), gate=((HEADS, 1, PAD), f32),
     bias=((HEADS, 128, 896), bf16), q=((PAIRS, PAD, 128), bf16), k=((PAIRS, PAD, 128), bf16),
     v=((PAIRS, PAD, 128), bf16), s=((PAD, PAD), f32), p=((HEADS, PAD, PAD), bf16), mixed=((PAIRS, PAD, 128), bf16),
@@ -376,12 +391,12 @@
 MESH = pl.DeviceIdType.MESH
 BLOCKS = (0, 1, 2)
 SEMS = dict(
-    wz=(3, 3), w1=(3, 3), w2=(3, 3, 2), w3=(3, 3), sm=(3,), ot=(3,), gt=(3,), r1=(3,), r2=(3, 2), r3=(3,),
+    wz=(3, 3), w1=(3, 3), w2=(3, 3, 2), w3=(3, 3), sm=(3,), rows=(2, 2, 3), r1=(3, 4), r2=(3, 4, 2), r3=(3, 4),
     r4=(3, 3), a1=(3,), a2=(3, 2), a3=(3,), sg=(5,),
 )
 COMM_SCRATCH = dict(
-    stage=((3, D, 192), bf16), rb1a=((2, 4, 2, 96, D), bf16), rb1i=((4, 4, 96, D), bf16), rb1o=((4, 4, 96, D), bf16),
-    rb2=((3, 2, 4, 96, D), bf16), rb3=((3, 4, 96, D), bf16), rb4=((3, 3, 96, D), bf16), sgr=((5, 32, BIAS), f32),
+    rb1a=((4, 2, 2, 96, D), bf16), rb1=((2, 4, 4, 96, D), bf16), rb2=((3, 4, 2, 96, D), bf16),
+    rb3=((3, 4, 96, D), bf16), rb4=((3, 3, 96, D), bf16), sgr=((5, 32, BIAS), f32), sgs=((5, 32, BIAS), f32), fin=((16, BIAS), f32),
 )
 
 
@@ -430,14 +445,8 @@
     def chunk(self, b, p, e):
         return self.block(b).at[e // 2, p, e % 2] if b == 0 else self.block(b).at[p, e]
 
-    def chunk_all(self, b, e):
-        return self.block(b).at[e // 2, :, e % 2] if b == 0 else self.block(b).at[:, e]
-
     def side(self, b, p, c):
         return self.block(b).at[pl.ds(2 * c, 2), p] if b == 0 else self.block(b).at[p, pl.ds(4 * c, 4)]
-
-    def side_all(self, b, c):
-        return self.block(b).at[pl.ds(2 * c, 2)] if b == 0 else self.block(b).at[:, pl.ds(4 * c, 4)]
 
     def wz(self, b, d):
         ref = self.chunk(b, self.z, self.e)
@@ -459,20 +468,30 @@
         ref = self.k.sm.at[self.z]
         return self.copy("sm", (d - 1,), ref, ref, (self.dp, self.ahead(d)))
 
-    def rows(self, name, d):
-        src, dst = (self.k.out, self.k.out_hbm) if name == "ot" else (self.k.gtok, self.k.gtok_hbm)
-        at = pl.ds(pl.multiple_of(self.z * SEQ, 16), SEQ)
-        return self.copy(name, (d - 1,), src.at[pl.ds(0, SEQ)], dst.at[at], (self.dp, self.ahead(d)))
-
-    def r1(self, b):
-        dst = (self.k.rb1a, self.k.rb1i, self.k.rb1o)[b]
-        return self.copy("r1", (b,), self.side_all(b, 1 - self.c), dst, self.core)
-
-    def r2(self, b, i):
-        return self.copy("r2", (b, i), self.chunk_all(b, (self.e1, self.e12)[i]), self.k.rb2.at[b, i], self.one)
-
-    def r3(self, b):
-        return self.copy("r3", (b,), self.chunk_all(b, self.e2), self.k.rb3.at[b], self.two)
+    def rows(self, a, way, j):
+        source, result = ((self.k.out, self.k.out_hbm), (self.k.gtok, self.k.gtok_hbm))[a]
+        slot = self.z - j if way == 0 else self.z + j
+        to = self.z + 1 if way == 0 else self.z - 1
+        at = result.at[pl.ds(pl.multiple_of(slot * SEQ, 16), SEQ)]
+        return self.copy("rows", (a, way, j), source.at[pl.ds(0, SEQ)] if j == 0 else at, at, (self.dp, to))
+
+    def sends(self, way, j):
+        z = self.z
+        return (z <= 2) & (z >= j) if way == 0 else (z >= 1) & (z + j <= 3)
+
+    def receives(self, way, j):
+        z = self.z
+        return z >= 1 + j if way == 0 else z + 1 + j <= 3
+
+    def r1(self, b, p):
+        dst = self.k.rb1a.at[p] if b == 0 else self.k.rb1.at[b - 1, p]
+        return self.copy("r1", (b, p), self.side(b, p, 1 - self.c), dst, self.core)
+
+    def r2(self, b, p, i):
+        return self.copy("r2", (b, p, i), self.chunk(b, p, (self.e1, self.e12)[i]), self.k.rb2.at[b, p, i], self.one)
+
+    def r3(self, b, p):
+        return self.copy("r3", (b, p), self.chunk(b, p, self.e2), self.k.rb3.at[b, p], self.two)
 
     def r4(self, b, d):
         to = self.ahead(d)
@@ -510,109 +529,136 @@
     lax.fori_loop(0, n, go, 0)
 
 
-def weight_stage(net, b, stage):
-    for d in (1, 3, 2):
-        if stage == 1:
-            net.wz(b, d).wait_recv()
-            net.w1(b, d).start()
-        elif stage == 2:
-            net.w1(b, d).wait_recv()
-            net.w2(b, d, 0).start()
-            net.w2(b, d, 1).start()
-        elif stage == 3:
-            net.w2(b, d, 0).wait_recv()
-            net.w2(b, d, 1).wait_recv()
-            net.w3(b, d).start()
-        else:
-            net.w3(b, d).wait_recv()
+def when(condition, fn):
+    @pl.when(condition)
+    def _():
+        fn()
+
+
+PIECES = ((0, 1), (0, 2), (0, 3), (1, 1), (2, 1), (1, 2), (2, 2), (1, 3), (2, 3))
+WINDOW = 3
+
+
+def weight_step(net, t):
+    if t < 9:
+        b, d = PIECES[t]
+        net.wz(b, d).wait_recv()
+        net.w1(b, d).start()
+        if t + WINDOW < 9:
+            net.wz(*PIECES[t + WINDOW]).start()
+    if 0 <= t - 1 < 9:
+        b, d = PIECES[t - 1]
+        net.w1(b, d).wait_recv()
+        net.w2(b, d, 0).start()
+        net.w2(b, d, 1).start()
+    if 0 <= t - 2 < 9:
+        b, d = PIECES[t - 2]
+        net.w2(b, d, 0).wait_recv()
+        net.w2(b, d, 1).wait_recv()
+        net.w3(b, d).start()
+    if 0 <= t - 3 < 9:
+        net.w3(*PIECES[t - 3]).wait_recv()
 
 
 def weights_sent(net):
-    for b in BLOCKS:
-        for d in (1, 2, 3):
-            net.wz(b, d).wait_send()
-            net.w1(b, d).wait_send()
-            net.w2(b, d, 0).wait_send()
-            net.w2(b, d, 1).wait_send()
-            net.w3(b, d).wait_send()
-
-
-def add_all(net, b, e, ref):
-    def go(p):
-        if b == 0:
-            net.k.wa[e // 2, p, e % 2] = net.k.wa[e // 2, p, e % 2] + ref[p]
-        else:
-            net.block(b)[p, e] = net.block(b)[p, e] + ref[p]
-    loop(4, go)
-
-
-def reduce_stage(net, b, stage):
-    k, c = net.k, net.c
-    if stage == 0:
-        net.r1(b).start()
-    elif stage == 1:
-        net.r1(b).wait_recv()
-        def go(i):
-            if b == 0:
-                t, p = i // 4, i % 4
-                for half in range(2):
-                    k.wa[2 * c + t, p, half] = k.wa[2 * c + t, p, half] + k.rb1a[t, p, half]
-            else:
-                ref, src = net.block(b), (k.rb1i, k.rb1o)[b - 1]
-                p, j = i // 2, 2 * (i % 2)
-                for h in range(2):
-                    ref[p, 4 * c + j + h] = ref[p, 4 * c + j + h] + src[p, j + h]
-        loop(8, go)
-        net.r2(b, 0).start()
-        net.r2(b, 1).start()
-    elif stage == 2:
-        net.r2(b, 1).wait_recv()
-        add_all(net, b, net.e2, k.rb2.at[b, 1])
-        net.r3(b).start()
-        net.r2(b, 0).wait_recv()
-        add_all(net, b, net.e, k.rb2.at[b, 0])
-    elif stage == 3:
-        net.r3(b).wait_recv()
-        add_all(net, b, net.e, k.rb3.at[b])
-        for d in (1, 3, 2):
-            net.r4(b, d).start()
-    elif stage == 4:
-        for d in (1, 3, 2):
-            net.r4(b, d).wait_recv()
-        if b == 0:
-            own = k.wa[net.e // 2, net.z, net.e % 2]
-        else:
-            own = net.block(b)[net.z, net.e]
-        total = (own.astype(f32) + k.rb4[b, 0].astype(f32)) + (k.rb4[b, 1].astype(f32) + k.rb4[b, 2].astype(f32))
-        if b == 0:
-            k.wa[net.e // 2, net.z, net.e % 2] = total.astype(bf16)
-        else:
-            net.block(b)[net.z, net.e] = total.astype(bf16)
-        net.keep(b).start()
-        net.a1(b).start()
-        net.a2(b, 0).start()
-    elif stage == 5:
-        net.a1(b).wait_recv()
-        net.a2(b, 1).start()
-    elif stage == 6:
-        net.keep(b).wait()
-        net.a2(b, 0).wait_recv()
-        net.a2(b, 1).wait_recv()
-        net.a3(b).start()
+    for b, d in PIECES:
+        net.wz(b, d).wait_send()
+        net.w1(b, d).wait_send()
+        net.w2(b, d, 0).wait_send()
+        net.w2(b, d, 1).wait_send()
+        net.w3(b, d).wait_send()
+
+
+def rows_step(net, a, j):
+    for way in (0, 1):
+        if j > 0:
+            when(net.receives(way, j - 1), lambda: net.rows(a, way, j - 1).wait_recv())
+        if j < 3:
+            when(net.sends(way, j), lambda: net.rows(a, way, j).start())
+
+
+def rows_sent(net, a):
+    for j in range(3):
+        for way in (0, 1):
+            when(net.sends(way, j), lambda: net.rows(a, way, j).wait_send())
+
+
+def add(net, b, p, e, ref):
+    k = net.k
+    if b == 0:
+        k.wa[e // 2, p, e % 2] = k.wa[e // 2, p, e % 2] + ref[...]
     else:
-        net.a3(b).wait_recv()
-        net.r1(b).wait_send()
-        for i in (0, 1):
-            net.r2(b, i).wait_send()
-            net.a2(b, i).wait_send()
-        net.r3(b).wait_send()
-        for d in (1, 2, 3):
-            net.r4(b, d).wait_send()
-        net.a1(b).wait_send()
-        net.a3(b).wait_send()
-
-
-def small_stage(net, i):
+        net.block(b)[p, e] = net.block(b)[p, e] + ref[...]
+
+
+def halves(net, b, p):
+    net.r1(b, p).wait_recv()
+    for j in range(4):
+        src = net.k.rb1a.at[p, j // 2, j % 2] if b == 0 else net.k.rb1.at[b - 1, p, j]
+        add(net, b, p, 4 * net.c + j, src)
+    net.r2(b, p, 1).start()
+    net.r2(b, p, 0).start()
+
+
+def quarters(net, b, p):
+    net.r2(b, p, 1).wait_recv()
+    add(net, b, p, net.e2, net.k.rb2.at[b, p, 1])
+    net.r3(b, p).start()
+    net.r2(b, p, 0).wait_recv()
+    add(net, b, p, net.e, net.k.rb2.at[b, p, 0])
+
+
+def eighths(net, b, i):
+    p = net.ahead(1 + i)
+    net.r3(b, p).wait_recv()
+    add(net, b, p, net.e, net.k.rb3.at[b, p])
+    if i < 3:
+        net.r4(b, 1 + i).start()
+
+
+def over_z(net, b):
+    k = net.k
+    for d in (1, 2, 3):
+        net.r4(b, d).wait_recv()
+    own = k.wa[net.e // 2, net.z, net.e % 2] if b == 0 else net.block(b)[net.z, net.e]
+    total = (own.astype(f32) + k.rb4[b, 0].astype(f32)) + (k.rb4[b, 1].astype(f32) + k.rb4[b, 2].astype(f32))
+    if b == 0:
+        k.wa[net.e // 2, net.z, net.e % 2] = total.astype(bf16)
+    else:
+        net.block(b)[net.z, net.e] = total.astype(bf16)
+    net.keep(b).start()
+    net.a1(b).start()
+    net.a2(b, 0).start()
+
+
+def around(net, b):
+    net.a1(b).wait_recv()
+    net.a2(b, 1).start()
+
+
+def to_core(net, b):
+    net.keep(b).wait()
+    net.a2(b, 0).wait_recv()
+    net.a2(b, 1).wait_recv()
+    net.a3(b).start()
+
+
+def gradients_sent(net, b):
+    net.a3(b).wait_recv()
+    for p in range(4):
+        net.r1(b, p).wait_send()
+        net.r2(b, p, 0).wait_send()
+        net.r2(b, p, 1).wait_send()
+        net.r3(b, p).wait_send()
+    for d in (1, 2, 3):
+        net.r4(b, d).wait_send()
+    net.a1(b).wait_send()
+    net.a2(b, 0).wait_send()
+    net.a2(b, 1).wait_send()
+    net.a3(b).wait_send()
+
+
+def small_step(net, i):
     k = net.k
     if i > 0:
         net.sg(i - 1).wait_recv()
@@ -629,211 +675,278 @@
     net = Net(k)
     z = net.z
     own_rows = pl.ds(pl.multiple_of(z * SEQ, 16), SEQ)
-    local = [
-        pltpu.make_async_copy(k.wq_hbm, k.stage.at[0], k.sem_in.at[0]),
-        pltpu.make_async_copy(k.wk_hbm, k.stage.at[1], k.sem_in.at[1]),
-        pltpu.make_async_copy(k.wv_hbm, k.stage.at[2], k.sem_in.at[2]),
-        pltpu.make_async_copy(k.wout_hbm, k.wa.at[3, z], k.sem_in.at[3]),
-        pltpu.make_async_copy(k.wi_hbm, k.wi.at[z], k.sem_in.at[4]),
-        pltpu.make_async_copy(k.wo_hbm, k.wo.at[z], k.sem_in.at[5]),
-        pltpu.make_async_copy(k.tok_hbm.at[own_rows], k.tok.at[pl.ds(0, SEQ)], k.sem_in.at[6]),
-        pltpu.make_async_copy(k.cot_hbm.at[own_rows], k.cot.at[pl.ds(0, SEQ)], k.sem_in.at[7]),
+    moves = [
+        (k.wq_hbm, k.wa.at[0, z]), (k.wk_hbm, k.wa.at[1, z]), (k.wv_hbm, k.wa.at[2, z]), (k.wout_hbm, k.wa.at[3, z]),
+        (k.wi_hbm, k.wi.at[z]), (k.wo_hbm, k.wo.at[z]),
+        (k.tok_hbm.at[own_rows], k.tok.at[pl.ds(0, SEQ)]), (k.cot_hbm.at[own_rows], k.cot.at[pl.ds(0, SEQ)]),
     ]
+    local = [pltpu.make_async_copy(src, dst, k.sem_in.at[i]) for i, (src, dst) in enumerate(moves)]
     for c in local:
         c.start()
+    net.greet()
+    for c in local[0:4]:
+        c.wait()
+    for piece in PIECES[0:WINDOW]:
+        net.wz(*piece).start()
     k.tok[SEQ:PAD] = jnp.zeros((PAD - SEQ, D), bf16)
     k.cot[SEQ:PAD] = jnp.zeros((PAD - SEQ, D), bf16)
     k.sg[...] = jnp.zeros((32, BIAS), f32)
     k.factor[...] = jnp.zeros((16, PAD), f32)
     own_small(k, z)
-    for t in range(3):
-        local[t].wait()
-        k.wa[t, z] = k.stage[t].T.reshape(2, 96, D)
-    net.greet()
-    for d in (1, 3, 2):
+    for d in (1, 2, 3):
         net.sm(d).start()
-    local[3].wait()
-    for d in (1, 3, 2):
-        net.wz(0, d).start()
-    local[4].wait()
-    local[5].wait()
-    for b in (1, 2):
-        for d in (1, 3, 2):
-            net.wz(b, d).start()
-    local[6].wait()
-    local[7].wait()
+    for c in local[4:8]:
+        c.wait()
+    weight_step(net, 0)
     mask_build(k, z)
-    weight_stage(net, 0, 1)
+    weight_step(net, 1)
     for d in (1, 2, 3):
         net.sm(d).wait_recv()
     gates(k)
-    weight_stage(net, 0, 2)
+    weight_step(net, 2)
     bias_tables(k)
-    weight_stage(net, 1, 1)
-    weight_stage(net, 0, 3)
-    weight_stage(net, 1, 2)
-    weight_stage(net, 2, 1)
-    weight_stage(net, 0, 4)
+    weight_step(net, 3)
+    weight_step(net, 4)
+    weight_step(net, 5)
     project(k)
 
     def forward(pr):
         attend(k, pr)
-        @pl.when(pr == 0)
-        def _():
-            weight_stage(net, 1, 3)
-            weight_stage(net, 2, 2)
-        @pl.when(pr == 3)
-        def _():
-            weight_stage(net, 2, 3)
+        when(pr == 1, lambda: weight_step(net, 6))
+        when(pr == 4, lambda: weight_step(net, 7))
     loop(PAIRS, forward)
     norm_one(k)
-    weight_stage(net, 1, 4)
-    weight_stage(net, 2, 4)
+    weight_step(net, 8)
     feed_init(k)
-    loop(4, lambda p: feed(k, p))
+
+    def layer_two(i):
+        when(i == 2, lambda: weight_step(net, 9))
+        when(i == 3, lambda: (weight_step(net, 10), weight_step(net, 11)))
+        feed(k, net.behind(i))
+    loop(4, layer_two)
     norm_two(k)
     here = [
         pltpu.make_async_copy(k.out.at[pl.ds(0, SEQ)], k.out_hbm.at[own_rows], k.sem_in.at[0]),
         pltpu.make_async_copy(k.gtok.at[pl.ds(0, SEQ)], k.gtok_hbm.at[own_rows], k.sem_in.at[1]),
     ]
     here[0].start()
-    for d in (1, 3, 2):
-        net.rows("ot", d).start()
+    rows_step(net, 0, 0)
     weights_sent(net)
-    loop(4, lambda p: feed_back(k, p))
-    reduce_stage(net, 2, 0)
-    reduce_stage(net, 1, 0)
+
+    def layer_two_back(i):
+        p = net.ahead(1 + i)
+        feed_back(k, p)
+        net.r1(2, p).start()
+        net.r1(1, p).start()
+        def last():
+            before = net.ahead(i)
+            halves(net, 2, before)
+            halves(net, 1, before)
+        when(i > 0, last)
+    loop(4, layer_two_back)
+    rows_step(net, 0, 1)
     norm_one_back(k)
-    reduce_stage(net, 2, 1)
-    reduce_stage(net, 1, 1)
+    both = lambda fn, i: (fn(net, 2, net.ahead(1 + i)), fn(net, 1, net.ahead(1 + i)))
+    pass_on = lambda i: (eighths(net, 2, i), eighths(net, 1, i))
+    both(halves, 3)
+    both(quarters, 0)
 
     def backward(pr):
         attend_back(k, pr)
-        for step, stage in ((1, 2), (3, 3), (4, 4), (5, 5)):
-            @pl.when(pr == step)
-            def _():
-                reduce_stage(net, 2, stage)
-                reduce_stage(net, 1, stage)
+        when(pr == 3, lambda: (both(quarters, 1), pass_on(0)))
+        when(pr == 5, lambda: rows_step(net, 0, 2))
     loop(PAIRS, backward)
     grad_input(k)
     here[1].start()
-    for d in (1, 3, 2):
-        net.rows("gt", d).start()
+    rows_step(net, 1, 0)
+    both(quarters, 2)
+    pass_on(1)
     grad_projections(k)
-    reduce_stage(net, 0, 0)
-    small_stage(net, 0)
-    reduce_stage(net, 2, 6)
-    reduce_stage(net, 1, 6)
-    reduce_stage(net, 0, 1)
-    small_stage(net, 1)
-    reduce_stage(net, 0, 2)
-    small_stage(net, 2)
-    reduce_stage(net, 0, 3)
-    small_stage(net, 3)
-    reduce_stage(net, 0, 4)
-    small_stage(net, 4)
-    reduce_stage(net, 0, 5)
-    small_stage(net, 5)
-    reduce_stage(net, 0, 6)
-    finish = pltpu.make_async_copy(k.sgs.at[4], k.sg_hbm, k.sem_in.at[2])
+    for i in range(4):
+        net.r1(0, net.ahead(1 + i)).start()
+    small_step(net, 0)
+    both(quarters, 3)
+    pass_on(2)
+    halves(net, 0, net.ahead(1))
+    halves(net, 0, net.ahead(2))
+    rows_step(net, 0, 3)
+    small_step(net, 1)
+    pass_on(3)
+    halves(net, 0, net.ahead(3))
+    halves(net, 0, net.ahead(4))
+    rows_step(net, 1, 1)
+    small_step(net, 2)
+    quarters(net, 0, net.ahead(1))
+    quarters(net, 0, net.ahead(2))
+    eighths(net, 0, 0)
+    small_step(net, 3)
+    quarters(net, 0, net.ahead(3))
+    eighths(net, 0, 1)
+    over_z(net, 2)
+    over_z(net, 1)
+    quarters(net, 0, net.ahead(4))
+    eighths(net, 0, 2)
+    small_step(net, 4)
+    eighths(net, 0, 3)
+    around(net, 2)
+    around(net, 1)
+    rows_step(net, 1, 2)
+    over_z(net, 0)
+    to_core(net, 2)
+    to_core(net, 1)
+    small_step(net, 5)
+    k.fin[...] = jnp.zeros((16, BIAS), f32)
+    k.fin[0:6, :] = k.sgs[4, 0:6, :]
+    k.fin[6:7, :] = k.sgs[4, pl.ds(6 + z, 1), :]
+    for i in range(3):
+        k.fin[8 + i : 9 + i, :] = k.sgs[4, pl.ds(12 + 3 * z + i, 1), :]
+    k.fin[11:13, :] = k.sgs[4, 24:26, :]
+    finish = pltpu.make_async_copy(k.fin, k.sg_hbm, k.sem_in.at[2])
     finish.start()
+    around(net, 0)
+    to_core(net, 0)
+    rows_step(net, 1, 3)
     for b in (2, 1, 0):
-        reduce_stage(net, b, 7)
+        gradients_sent(net, b)
     for i in range(5):
         net.sg(i).wait_send()
     for d in (1, 2, 3):
         net.sm(d).wait_send()
-        for name in ("ot", "gt"):
-            net.rows(name, d).wait_send()
-            net.rows(name, d).wait_recv()
+    for a in (0, 1):
+        rows_sent(net, a)
     here[0].wait()
     here[1].wait()
     finish.wait()
 
 
-def pack(offset_bucket, b_query, b_value, gate_scale, rel_table, b_inner, shared, gate_weight, gate_bias):
-    def row(v):
-        return jnp.pad(v, (0, BIAS - v.shape[0]))
-    rows = [row(rel_table[:, i]) for i in range(3)]
-    rows += [row(jnp.concatenate([b_query, b_value])), row(b_inner)]
-    rows += [jnp.broadcast_to(gate_scale[i], (BIAS,)) for i in range(3)]
-    rows += [row(v) for v in shared] + [jnp.zeros(BIAS, bf16)] * 2
-    gw = jnp.concatenate([jnp.tile(gate_weight.T, (1, HEADS)), jnp.broadcast_to(gate_bias[:, None], (8, BIAS - D))], 1)
-    small = jnp.concatenate([jnp.stack(rows), gw])
-    rev = offset_bucket[::-1]
-    bucket = jnp.concatenate([rev[111:991], jnp.full((33,), -1, jnp.int32), rev[0:111]])[None]
-    return small, bucket
+def finish_kernel(out, gtok, ra, ri, ro, sg, *rest):
+    names = FINAL + ("stage", "wide", "sem")
+    k = K()
+    for name, ref in zip(names, rest):
+        setattr(k, name, ref)
+    copies = [pltpu.make_async_copy(out, k.output, k.sem.at[0]), pltpu.make_async_copy(gtok, k.grad_tokens, k.sem.at[1])]
+    for c in copies:
+        c.start()
+    inward = [pltpu.make_async_copy(src, k.stage.at[i], k.sem.at[2 + i]) for i, src in enumerate((ri, ro, ra))]
+    for c in inward:
+        c.start()
+    row = lambda r, lane, n: sg[r : r + 1, lane : lane + n].reshape(n)
+    k.b_out[...], k.norm1_gain[...], k.norm1_bias[...] = row(0, 0, D), row(1, 0, D), row(2, 0, D)
+    k.b_outer[...], k.norm2_gain[...], k.norm2_bias[...] = row(3, 0, D), row(4, 0, D), row(5, 0, D)
+    k.b_inner[...], k.b_query[...], k.b_value[...] = row(6, 0, D), row(6, D, 192), row(8, 640, 192)
+    k.rel_table[...] = sg[8:11, 0:NB]
+    lane = lax.broadcasted_iota(jnp.int32, (1, 128), 1)
+    cell = lambda r, at: sg[r : r + 1, at : at + 128]
+    k.gate_scale[...] = jnp.where(lane == 0, cell(8, 512), jnp.where(lane == 1, cell(9, 512), cell(10, 512)))[:, 0:3]
+    k.gate_bias[...] = jnp.where(lane < 4, cell(11, D), cell(12, D))[:, 0:8]
+    for i in (0, 1):
+        heads = cell(11 + i, 0)
+        for pr in range(1, PAIRS):
+            heads = heads + cell(11 + i, 128 * pr)
+        k.gate_weight[4 * i : 4 * i + 4, :] = jnp.broadcast_to(heads[:, 0:HEAD] + heads[:, HEAD:128], (4, HEAD))
+    outward = []
+    for i, c in enumerate(inward):
+        c.wait()
+        def widen(j):
+            k.wide[i, j] = k.stage[i, j].astype(f32)
+        loop(8, widen)
+        if i < 2:
+            to = [(k.wide.at[i], (k.w_inner, k.w_outer)[i])]
+        else:
+            to = [(k.wide.at[i, pl.ds(2 * j, 2)], ref) for j, ref in enumerate((k.w_query, k.w_key, k.w_value, k.w_out))]
+        for src, dst in to:
+            copy = pltpu.make_async_copy(src, dst, k.sem.at[5 + len(outward)])
+            copy.start()
+            outward.append(copy)
+    for c in copies + outward:
+        c.wait()
+
+
+FINAL = (
+    "output", "grad_tokens", "w_query", "w_key", "w_value", "w_out", "w_inner", "w_outer", "b_query", "b_value", "b_out",
+    "gate_weight", "gate_bias", "gate_scale", "rel_table", "norm1_gain", "norm1_bias", "b_inner", "b_outer", "norm2_gain",
+    "norm2_bias",
+)
 
 
 def body(
     tokens, slot_kind, offset_bucket, w_query, b_query, w_key, w_value, b_value, w_out, b_out, gate_weight, gate_bias,
     gate_scale, rel_table, norm1_gain, norm1_bias, w_inner, b_inner, w_outer, b_outer, norm2_gain, norm2_bias, cotangent,
 ):
-    shared = (b_out, norm1_gain, norm1_bias, b_outer, norm2_gain, norm2_bias)
-    small, bucket = pack(offset_bucket, b_query, b_value, gate_scale, rel_table, b_inner, shared, gate_weight, gate_bias)
-    z = lax.axis_index("tensor")
     n_dp = lax.axis_size("dp")
     rows = tokens.shape[0]
     shape = jax.ShapeDtypeStruct
-    names = ["kinds", "bucket", "small", "tok_hbm", "cot_hbm", "wq_hbm", "wk_hbm", "wv_hbm", "wout_hbm", "wi_hbm", "wo_hbm"]
-    names += ["out_hbm", "gtok_hbm", "ra", "ri", "ro", "sg_hbm"]
+    anywhere = pl.BlockSpec(memory_space=pl.ANY)
+    vmem = pl.BlockSpec(memory_space=pltpu.VMEM)
+    smem = pl.BlockSpec(memory_space=pltpu.SMEM)
+    given = dict(
+        kinds=(smem, slot_kind), bucket=(vmem, offset_bucket.reshape(1, OFFSETS)), rel=(vmem, rel_table.T),
+        b_query=(vmem, b_query), b_value=(vmem, b_value), b_inner=(vmem, b_inner), scale=(vmem, gate_scale.reshape(1, 3)),
+        gw=(vmem, gate_weight.T), gate_bias=(vmem, gate_bias), b_out=(vmem, b_out), b_outer=(vmem, b_outer),
+        norm1_gain=(vmem, norm1_gain), norm1_bias=(vmem, norm1_bias), norm2_gain=(vmem, norm2_gain),
+        norm2_bias=(vmem, norm2_bias), tok_hbm=(anywhere, tokens), cot_hbm=(anywhere, cotangent),
+        wq_hbm=(anywhere, w_query.T.reshape(2, 96, D)), wk_hbm=(anywhere, w_key.T.reshape(2, 96, D)),
+        wv_hbm=(anywhere, w_value.T.reshape(2, 96, D)), wout_hbm=(anywhere, w_out.reshape(2, 96, D)),
+        wi_hbm=(anywhere, w_inner.reshape(8, 96, D)), wo_hbm=(anywhere, w_outer.reshape(8, 96, D)),
+    )
+    names = list(given) + ["out_hbm", "gtok_hbm", "ra", "ri", "ro", "sg_hbm"]
     scratch = []
     for name, (dims, dtype) in (COMPUTE_SCRATCH | COMM_SCRATCH).items():
         names.append(name)
         scratch.append(pltpu.VMEM(dims, dtype))
-    names.append("sgs")
-    scratch.append(pltpu.VMEM((5, 32, BIAS), f32))
     for name, dims in SEMS.items():
         names.append("sem_" + name)
         scratch.append(pltpu.SemaphoreType.DMA((2, *dims)))
     for name, count in (("sem_in", 8), ("sem_keep", 3)):
         names.append(name)
         scratch.append(pltpu.SemaphoreType.DMA((count,)))
-    anywhere = pl.BlockSpec(memory_space=pl.ANY)
-    vmem = pl.BlockSpec(memory_space=pltpu.VMEM)
-    smem = pl.BlockSpec(memory_space=pltpu.SMEM)
+    whole = shape((8, 96, D), bf16)
     out, gtok, ra, ri, ro, sg = pl.pallas_call(
         functools.partial(kernel, names),
-        in_specs=[smem, vmem, vmem] + [anywhere] * 8,
+        in_specs=[spec for spec, _ in given.values()],
         out_specs=[anywhere] * 6,
-        out_shape=[
-            shape((rows, D), bf16), shape((rows, D), bf16), shape((8, 96, D), bf16), shape((8, 96, D), bf16),
-            shape((8, 96, D), bf16), shape((32, BIAS), f32),
-        ],
+        out_shape=[shape((rows, D), bf16), shape((rows, D), bf16), whole, whole, whole, shape((16, BIAS), f32)],
         scratch_shapes=scratch,
         compiler_params=pltpu.CompilerParams(collective_id=0, has_side_effects=True, vmem_limit_bytes=VMEM_LIMIT),
-    )(
-        slot_kind, bucket, small, tokens, cotangent, w_query, w_key, w_value, w_out.reshape(2, 96, D),
-        w_inner.reshape(8, 96, D), w_outer.reshape(8, 96, D),
-    )
+    )(*[value for _, value in given.values()])
     if n_dp > 8:
         groups = [list(range(g, n_dp, 8)) for g in range(8)]
         ra, ri, ro, sg = lax.psum((ra.astype(f32), ri.astype(f32), ro.astype(f32), sg), "dp", axis_index_groups=groups)
-    ra = ra.reshape(4, 192, D).astype(f32)
-    pick = lambda v, size: lax.dynamic_slice_in_dim(v, z * size, size, 0)
-    return (
-        out,
-        gtok,
-        ra[0].T,
-        pick(sg[10], 192),
-        ra[1].T,
-        ra[2].T,
-        pick(sg[11], 192),
-        ra[3],
-        sg[0, :D],
-        jnp.concatenate([jnp.broadcast_to(jnp.sum(sg[24 + i, :D].reshape(HEADS, HEAD), 0)[:, None], (HEAD, 4)) for i in (0, 1)], 1),
-        jnp.concatenate([jnp.broadcast_to(sg[24 + i, D], (4,)) for i in (0, 1)]),
-        pick(sg[12:24, 512], 3),
-        pick(sg[12:24, :NB], 3).T,
-        sg[1, :D],
-        sg[2, :D],
-        ri.reshape(D, D).astype(f32),
-        lax.dynamic_index_in_dim(sg[6:10, :D], z, 0, False),
-        ro.reshape(D, D).astype(f32),
-        sg[3, :D],
-        sg[4, :D],
-        sg[5, :D],
+        ra, ri, ro = ra.astype(bf16), ri.astype(bf16), ro.astype(bf16)
+    vector = shape((D,), f32)
+    part = shape((2, 96, D), f32)
+    final = dict(
+        output=(anywhere, shape((rows, D), bf16)), grad_tokens=(anywhere, shape((rows, D), bf16)),
+        w_query=(anywhere, part), w_key=(anywhere, part), w_value=(anywhere, part), w_out=(anywhere, part),
+        w_inner=(anywhere, shape((8, 96, D), f32)), w_outer=(anywhere, shape((8, 96, D), f32)),
+        b_query=(vmem, shape((192,), f32)), b_value=(vmem, shape((192,), f32)), gate_weight=(vmem, shape((8, HEAD), f32)),
+        gate_bias=(vmem, shape((1, 8), f32)), gate_scale=(vmem, shape((1, 3), f32)), rel_table=(vmem, shape((3, NB), f32)),
     )
+    specs, shapes = zip(*[final.get(name, (vmem, vector)) for name in FINAL])
+    results = pl.pallas_call(
+        finish_kernel,
+        in_specs=[anywhere] * 5 + [vmem],
+        out_specs=list(specs),
+        out_shape=list(shapes),
+        scratch_shapes=[pltpu.VMEM((3, 8, 96, D), bf16), pltpu.VMEM((3, 8, 96, D), f32), pltpu.SemaphoreType.DMA((11,))],
+        compiler_params=pltpu.CompilerParams(vmem_limit_bytes=32 * 2**20),
+    )(out, gtok, ra, ri, ro, sg)
+    r = dict(zip(FINAL, results))
+    for name in ("w_query", "w_key", "w_value"):
+        r[name] = r[name].reshape(192, D).T
+    r["w_out"] = r["w_out"].reshape(192, D)
+    r["w_inner"] = r["w_inner"].reshape(D, D)
+    r["w_outer"] = r["w_outer"].reshape(D, D)
+    r["gate_weight"] = r["gate_weight"].T
+    r["gate_bias"] = r["gate_bias"].reshape(8)
+    r["gate_scale"] = r["gate_scale"].reshape(3)
+    r["rel_table"] = r["rel_table"].T
+    order = (
+        "output", "grad_tokens", "w_query", "b_query", "w_key", "w_value", "b_value", "w_out", "b_out", "gate_weight",
+        "gate_bias", "gate_scale", "rel_table", "norm1_gain", "norm1_bias", "w_inner", "b_inner", "w_outer", "b_outer",
+        "norm2_gain", "norm2_bias",
+    )
+    return tuple(r[name] for name in order)
 
 
 def solution(mesh):

time: 330 us -> 246 us (0.75); the launches traced: 325 us -> 245 us
  Pallas kernels: 282 us -> 236 us
  local copies, waits for them, and re-layouts: 37.2 us -> 8.36 us
  other arithmetic: 4.77 us -> 0 us
    pallas_call x1 -> x2, Pallas kernels: 282 us -> 236 us  [the longest x1 231 us: body(): pl.pallas_call(functools.partial(kernel, names), in_specs=[spec for spec,...]
    slice x11 -> x0, local copies, waits for them, and re-layouts: 11.9 us -> none  [the longest x1 2.81 us: body(): ra[3]]
    pad x10 -> x0, local copies, waits for them, and re-layouts: 4.82 us -> none  [row(): return jnp.pad(v, (0, BIAS - v.shape[0]))]
    unnamed x15 -> x12, local copies, waits for them, and re-layouts: 11.2 us -> 8.36 us
where the time goes in v2:
time: 246 us; the launch traced here: 245 us
  Pallas kernels  236 us (96%)
  local copies, waits for them, and re-layouts  8.36 us (3%)
    pallas_call x1, Pallas kernels, body(): pl.pallas_call(functools.partial(kernel, names), in_specs=[spec for spec,...  231 us
    unnamed x12, local copies, waits for them, and re-layouts  8.36 us
    pallas_call x1, Pallas kernels, body(): pl.pallas_call(finish_kernel, in_specs=[anywhere] * 5 + [vmem], out_specs...  5.5 us

profile of v2, /device:TPU:0, one launch (start us, length us, event | category | flops | bytes accessed | tf_op | source)
XLA Modules:
  0.0 245.3 jit_solution(9130589727083842831)
XLA Ops:
  0.7 230.6 %shard_map.382 = (bf16[1984,768]{1,0:T(8,128)(2,1)}, bf16[1984,768]{1,0:T(8,128)(2,1)}, bf16[8,96,768]{2,1,0:T(8,128)(2,1)}, bf16[8,96,768]{2,1,0:T(8,128)(2,1)}...) custom-call(s32[4]{0:T(128)} %refs_0_.1, s32[1,991]{1,0:T(1,128)} %bitcast.38, bf16[3,320]{1,0:T(4,128)(2,1)} %bitcast.39, ...), custom_call_target="tpu_custom_call" | custom-call | tf_op jit(solution)/shard_map/pallas_call | solution.py:904
  231.3 0.0 copy-start
  231.3 1.9 copy-done
  233.1 0.0 copy-start.1
  233.1 1.9 copy-done.1
  235.0 0.0 copy-start.2
  235.0 1.3 copy-done.2
  236.3 0.0 copy-start.3
  236.3 1.3 copy-done.3
  237.5 0.0 copy-start.4
  237.5 1.3 copy-done.4
  238.8 0.0 copy-start.5
  238.8 0.8 copy-done.5
  239.6 5.5 %shard_map.383 = (bf16[1984,768]{1,0:T(8,128)(2,1)}, bf16[1984,768]{1,0:T(8,128)(2,1)}, f32[2,96,768]{2,1,0:T(8,128)}, f32[2,96,768]{2,1,0:T(8,128)}, f32[2,96,7...) custom-call(bf16[1984,768]{1,0:T(8,128)(2,1)S(1)} %copy-done, ...), custom_call_target="tpu_custom_call" | custom-call | tf_op jit(solution)/shard_map/pallas_call | solution.py:926
Async XLA Ops:
  231.3 1.9 copy-start
  233.1 1.9 copy-start.1
  235.0 1.3 copy-start.2
  236.3 1.3 copy-start.3
  237.5 1.3 copy-start.4
  238.8 0.8 copy-start.5

commit v3 on v2

--- a/solution.py
+++ b/solution.py
@@ -56,10 +56,10 @@
     return ref[i].reshape(D, D)
 
 
-def rows_loop(step, body, carry):
+def rows_loop(step, body, carry, first=0, last=PAD):
     def go(c, carry):
         return body(pl.ds(pl.multiple_of(c * step, step), step), carry)
-    return lax.fori_loop(0, PAD // step, go, carry)
+    return lax.fori_loop(first // step, last // step, go, carry)
 
 
 class K:
@@ -228,7 +228,7 @@
     k.fb[...] = jnp.zeros((PAD, D), f32)
 
 
-def norm_two(k):
+def norm_two(k, part):
     b_outer, gain1, shift1 = line(k.b_outer), line(k.norm1_gain), line(k.norm1_bias)
     gain2, shift2 = line(k.norm2_gain), line(k.norm2_bias)
     def go(rows, carry):
@@ -243,9 +243,9 @@
         k.fb[rows, :] = residual_scale * g2
         return g_gain + fold(up * n), g_shift + fold(up), g_b + fold(low.astype(f32))
     zero = jnp.zeros((8, D), f32)
-    g_gain, g_shift, g_b = rows_loop(32, go, (zero, zero, zero))
+    g_gain, g_shift, g_b = rows_loop(32, go, (zero, zero, zero), 256 * part, 256 * part + 256)
     for row, v in ((3, g_b), (4, g_gain), (5, g_shift)):
-        k.sg[row : row + 1, 0:D] = jnp.sum(v, axis=0, keepdims=True)
+        k.sg[row : row + 1, 0:D] += jnp.sum(v, axis=0, keepdims=True)
 
 
 def feed_back(k, p):
@@ -343,29 +343,32 @@
     rel = dot_t(goff, k.hot[...].astype(f32), precision=highest)
     k.sg[12:24, 0:NB] = rel[0:HEADS]
     k.sg[12:24, 512:640] = jnp.broadcast_to(gscale, (16, 128))[0:HEADS]
-    return dot(dz.T, weights)
+    for t, src in ((0, k.q), (2, k.v)):
+        row = jnp.sum(fold(mixed_all(src).astype(f32)), axis=0, keepdims=True)
+        for p in range(4):
+            at, lane = (6 + p, D) if t == 0 else (12 + 3 * p, 640)
+            k.sg[at : at + 1, lane : lane + 192] = row[:, 192 * p : 192 * p + 192]
+    k.fa[...] = dot(dz.T, weights)
 
 
 def grad_input(k):
-    k.fa[...] = gate_back(k)
     for t, src in ((0, k.q), (1, k.k), (2, k.v)):
         k.fa[...] += dot(mixed_all(src), wide(k.wa, t))
+
+
+def grad_rows(k, part):
     def go(rows, _):
         k.gtok[rows, :] = (k.fb[rows, :] + k.fa[rows, :]).astype(bf16)
         return 0
-    rows_loop(32, go, 0)
-
-
-def grad_projections(k):
-    for t, src in ((0, k.q), (1, k.k), (2, k.v)):
-        g = mixed_all(src)
-        if t != 1:
-            row = jnp.sum(fold(g.astype(f32)), axis=0, keepdims=True)
-            for p in range(4):
-                at, lane = (6 + p, D) if t == 0 else (12 + 3 * p, 640)
-                k.sg[at : at + 1, lane : lane + 192] = row[:, 192 * p : 192 * p + 192]
-        k.wa[t] = dot_l(g, k.tok[...]).astype(bf16).reshape(4, 2, 96, D)
-    k.wa[3] = dot_l(mixed_all(k.mixed), k.gb[...]).astype(bf16).reshape(4, 2, 96, D)
+    rows_loop(32, go, 0, 256 * part, 256 * part + 256)
+
+
+def grad_projections(k, part):
+    own = lambda ref: jnp.concatenate([ref[3 * part + i] for i in range(3)], axis=1)
+    for t, src, right in ((0, k.q, k.tok), (1, k.k, k.tok), (2, k.v, k.tok), (3, k.mixed, k.gb)):
+        g = dot_l(own(src), right[...]).astype(bf16).reshape(2, 2, 96, D)
+        for i in range(2):
+            k.wa[t, 2 * part + i] = g[i]
 
 
 def each(n, fn, k):
@@ -391,12 +394,12 @@
 MESH = pl.DeviceIdType.MESH
 BLOCKS = (0, 1, 2)
 SEMS = dict(
-    wz=(3, 3), w1=(3, 3), w2=(3, 3, 2), w3=(3, 3), sm=(3,), rows=(2, 2, 3), r1=(3, 4), r2=(3, 4, 2), r3=(3, 4),
-    r4=(3, 3), a1=(3,), a2=(3, 2), a3=(3,), sg=(5,),
+    wz=(3, 3), w1=(3, 3), w2=(3, 3, 2), w3=(3, 3), sm=(3,), rows=(2, 2, 6), r1=(3, 4), r2=(3, 4, 2), r3=(3, 4),
+    r4=(3, 2, 3), a1=(3,), a2=(3, 2), a3=(3,), sg=(6,),
 )
 COMM_SCRATCH = dict(
     rb1a=((4, 2, 2, 96, D), bf16), rb1=((2, 4, 4, 96, D), bf16), rb2=((3, 4, 2, 96, D), bf16),
-    rb3=((3, 4, 96, D), bf16), rb4=((3, 3, 96, D), bf16), sgr=((5, 32, BIAS), f32), sgs=((5, 32, BIAS), f32), fin=((16, BIAS), f32),
+    rb3=((3, 4, 96, D), bf16), rb4=((3, 2, 3, 96, D), bf16), sgr=((5, 32, BIAS), f32), sgs=((6, 32, BIAS), f32), fin=((16, BIAS), f32),
 )
 
 
@@ -468,19 +471,20 @@
         ref = self.k.sm.at[self.z]
         return self.copy("sm", (d - 1,), ref, ref, (self.dp, self.ahead(d)))
 
-    def rows(self, a, way, j):
+    def rows(self, a, way, n):
         source, result = ((self.k.out, self.k.out_hbm), (self.k.gtok, self.k.gtok_hbm))[a]
+        j, (start, size) = n // 2, PARTS[n % 2]
         slot = self.z - j if way == 0 else self.z + j
         to = self.z + 1 if way == 0 else self.z - 1
-        at = result.at[pl.ds(pl.multiple_of(slot * SEQ, 16), SEQ)]
-        return self.copy("rows", (a, way, j), source.at[pl.ds(0, SEQ)] if j == 0 else at, at, (self.dp, to))
-
-    def sends(self, way, j):
-        z = self.z
+        at = result.at[pl.ds(pl.multiple_of(slot * SEQ + start, 16), size)]
+        return self.copy("rows", (a, way, n), source.at[pl.ds(start, size)] if j == 0 else at, at, (self.dp, to))
+
+    def sends(self, way, n):
+        z, j = self.z, n // 2
         return (z <= 2) & (z >= j) if way == 0 else (z >= 1) & (z + j <= 3)
 
-    def receives(self, way, j):
-        z = self.z
+    def receives(self, way, n):
+        z, j = self.z, n // 2
         return z >= 1 + j if way == 0 else z + 1 + j <= 3
 
     def r1(self, b, p):
@@ -493,9 +497,9 @@
     def r3(self, b, p):
         return self.copy("r3", (b, p), self.chunk(b, p, self.e2), self.k.rb3.at[b, p], self.two)
 
-    def r4(self, b, d):
-        to = self.ahead(d)
-        return self.copy("r4", (b, d - 1), self.chunk(b, to, self.e), self.k.rb4.at[b, d - 1], (self.dp, to))
+    def r4(self, b, way, p):
+        to, i = (self.z + 1, p - 1) if way == 0 else (self.z - 1, p)
+        return self.copy("r4", (b, way, i), self.chunk(b, p, self.e), self.k.rb4.at[b, way, i], (self.dp, to))
 
     def result(self, b, e):
         return (self.k.ra, self.k.ri, self.k.ro)[b].at[e]
@@ -515,8 +519,13 @@
         return self.copy("a3", (b,), ref, ref, self.core)
 
     def sg(self, i):
-        device = (self.core, self.x, self.y, (self.dp, self.flip(1)), (self.dp, self.flip(2)))[i]
-        return self.copy("sg", (i,), self.k.sg if i == 0 else self.k.sgs.at[i - 1], self.k.sgr.at[i], device)
+        k, half = self.k, pl.ds(16 * self.c, 16)
+        if i < 3:
+            return self.copy("sg", (i,), k.sgs.at[i], k.sgr.at[i], (self.core, self.x, self.y)[i])
+        if i < 5:
+            device = (self.dp, self.flip(1 if i == 3 else 2))
+            return self.copy("sg", (i,), k.sgs.at[i, half], k.sgr.at[i, half], device)
+        return self.copy("sg", (i,), k.sgs.at[5, half], k.sgs.at[5, half], self.core)
 
     def flip(self, bit):
         return self.z + bit * (1 - 2 * ((self.z // bit) % 2))
@@ -536,7 +545,9 @@
 
 
 PIECES = ((0, 1), (0, 2), (0, 3), (1, 1), (2, 1), (1, 2), (2, 2), (1, 3), (2, 3))
-WINDOW = 3
+WINDOW = 2
+PARTS = ((0, 256), (256, 240))
+ORDER = (3, 0, 2, 1)
 
 
 def weight_step(net, t):
@@ -551,13 +562,13 @@
         net.w1(b, d).wait_recv()
         net.w2(b, d, 0).start()
         net.w2(b, d, 1).start()
-    if 0 <= t - 2 < 9:
-        b, d = PIECES[t - 2]
+    if 0 <= t - 3 < 9:
+        b, d = PIECES[t - 3]
         net.w2(b, d, 0).wait_recv()
         net.w2(b, d, 1).wait_recv()
         net.w3(b, d).start()
-    if 0 <= t - 3 < 9:
-        net.w3(*PIECES[t - 3]).wait_recv()
+    if 0 <= t - 4 < 9:
+        net.w3(*PIECES[t - 4]).wait_recv()
 
 
 def weights_sent(net):
@@ -569,18 +580,21 @@
         net.w3(b, d).wait_send()
 
 
-def rows_step(net, a, j):
+def rows_own(net, a, part):
     for way in (0, 1):
-        if j > 0:
-            when(net.receives(way, j - 1), lambda: net.rows(a, way, j - 1).wait_recv())
-        if j < 3:
-            when(net.sends(way, j), lambda: net.rows(a, way, j).start())
+        when(net.sends(way, part), lambda: net.rows(a, way, part).start())
+
+
+def rows_next(net, a, way, n):
+    when(net.receives(way, n - 1), lambda: net.rows(a, way, n - 1).wait_recv())
+    if n + 1 < 6:
+        when(net.sends(way, n + 1), lambda: net.rows(a, way, n + 1).start())
 
 
 def rows_sent(net, a):
-    for j in range(3):
+    for n in range(6):
         for way in (0, 1):
-            when(net.sends(way, j), lambda: net.rows(a, way, j).wait_send())
+            when(net.sends(way, n), lambda: net.rows(a, way, n).wait_send())
 
 
 def add(net, b, p, e, ref):
@@ -608,24 +622,33 @@
     add(net, b, p, net.e, net.k.rb2.at[b, p, 0])
 
 
-def eighths(net, b, i):
-    p = net.ahead(1 + i)
+def eighths(net, b, p):
     net.r3(b, p).wait_recv()
     add(net, b, p, net.e, net.k.rb3.at[b, p])
-    if i < 3:
-        net.r4(b, 1 + i).start()
+    if p > 0:
+        when(net.z == 0, lambda: net.r4(b, 0, p).start())
+    if p < 3:
+        when(net.z == 3, lambda: net.r4(b, 1, p).start())
+
+
+def chain(net, b, p):
+    def link(way, i):
+        net.r4(b, way, p).wait_recv()
+        add(net, b, p, net.e, net.k.rb4.at[b, way, i])
+        net.r4(b, way, p).start()
+    if p > 1:
+        when((net.z > 0) & (net.z < p), lambda: link(0, p - 1))
+    if p < 2:
+        when((net.z > p) & (net.z < 3), lambda: link(1, p))
 
 
 def over_z(net, b):
-    k = net.k
-    for d in (1, 2, 3):
-        net.r4(b, d).wait_recv()
-    own = k.wa[net.e // 2, net.z, net.e % 2] if b == 0 else net.block(b)[net.z, net.e]
-    total = (own.astype(f32) + k.rb4[b, 0].astype(f32)) + (k.rb4[b, 1].astype(f32) + k.rb4[b, 2].astype(f32))
-    if b == 0:
-        k.wa[net.e // 2, net.z, net.e % 2] = total.astype(bf16)
-    else:
-        net.block(b)[net.z, net.e] = total.astype(bf16)
+    k, z = net.k, net.z
+    def last(way, i):
+        net.r4(b, way, z).wait_recv()
+        add(net, b, z, net.e, k.rb4.at[b, way, i])
+    when(z > 0, lambda: last(0, z - 1))
+    when(z < 3, lambda: last(1, z))
     net.keep(b).start()
     net.a1(b).start()
     net.a2(b, 0).start()
@@ -650,22 +673,91 @@
         net.r2(b, p, 0).wait_send()
         net.r2(b, p, 1).wait_send()
         net.r3(b, p).wait_send()
-    for d in (1, 2, 3):
-        net.r4(b, d).wait_send()
+    for p in range(4):
+        when(net.z < p, lambda: net.r4(b, 0, p).wait_send())
+        when(net.z > p, lambda: net.r4(b, 1, p).wait_send())
     net.a1(b).wait_send()
     net.a2(b, 0).wait_send()
     net.a2(b, 1).wait_send()
     net.a3(b).wait_send()
 
 
+def halves_out(net, b, p):
+    net.r1(b, p).start()
+
+
 def small_step(net, i):
-    k = net.k
-    if i > 0:
+    k, half = net.k, pl.ds(16 * net.c, 16)
+    if i == 0:
+        k.sgs[0] = k.sg[...]
+    else:
         net.sg(i - 1).wait_recv()
-        mine = k.sg[...] if i == 1 else k.sgs[i - 2]
-        k.sgs[i - 1] = mine + k.sgr[i - 1]
-    if i < 5:
+    if 0 < i < 4:
+        k.sgs[i] = k.sgs[i - 1] + k.sgr[i - 1]
+    elif 3 < i < 6:
+        k.sgs[i, half, :] = k.sgs[i - 1, half, :] + k.sgr[i - 1, half, :]
+    if i < 6:
         net.sg(i).start()
+
+
+STEPS = dict(
+    rows_own=rows_own, rows_next=rows_next, halves_out=halves_out, halves=halves, quarters=quarters, eighths=eighths,
+    chain=chain, over_z=over_z, around=around, to_core=to_core, small=small_step,
+)
+PLAN = {
+    "n2a": [
+        ("rows_own", 0, 0),
+    ],
+    "n2b": [
+        ("rows_own", 0, 1),
+    ],
+    "fb0": [
+        ("halves_out", 1, 3),
+    ],
+    "fb1": [
+        ("halves_out", 2, 0), ("rows_next", 0, 0, 1), ("halves", 1, 3), ("halves_out", 1, 0),
+    ],
+    "fb2": [
+        ("halves_out", 2, 2), ("halves", 2, 0), ("rows_next", 0, 1, 1), ("halves_out", 2, 3),
+    ],
+    "fb3": [
+        ("halves_out", 1, 1), ("rows_next", 0, 1, 2), ("halves", 2, 2), ("halves", 1, 0), ("halves_out", 1, 2),
+        ("halves_out", 2, 1), ("rows_next", 0, 0, 2), ("quarters", 2, 0),
+    ],
+    "ab0": [
+        ("quarters", 2, 2), ("rows_next", 0, 1, 3), ("halves", 2, 3),
+    ],
+    "ab2": [
+        ("halves", 1, 1), ("rows_next", 0, 0, 3), ("eighths", 2, 2), ("halves", 1, 2),
+    ],
+    "gateb": [
+        ("chain", 2, 2),
+    ],
+    "gin": [
+        ("rows_own", 1, 0), ("quarters", 2, 3), ("quarters", 1, 0),
+    ],
+    "gin2": [
+        ("rows_next", 0, 1, 4), ("quarters", 1, 2),
+    ],
+    "gp0": [
+        ("halves_out", 0, 0), ("eighths", 2, 0), ("halves_out", 0, 1), ("halves", 2, 1), ("quarters", 1, 3),
+        ("small", 0), ("quarters", 1, 1), ("rows_own", 1, 1),
+    ],
+    "gp1": [
+        ("halves_out", 0, 2), ("halves", 0, 1), ("halves_out", 0, 3), ("rows_next", 1, 0, 1), ("eighths", 1, 2),
+        ("eighths", 1, 0), ("quarters", 2, 1), ("halves", 0, 3), ("rows_next", 1, 1, 1), ("rows_next", 1, 0, 2),
+        ("halves", 0, 0), ("small", 1), ("eighths", 2, 1), ("quarters", 0, 3), ("quarters", 0, 1), ("eighths", 1, 1),
+        ("halves", 0, 2), ("rows_next", 0, 1, 5), ("rows_next", 0, 1, 6), ("chain", 2, 0), ("chain", 1, 2),
+        ("eighths", 2, 3), ("quarters", 0, 0), ("rows_next", 0, 0, 4), ("chain", 1, 0), ("eighths", 0, 3),
+        ("small", 2), ("chain", 2, 1), ("eighths", 1, 3), ("rows_next", 1, 1, 2), ("eighths", 0, 1), ("chain", 2, 3),
+        ("rows_next", 1, 1, 3), ("quarters", 0, 2), ("eighths", 0, 0), ("over_z", 2), ("chain", 1, 1),
+        ("chain", 0, 3), ("chain", 0, 1), ("chain", 1, 3), ("eighths", 0, 2), ("around", 2), ("chain", 0, 2),
+        ("over_z", 1), ("rows_next", 1, 0, 3), ("chain", 0, 0), ("small", 3), ("to_core", 2), ("around", 1),
+        ("over_z", 0), ("small", 4), ("to_core", 1), ("rows_next", 1, 1, 4), ("rows_next", 1, 1, 5), ("around", 0),
+        ("rows_next", 0, 0, 5), ("rows_next", 1, 0, 4), ("rows_next", 1, 0, 5), ("small", 5), ("to_core", 0),
+        ("rows_next", 1, 1, 6), ("small", 6), ("rows_next", 1, 0, 6), ("rows_next", 0, 0, 6),
+    ],
+}
 
 
 def kernel(names, *refs):
@@ -708,107 +800,70 @@
     weight_step(net, 3)
     weight_step(net, 4)
     weight_step(net, 5)
+    weight_step(net, 6)
     project(k)
 
     def forward(pr):
         attend(k, pr)
-        when(pr == 1, lambda: weight_step(net, 6))
-        when(pr == 4, lambda: weight_step(net, 7))
+        when(pr == 1, lambda: weight_step(net, 7))
+        when(pr == 4, lambda: weight_step(net, 8))
     loop(PAIRS, forward)
     norm_one(k)
-    weight_step(net, 8)
+    weight_step(net, 9)
     feed_init(k)
 
     def layer_two(i):
-        when(i == 2, lambda: weight_step(net, 9))
-        when(i == 3, lambda: (weight_step(net, 10), weight_step(net, 11)))
+        when(i == 2, lambda: weight_step(net, 10))
+        when(i == 3, lambda: (weight_step(net, 11), weight_step(net, 12)))
         feed(k, net.behind(i))
     loop(4, layer_two)
-    norm_two(k)
     here = [
         pltpu.make_async_copy(k.out.at[pl.ds(0, SEQ)], k.out_hbm.at[own_rows], k.sem_in.at[0]),
         pltpu.make_async_copy(k.gtok.at[pl.ds(0, SEQ)], k.gtok_hbm.at[own_rows], k.sem_in.at[1]),
     ]
+    run = lambda key: [STEPS[name](net, *given) for name, *given in PLAN.get(key, ())]
+    norm_two(k, 0)
+    run("n2a")
+    norm_two(k, 1)
+    run("n2b")
     here[0].start()
-    rows_step(net, 0, 0)
     weights_sent(net)
 
     def layer_two_back(i):
-        p = net.ahead(1 + i)
-        feed_back(k, p)
-        net.r1(2, p).start()
-        net.r1(1, p).start()
-        def last():
-            before = net.ahead(i)
-            halves(net, 2, before)
-            halves(net, 1, before)
-        when(i > 0, last)
+        feed_back(k, (1 - i % 2) * (3 - i // 2) + (i % 2) * (i // 2))
+        for n in range(4):
+            when(i == n, lambda: run("fb" + str(n)))
     loop(4, layer_two_back)
-    rows_step(net, 0, 1)
     norm_one_back(k)
-    both = lambda fn, i: (fn(net, 2, net.ahead(1 + i)), fn(net, 1, net.ahead(1 + i)))
-    pass_on = lambda i: (eighths(net, 2, i), eighths(net, 1, i))
-    both(halves, 3)
-    both(quarters, 0)
+    run("n1b")
 
     def backward(pr):
         attend_back(k, pr)
-        when(pr == 3, lambda: (both(quarters, 1), pass_on(0)))
-        when(pr == 5, lambda: rows_step(net, 0, 2))
+        for n in range(PAIRS):
+            when(pr == n, lambda: run("ab" + str(n)))
     loop(PAIRS, backward)
+    gate_back(k)
+    run("gateb")
     grad_input(k)
+    grad_rows(k, 0)
+    run("gin")
+    grad_rows(k, 1)
     here[1].start()
-    rows_step(net, 1, 0)
-    both(quarters, 2)
-    pass_on(1)
-    grad_projections(k)
-    for i in range(4):
-        net.r1(0, net.ahead(1 + i)).start()
-    small_step(net, 0)
-    both(quarters, 3)
-    pass_on(2)
-    halves(net, 0, net.ahead(1))
-    halves(net, 0, net.ahead(2))
-    rows_step(net, 0, 3)
-    small_step(net, 1)
-    pass_on(3)
-    halves(net, 0, net.ahead(3))
-    halves(net, 0, net.ahead(4))
-    rows_step(net, 1, 1)
-    small_step(net, 2)
-    quarters(net, 0, net.ahead(1))
-    quarters(net, 0, net.ahead(2))
-    eighths(net, 0, 0)
-    small_step(net, 3)
-    quarters(net, 0, net.ahead(3))
-    eighths(net, 0, 1)
-    over_z(net, 2)
-    over_z(net, 1)
-    quarters(net, 0, net.ahead(4))
-    eighths(net, 0, 2)
-    small_step(net, 4)
-    eighths(net, 0, 3)
-    around(net, 2)
-    around(net, 1)
-    rows_step(net, 1, 2)
-    over_z(net, 0)
-    to_core(net, 2)
-    to_core(net, 1)
-    small_step(net, 5)
+    run("gin2")
+    for part in (0, 1):
+        grad_projections(k, part)
+        run("gp" + str(part))
     k.fin[...] = jnp.zeros((16, BIAS), f32)
-    k.fin[0:6, :] = k.sgs[4, 0:6, :]
-    k.fin[6:7, :] = k.sgs[4, pl.ds(6 + z, 1), :]
+    k.fin[0:6, :] = k.sgs[5, 0:6, :]
+    k.fin[6:7, :] = k.sgs[5, pl.ds(6 + z, 1), :]
     for i in range(3):
-        k.fin[8 + i : 9 + i, :] = k.sgs[4, pl.ds(12 + 3 * z + i, 1), :]
-    k.fin[11:13, :] = k.sgs[4, 24:26, :]
+        k.fin[8 + i : 9 + i, :] = k.sgs[5, pl.ds(12 + 3 * z + i, 1), :]
+    k.fin[11:13, :] = k.sgs[5, 24:26, :]
     finish = pltpu.make_async_copy(k.fin, k.sg_hbm, k.sem_in.at[2])
     finish.start()
-    around(net, 0)
-    to_core(net, 0)
-    rows_step(net, 1, 3)
     for b in (2, 1, 0):
         gradients_sent(net, b)
-    for i in range(5):
+    for i in range(6):
         net.sg(i).wait_send()
     for d in (1, 2, 3):
         net.sm(d).wait_send()
@@ -820,15 +875,16 @@
 
 
 def finish_kernel(out, gtok, ra, ri, ro, sg, *rest):
-    names = FINAL + ("stage", "wide", "sem")
+    names = FINAL + ("stage", "wide", "rows", "sem")
     k = K()
     for name, ref in zip(names, rest):
         setattr(k, name, ref)
-    copies = [pltpu.make_async_copy(out, k.output, k.sem.at[0]), pltpu.make_async_copy(gtok, k.grad_tokens, k.sem.at[1])]
-    for c in copies:
-        c.start()
     inward = [pltpu.make_async_copy(src, k.stage.at[i], k.sem.at[2 + i]) for i, src in enumerate((ri, ro, ra))]
     for c in inward:
+        c.start()
+    pairs = [(out, k.rows.at[0], k.output), (gtok, k.rows.at[1], k.grad_tokens)]
+    copies = [pltpu.make_async_copy(src, via, k.sem.at[i]) for i, (src, via, _) in enumerate(pairs)]
+    for c in copies:
         c.start()
     row = lambda r, lane, n: sg[r : r + 1, lane : lane + n].reshape(n)
     k.b_out[...], k.norm1_gain[...], k.norm1_bias[...] = row(0, 0, D), row(1, 0, D), row(2, 0, D)
@@ -858,7 +914,11 @@
             copy = pltpu.make_async_copy(src, dst, k.sem.at[5 + len(outward)])
             copy.start()
             outward.append(copy)
-    for c in copies + outward:
+    for i, (c, (_, via, dst)) in enumerate(zip(copies, pairs)):
+        c.wait()
+        outward.append(pltpu.make_async_copy(via, dst, k.sem.at[i]))
+        outward[-1].start()
+    for c in outward:
         c.wait()
 
 
@@ -928,8 +988,8 @@
         in_specs=[anywhere] * 5 + [vmem],
         out_specs=list(specs),
         out_shape=list(shapes),
-        scratch_shapes=[pltpu.VMEM((3, 8, 96, D), bf16), pltpu.VMEM((3, 8, 96, D), f32), pltpu.SemaphoreType.DMA((11,))],
-        compiler_params=pltpu.CompilerParams(vmem_limit_bytes=32 * 2**20),
+        scratch_shapes=[pltpu.VMEM((3, 8, 96, D), bf16), pltpu.VMEM((3, 8, 96, D), f32), pltpu.VMEM((2, rows, D), bf16), pltpu.SemaphoreType.DMA((11,))],
+        compiler_params=pltpu.CompilerParams(vmem_limit_bytes=VMEM_LIMIT),
     )(out, gtok, ra, ri, ro, sg)
     r = dict(zip(FINAL, results))
     for name in ("w_query", "w_key", "w_value"):

time: 246 us -> 207 us (0.84)
  Pallas kernels: 236 us -> 206 us
  local copies, waits for them, and re-layouts: 8.36 us -> 0 us
    pallas_call x1, Pallas kernels: 231 us -> 196 us  [body(): pl.pallas_call(functools.partial(kernel, names), in_specs=[spec for spec,...]
    unnamed x12 -> x0, local copies, waits for them, and re-layouts: 8.36 us -> none
    pallas_call x1, Pallas kernels: 5.5 us -> 10.3 us  [body(): pl.pallas_call(finish_kernel, in_specs=[anywhere] * 5 + [vmem], out_specs...]
where the time goes in v3:
time: 207 us
  Pallas kernels  206 us (100%)
    pallas_call x1, Pallas kernels, body(): pl.pallas_call(functools.partial(kernel, names), in_specs=[spec for spec,...  196 us
    pallas_call x1, Pallas kernels, body(): pl.pallas_call(finish_kernel, in_specs=[anywhere] * 5 + [vmem], out_specs...  10.3 us

profile of v3, /device:TPU:0, one launch (start us, length us, event | category | flops | bytes accessed | tf_op | source)
XLA Modules:
  0.0 207.3 jit_solution(7147327577514759911)
XLA Ops:
  0.7 196.2 %shard_map.382 = (bf16[1984,768]{1,0:T(8,128)(2,1)}, bf16[1984,768]{1,0:T(8,128)(2,1)}, bf16[8,96,768]{2,1,0:T(8,128)(2,1)}, bf16[8,96,768]{2,1,0:T(8,128)(2,1)}...) custom-call(s32[4]{0:T(128)} %refs_0_.1, s32[1,991]{1,0:T(1,128)} %bitcast.38, bf16[3,320]{1,0:T(4,128)(2,1)} %bitcast.39, ...), custom_call_target="tpu_custom_call" | custom-call | tf_op jit(solution)/shard_map/pallas_call | solution.py:964
  196.8 10.3 %shard_map.383 = (bf16[1984,768]{1,0:T(8,128)(2,1)}, bf16[1984,768]{1,0:T(8,128)(2,1)}, f32[2,96,768]{2,1,0:T(8,128)}, f32[2,96,768]{2,1,0:T(8,128)}, f32[2,96,7...) custom-call(bf16[1984,768]{1,0:T(8,128)(2,1)} %get-tuple-element.48., ...), custom_call_target="tpu_custom_call" | custom-call | tf_op jit(solution)/shard_map/pallas_call | solution.py:986

commit v4 on v3

--- a/solution.py
+++ b/solution.py
@@ -19,6 +19,7 @@
 VMEM_LIMIT = 64 * 2**20 - 2**16
 OFFSETS = 991
 HALF = SEQ // 2
+PARTS = ((0, 128), (128, 320), (320, PAD))
 f32 = jnp.float32
 bf16 = jnp.bfloat16
 residual_scale = 24.0**0.25
@@ -211,7 +212,7 @@
     rows_loop(32, go, 0)
 
 
-def feed(k, p):
+def feed_in(k, p):
     k.fa[...] = dot(k.hid[...], wide(k.wi, p))
     b = k.sm[p, 4:5, 0:D]
     def go(rows, _):
@@ -221,11 +222,10 @@
         k.dg[p, rows, :] = (half + x * (jnp.exp(-0.5 * x * x) * (1.0 / math.sqrt(2.0 * math.pi)))).astype(bf16)
         return 0
     rows_loop(16, go, 0)
-    k.fb[...] += dot(k.act[p], wide(k.wo, p))
-
-
-def feed_init(k):
-    k.fb[...] = jnp.zeros((PAD, D), f32)
+
+
+def feed_out(k, p, first=0, last=PAD):
+    k.fb[first:last, :] += dot(k.act[p, first:last, :], wide(k.wo, p))
 
 
 def norm_two(k, part):
@@ -243,7 +243,7 @@
         k.fb[rows, :] = residual_scale * g2
         return g_gain + fold(up * n), g_shift + fold(up), g_b + fold(low.astype(f32))
     zero = jnp.zeros((8, D), f32)
-    g_gain, g_shift, g_b = rows_loop(32, go, (zero, zero, zero), 256 * part, 256 * part + 256)
+    g_gain, g_shift, g_b = rows_loop(32, go, (zero, zero, zero), *PARTS[part])
     for row, v in ((3, g_b), (4, g_gain), (5, g_shift)):
         k.sg[row : row + 1, 0:D] += jnp.sum(v, axis=0, keepdims=True)
 
@@ -276,13 +276,12 @@
     g_gain, g_shift, g_b = rows_loop(32, go, (zero, zero, zero))
     for row, v in ((0, g_b), (1, g_gain), (2, g_shift)):
         k.sg[row : row + 1, 0:D] = jnp.sum(v, axis=0, keepdims=True)
-    gm = dot_t(k.gb[...], wide(k.wa, 3)).astype(bf16)
-    for pr in range(PAIRS):
-        k.gm[pr] = gm[:, 128 * pr : 128 * pr + 128]
+    k.hid[...] = dot_t(k.gb[...], wide(k.wa, 3)).astype(bf16)
 
 
 def attend_back(k, pr):
-    qp, kp, vp, gm = k.q[pr], k.k[pr], k.v[pr], k.gm[pr]
+    qp, kp, vp = k.q[pr], k.k[pr], k.v[pr]
+    gm = k.hid[:, pl.ds(pl.multiple_of(128 * pr, 128), 128)]
     tq = tk = tv = None
     for hh in range(2):
         h = pr * 2 + hh
@@ -358,9 +357,9 @@
 
 def grad_rows(k, part):
     def go(rows, _):
-        k.gtok[rows, :] = (k.fb[rows, :] + k.fa[rows, :]).astype(bf16)
+        k.cot[rows, :] = (k.fb[rows, :] + k.fa[rows, :]).astype(bf16)
         return 0
-    rows_loop(32, go, 0, 256 * part, 256 * part + 256)
+    rows_loop(32, go, 0, *PARTS[part])
 
 
 def grad_projections(k, part):
@@ -385,8 +384,8 @@
     v=((PAIRS, PAD, 128), bf16), s=((PAD, PAD), f32), p=((HEADS, PAD, PAD), bf16), mixed=((PAIRS, PAD, 128), bf16),
     fa=((PAD, D), f32), fb=((PAD, D), f32), n1=((PAD, D), f32), inv1=((PAD, 128), f32), hid=((PAD, D), bf16),
     act=((4, PAD, D), bf16), dg=((4, PAD, D), bf16), out=((PAD, D), bf16), gb=((PAD, D), bf16),
-    gm=((PAIRS, PAD, 128), bf16), gs=((PAD, PAD), bf16), a=((128, BIAS), f32), ggate=((HEADS, 1, PAD), f32),
-    goff=((HEADS, 1, BIAS), f32), gtok=((PAD, D), bf16), sg=((32, BIAS), f32),
+    gs=((PAD, PAD), bf16), a=((128, BIAS), f32), ggate=((HEADS, 1, PAD), f32),
+    goff=((HEADS, 1, BIAS), f32), sg=((32, BIAS), f32),
     wa=((4, 4, 2, 96, D), bf16), wi=((4, 8, 96, D), bf16), wo=((4, 8, 96, D), bf16),
 )
 
@@ -394,7 +393,7 @@
 MESH = pl.DeviceIdType.MESH
 BLOCKS = (0, 1, 2)
 SEMS = dict(
-    wz=(3, 3), w1=(3, 3), w2=(3, 3, 2), w3=(3, 3), sm=(3,), rows=(2, 2, 6), r1=(3, 4), r2=(3, 4, 2), r3=(3, 4),
+    wz=(3, 2, 3), w1=(3, 2, 3), w2=(3, 2, 3, 2), w3=(3, 2, 3), sm=(3,), rows=(2, 2, 9), r1=(3, 4), r2=(3, 4, 2), r3=(3, 4),
     r4=(3, 2, 3), a1=(3,), a2=(3, 2), a3=(3,), sg=(6,),
 )
 COMM_SCRATCH = dict(
@@ -440,7 +439,9 @@
         peers = [self.core, self.one, self.two] + [(self.dp, self.ahead(dz)) for dz in (1, 2, 3)]
         for peer in peers:
             pl.semaphore_signal(barrier, inc=1, device_id=peer, device_id_type=MESH)
-        pl.semaphore_wait(barrier, len(peers))
+
+    def all_here(self):
+        pl.semaphore_wait(pltpu.get_barrier_semaphore(), 6)
 
     def block(self, b):
         return (self.k.wa, self.k.wi, self.k.wo)[b]
@@ -451,41 +452,43 @@
     def side(self, b, p, c):
         return self.block(b).at[pl.ds(2 * c, 2), p] if b == 0 else self.block(b).at[p, pl.ds(4 * c, 4)]
 
-    def wz(self, b, d):
-        ref = self.chunk(b, self.z, self.e)
-        return self.copy("wz", (b, d - 1), ref, ref, (self.dp, self.ahead(d)))
-
-    def w1(self, b, d):
-        ref = self.chunk(b, self.behind(d), self.e)
-        return self.copy("w1", (b, d - 1), ref, ref, self.one)
-
-    def w2(self, b, d, i):
-        ref = self.chunk(b, self.behind(d), (self.e, self.e1)[i])
-        return self.copy("w2", (b, d - 1, i), ref, ref, self.two)
-
-    def w3(self, b, d):
-        ref = self.side(b, self.behind(d), self.c)
-        return self.copy("w3", (b, d - 1), ref, ref, self.core)
+    def plane(self, way, j):
+        return self.z - 1 - j if way == 0 else self.z + 1 + j
+
+    def wz(self, b, way, j):
+        ref = self.chunk(b, self.plane(way, j - 1), self.e)
+        return self.copy("wz", (b, way, j), ref, ref, (self.dp, self.z + 1 if way == 0 else self.z - 1))
+
+    def w1(self, b, way, j):
+        ref = self.chunk(b, self.plane(way, j), self.e)
+        return self.copy("w1", (b, way, j), ref, ref, self.one)
+
+    def w2(self, b, way, j, i):
+        ref = self.chunk(b, self.plane(way, j), (self.e, self.e1)[i])
+        return self.copy("w2", (b, way, j, i), ref, ref, self.two)
+
+    def w3(self, b, way, j):
+        ref = self.side(b, self.plane(way, j), self.c)
+        return self.copy("w3", (b, way, j), ref, ref, self.core)
 
     def sm(self, d):
         ref = self.k.sm.at[self.z]
         return self.copy("sm", (d - 1,), ref, ref, (self.dp, self.ahead(d)))
 
     def rows(self, a, way, n):
-        source, result = ((self.k.out, self.k.out_hbm), (self.k.gtok, self.k.gtok_hbm))[a]
-        j, (start, size) = n // 2, PARTS[n % 2]
+        source, result = ((self.k.out, self.k.out_hbm), (self.k.cot, self.k.gtok_hbm))[a]
+        j, (start, stop) = n // 3, PARTS[n % 3]
+        size = min(stop, SEQ) - start
         slot = self.z - j if way == 0 else self.z + j
         to = self.z + 1 if way == 0 else self.z - 1
         at = result.at[pl.ds(pl.multiple_of(slot * SEQ + start, 16), size)]
         return self.copy("rows", (a, way, n), source.at[pl.ds(start, size)] if j == 0 else at, at, (self.dp, to))
 
-    def sends(self, way, n):
-        z, j = self.z, n // 2
-        return (z <= 2) & (z >= j) if way == 0 else (z >= 1) & (z + j <= 3)
-
-    def receives(self, way, n):
-        z, j = self.z, n // 2
-        return z >= 1 + j if way == 0 else z + 1 + j <= 3
+    def sends(self, way, j):
+        return (self.z <= 2) & (self.z >= j) if way == 0 else (self.z >= 1) & (self.z + j <= 3)
+
+    def receives(self, way, j):
+        return self.z >= 1 + j if way == 0 else self.z + 1 + j <= 3
 
     def r1(self, b, p):
         dst = self.k.rb1a.at[p] if b == 0 else self.k.rb1.at[b - 1, p]
@@ -544,57 +547,71 @@
         fn()
 
 
-PIECES = ((0, 1), (0, 2), (0, 3), (1, 1), (2, 1), (1, 2), (2, 2), (1, 3), (2, 3))
-WINDOW = 2
-PARTS = ((0, 256), (256, 240))
 ORDER = (3, 0, 2, 1)
 
 
-def weight_step(net, t):
-    if t < 9:
-        b, d = PIECES[t]
-        net.wz(b, d).wait_recv()
-        net.w1(b, d).start()
-        if t + WINDOW < 9:
-            net.wz(*PIECES[t + WINDOW]).start()
-    if 0 <= t - 1 < 9:
-        b, d = PIECES[t - 1]
-        net.w1(b, d).wait_recv()
-        net.w2(b, d, 0).start()
-        net.w2(b, d, 1).start()
-    if 0 <= t - 3 < 9:
-        b, d = PIECES[t - 3]
-        net.w2(b, d, 0).wait_recv()
-        net.w2(b, d, 1).wait_recv()
-        net.w3(b, d).start()
-    if 0 <= t - 4 < 9:
-        net.w3(*PIECES[t - 4]).wait_recv()
+def weight_own(net, b):
+    for way in (0, 1):
+        when(net.sends(way, 0), lambda: net.wz(b, way, 0).start())
+
+
+def weight_one(net, b, way, j):
+    def step():
+        net.wz(b, way, j).wait_recv()
+        if j < 2:
+            when(net.sends(way, j + 1), lambda: net.wz(b, way, j + 1).start())
+        net.w1(b, way, j).start()
+    when(net.receives(way, j), step)
+
+
+def weight_two(net, b, way, j):
+    def step():
+        net.w1(b, way, j).wait_recv()
+        net.w2(b, way, j, 0).start()
+        net.w2(b, way, j, 1).start()
+    when(net.receives(way, j), step)
+
+
+def weight_core(net, b, way, j):
+    def step():
+        net.w2(b, way, j, 0).wait_recv()
+        net.w2(b, way, j, 1).wait_recv()
+        net.w3(b, way, j).start()
+    when(net.receives(way, j), step)
+
+
+def weight_there(net, b, way, j):
+    when(net.receives(way, j), lambda: net.w3(b, way, j).wait_recv())
 
 
 def weights_sent(net):
-    for b, d in PIECES:
-        net.wz(b, d).wait_send()
-        net.w1(b, d).wait_send()
-        net.w2(b, d, 0).wait_send()
-        net.w2(b, d, 1).wait_send()
-        net.w3(b, d).wait_send()
+    for b in BLOCKS:
+        for way in (0, 1):
+            for j in range(3):
+                def step():
+                    net.w1(b, way, j).wait_send()
+                    net.w2(b, way, j, 0).wait_send()
+                    net.w2(b, way, j, 1).wait_send()
+                    net.w3(b, way, j).wait_send()
+                when(net.sends(way, j), lambda: net.wz(b, way, j).wait_send())
+                when(net.receives(way, j), step)
 
 
 def rows_own(net, a, part):
     for way in (0, 1):
-        when(net.sends(way, part), lambda: net.rows(a, way, part).start())
+        when(net.sends(way, 0), lambda: net.rows(a, way, part).start())
 
 
 def rows_next(net, a, way, n):
-    when(net.receives(way, n - 1), lambda: net.rows(a, way, n - 1).wait_recv())
-    if n + 1 < 6:
-        when(net.sends(way, n + 1), lambda: net.rows(a, way, n + 1).start())
+    when(net.receives(way, (n - 1) // 3), lambda: net.rows(a, way, n - 1).wait_recv())
+    if n + 2 < 9:
+        when(net.sends(way, (n + 2) // 3), lambda: net.rows(a, way, n + 2).start())
 
 
 def rows_sent(net, a):
-    for n in range(6):
+    for n in range(9):
         for way in (0, 1):
-            when(net.sends(way, n), lambda: net.rows(a, way, n).wait_send())
+            when(net.sends(way, n // 3), lambda: net.rows(a, way, n).wait_send())
 
 
 def add(net, b, p, e, ref):
@@ -686,7 +703,7 @@
     net.r1(b, p).start()
 
 
-def small_step(net, i):
+def small_sum(net, i):
     k, half = net.k, pl.ds(16 * net.c, 16)
     if i == 0:
         k.sgs[0] = k.sg[...]
@@ -700,64 +717,141 @@
         net.sg(i).start()
 
 
-STEPS = dict(
-    rows_own=rows_own, rows_next=rows_next, halves_out=halves_out, halves=halves, quarters=quarters, eighths=eighths,
-    chain=chain, over_z=over_z, around=around, to_core=to_core, small=small_step,
+PLAN = (
+    (
+        (weight_own, 0), (weight_own, 2), (weight_one, 0, 0, 0), (weight_one, 0, 1, 0), (weight_own, 1),
+        (weight_two, 0, 0, 0),
+    ),
+    (
+        (weight_one, 0, 1, 1), (weight_one, 0, 0, 1), (weight_two, 0, 1, 0), (weight_core, 0, 0, 0),
+        (weight_two, 0, 1, 1), (weight_one, 1, 0, 0), (weight_one, 0, 1, 2), (weight_one, 0, 0, 2),
+        (weight_two, 0, 0, 1), (weight_one, 1, 1, 0), (weight_two, 0, 0, 2), (weight_one, 2, 0, 0),
+        (weight_core, 0, 1, 0),
+    ),
+    (
+        (weight_one, 2, 0, 1), (weight_core, 0, 0, 1), (weight_there, 0, 0, 0), (weight_core, 0, 1, 1),
+        (weight_two, 0, 1, 2), (weight_core, 0, 0, 2), (weight_one, 1, 1, 1), (weight_one, 1, 1, 2),
+        (weight_one, 2, 1, 0), (weight_one, 1, 0, 1), (weight_two, 1, 0, 0), (weight_core, 0, 1, 2),
+    ),
+    (
+        (weight_there, 0, 1, 0),
+    ),
+    (
+        (weight_one, 2, 0, 2), (weight_two, 1, 1, 1), (weight_two, 2, 0, 0), (weight_there, 0, 0, 1),
+        (weight_two, 1, 1, 2), (weight_there, 0, 0, 2), (weight_one, 2, 1, 1), (weight_there, 0, 1, 1),
+        (weight_there, 0, 1, 2),
+    ),
+    (),
+    (),
+    (
+        (weight_core, 1, 0, 0), (weight_two, 2, 1, 0), (weight_two, 1, 1, 0), (weight_two, 2, 0, 2),
+        (weight_core, 1, 1, 1), (weight_one, 1, 0, 2), (weight_two, 1, 0, 1), (weight_two, 2, 0, 1),
+    ),
+    (),
+    (
+        (weight_core, 1, 1, 2),
+    ),
+    (),
+    (
+        (weight_core, 2, 0, 2), (weight_two, 1, 0, 2), (weight_core, 2, 0, 0), (weight_one, 2, 1, 2),
+        (weight_core, 2, 1, 0), (weight_two, 2, 1, 1),
+    ),
+    (
+        (weight_there, 2, 0, 2), (weight_there, 1, 0, 0), (weight_core, 1, 1, 0), (weight_two, 2, 1, 2),
+        (weight_core, 1, 0, 1), (weight_there, 1, 1, 2),
+    ),
+    (
+        (weight_there, 2, 0, 0), (weight_core, 2, 1, 1),
+    ),
+    (
+        (weight_there, 2, 1, 0), (weight_there, 1, 1, 1), (weight_core, 2, 0, 1),
+    ),
+    (
+        (weight_there, 1, 1, 0), (weight_core, 1, 0, 2),
+    ),
+    (),
+    (),
+    (
+        (weight_there, 1, 0, 1),
+    ),
+    (
+        (weight_there, 2, 1, 1), (weight_there, 2, 0, 1),
+    ),
+    (
+        (weight_core, 2, 1, 2),
+    ),
+    (),
+    (
+        (weight_there, 1, 0, 2),
+    ),
+    (),
+    (),
+    (
+        (weight_there, 2, 1, 2),
+    ),
+    (),
+    (
+        (rows_own, 0, 0),
+    ),
+    (
+        (rows_own, 0, 1),
+    ),
+    (),
+    (
+        (halves_out, 2, 3), (rows_own, 0, 2), (halves_out, 1, 3), (rows_next, 0, 0, 1),
+    ),
+    (
+        (halves_out, 1, 0), (rows_next, 0, 1, 1), (halves_out, 2, 0), (halves, 2, 3),
+    ),
+    (
+        (halves_out, 2, 2), (rows_next, 0, 0, 2), (halves_out, 1, 2), (halves, 1, 0), (halves, 1, 3),
+        (rows_next, 0, 1, 2),
+    ),
+    (
+        (rows_next, 0, 1, 3), (halves_out, 2, 1), (rows_next, 0, 1, 4), (halves_out, 1, 1), (rows_next, 0, 0, 3),
+        (rows_next, 0, 0, 4), (halves, 2, 0), (halves, 1, 2),
+    ),
+    (),
+    (
+        (quarters, 2, 0), (quarters, 2, 3),
+    ),
+    (),
+    (
+        (halves, 2, 1), (rows_next, 0, 1, 5),
+    ),
+    (),
+    (
+        (rows_next, 0, 1, 6), (rows_next, 0, 0, 5),
+    ),
+    (),
+    (),
+    (
+        (rows_own, 1, 0), (quarters, 1, 2), (small_sum, 0), (eighths, 2, 3), (halves, 2, 2),
+    ),
+    (
+        (rows_next, 0, 1, 7), (rows_own, 1, 1),
+    ),
+    (
+        (rows_own, 1, 2), (halves, 1, 1),
+    ),
+    (),
+    (
+        (halves_out, 0, 2), (quarters, 1, 0), (halves_out, 0, 3), (halves_out, 0, 0), (quarters, 1, 3),
+        (eighths, 2, 0), (rows_next, 0, 1, 8), (rows_next, 1, 1, 1), (quarters, 1, 1), (eighths, 1, 2),
+        (quarters, 2, 1), (halves, 0, 3), (rows_next, 1, 0, 1), (rows_next, 1, 1, 2), (eighths, 1, 0), (halves, 0, 2),
+        (eighths, 2, 1), (rows_next, 1, 0, 2), (quarters, 0, 3), (rows_next, 1, 0, 3), (halves, 0, 0),
+        (eighths, 1, 3), (halves_out, 0, 1), (rows_next, 1, 0, 4), (small_sum, 1), (eighths, 1, 1), (quarters, 2, 2),
+        (quarters, 0, 2), (chain, 2, 0), (eighths, 0, 3), (chain, 1, 2), (halves, 0, 1), (chain, 1, 0),
+        (rows_next, 0, 0, 6), (rows_next, 1, 1, 3), (chain, 1, 3), (quarters, 0, 0), (rows_next, 0, 1, 9),
+        (small_sum, 2), (chain, 1, 1), (chain, 2, 3), (chain, 2, 1), (eighths, 2, 2), (rows_next, 1, 1, 4),
+        (eighths, 0, 2), (quarters, 0, 1), (rows_next, 0, 0, 7), (chain, 0, 3), (chain, 2, 2), (rows_next, 1, 1, 5),
+        (chain, 0, 2), (eighths, 0, 0), (rows_next, 1, 0, 5), (over_z, 1), (chain, 0, 0), (eighths, 0, 1),
+        (over_z, 2), (around, 1), (chain, 0, 1), (small_sum, 3), (rows_next, 0, 0, 8), (around, 2), (over_z, 0),
+        (small_sum, 4), (to_core, 1), (rows_next, 1, 1, 6), (rows_next, 1, 1, 7), (around, 0), (rows_next, 0, 0, 9),
+        (rows_next, 1, 0, 6), (rows_next, 1, 1, 8), (to_core, 2), (rows_next, 1, 0, 7), (small_sum, 5), (to_core, 0),
+        (small_sum, 6), (rows_next, 1, 1, 9), (rows_next, 1, 0, 8), (rows_next, 1, 0, 9),
+    ),
 )
-PLAN = {
-    "n2a": [
-        ("rows_own", 0, 0),
-    ],
-    "n2b": [
-        ("rows_own", 0, 1),
-    ],
-    "fb0": [
-        ("halves_out", 1, 3),
-    ],
-    "fb1": [
-        ("halves_out", 2, 0), ("rows_next", 0, 0, 1), ("halves", 1, 3), ("halves_out", 1, 0),
-    ],
-    "fb2": [
-        ("halves_out", 2, 2), ("halves", 2, 0), ("rows_next", 0, 1, 1), ("halves_out", 2, 3),
-    ],
-    "fb3": [
-        ("halves_out", 1, 1), ("rows_next", 0, 1, 2), ("halves", 2, 2), ("halves", 1, 0), ("halves_out", 1, 2),
-        ("halves_out", 2, 1), ("rows_next", 0, 0, 2), ("quarters", 2, 0),
-    ],
-    "ab0": [
-        ("quarters", 2, 2), ("rows_next", 0, 1, 3), ("halves", 2, 3),
-    ],
-    "ab2": [
-        ("halves", 1, 1), ("rows_next", 0, 0, 3), ("eighths", 2, 2), ("halves", 1, 2),
-    ],
-    "gateb": [
-        ("chain", 2, 2),
-    ],
-    "gin": [
-        ("rows_own", 1, 0), ("quarters", 2, 3), ("quarters", 1, 0),
-    ],
-    "gin2": [
-        ("rows_next", 0, 1, 4), ("quarters", 1, 2),
-    ],
-    "gp0": [
-        ("halves_out", 0, 0), ("eighths", 2, 0), ("halves_out", 0, 1), ("halves", 2, 1), ("quarters", 1, 3),
-        ("small", 0), ("quarters", 1, 1), ("rows_own", 1, 1),
-    ],
-    "gp1": [
-        ("halves_out", 0, 2), ("halves", 0, 1), ("halves_out", 0, 3), ("rows_next", 1, 0, 1), ("eighths", 1, 2),
-        ("eighths", 1, 0), ("quarters", 2, 1), ("halves", 0, 3), ("rows_next", 1, 1, 1), ("rows_next", 1, 0, 2),
-        ("halves", 0, 0), ("small", 1), ("eighths", 2, 1), ("quarters", 0, 3), ("quarters", 0, 1), ("eighths", 1, 1),
-        ("halves", 0, 2), ("rows_next", 0, 1, 5), ("rows_next", 0, 1, 6), ("chain", 2, 0), ("chain", 1, 2),
-        ("eighths", 2, 3), ("quarters", 0, 0), ("rows_next", 0, 0, 4), ("chain", 1, 0), ("eighths", 0, 3),
-        ("small", 2), ("chain", 2, 1), ("eighths", 1, 3), ("rows_next", 1, 1, 2), ("eighths", 0, 1), ("chain", 2, 3),
-        ("rows_next", 1, 1, 3), ("quarters", 0, 2), ("eighths", 0, 0), ("over_z", 2), ("chain", 1, 1),
-        ("chain", 0, 3), ("chain", 0, 1), ("chain", 1, 3), ("eighths", 0, 2), ("around", 2), ("chain", 0, 2),
-        ("over_z", 1), ("rows_next", 1, 0, 3), ("chain", 0, 0), ("small", 3), ("to_core", 2), ("around", 1),
-        ("over_z", 0), ("small", 4), ("to_core", 1), ("rows_next", 1, 1, 4), ("rows_next", 1, 1, 5), ("around", 0),
-        ("rows_next", 0, 0, 5), ("rows_next", 1, 0, 4), ("rows_next", 1, 0, 5), ("small", 5), ("to_core", 0),
-        ("rows_next", 1, 1, 6), ("small", 6), ("rows_next", 1, 0, 6), ("rows_next", 0, 0, 6),
-    ],
-}
 
 
 def kernel(names, *refs):
@@ -775,84 +869,91 @@
     local = [pltpu.make_async_copy(src, dst, k.sem_in.at[i]) for i, (src, dst) in enumerate(moves)]
     for c in local:
         c.start()
+    run = lambda n: [step(net, *given) for step, *given in PLAN[n]]
     net.greet()
-    for c in local[0:4]:
-        c.wait()
-    for piece in PIECES[0:WINDOW]:
-        net.wz(*piece).start()
     k.tok[SEQ:PAD] = jnp.zeros((PAD - SEQ, D), bf16)
     k.cot[SEQ:PAD] = jnp.zeros((PAD - SEQ, D), bf16)
     k.sg[...] = jnp.zeros((32, BIAS), f32)
     k.factor[...] = jnp.zeros((16, PAD), f32)
+    k.fb[...] = jnp.zeros((PAD, D), f32)
+    for c in local[0:6]:
+        c.wait()
+    net.all_here()
+    run(0)
     own_small(k, z)
     for d in (1, 2, 3):
         net.sm(d).start()
-    for c in local[4:8]:
-        c.wait()
-    weight_step(net, 0)
+    run(1)
     mask_build(k, z)
-    weight_step(net, 1)
+    run(2)
     for d in (1, 2, 3):
         net.sm(d).wait_recv()
+    for c in local[6:8]:
+        c.wait()
     gates(k)
-    weight_step(net, 2)
+    run(3)
     bias_tables(k)
-    weight_step(net, 3)
-    weight_step(net, 4)
-    weight_step(net, 5)
-    weight_step(net, 6)
+    run(4)
     project(k)
+    run(5)
 
     def forward(pr):
         attend(k, pr)
-        when(pr == 1, lambda: weight_step(net, 7))
-        when(pr == 4, lambda: weight_step(net, 8))
+        for n in range(PAIRS):
+            when(pr == n, lambda: run(6 + n))
     loop(PAIRS, forward)
     norm_one(k)
-    weight_step(net, 9)
-    feed_init(k)
-
-    def layer_two(i):
-        when(i == 2, lambda: weight_step(net, 10))
-        when(i == 3, lambda: (weight_step(net, 11), weight_step(net, 12)))
-        feed(k, net.behind(i))
-    loop(4, layer_two)
+    run(12)
+
+    feed_in(k, z)
+    run(13)
+    feed_out(k, z)
+    run(14)
+    last = 3 - 3 * (z // 2)
+
+    def layer_two(n):
+        p = z + (2 * (n % 2) - 1) * (1 + n // 2)
+        when((p >= 0) & (p <= 3), lambda: feed_in(k, p))
+        for i in range(6):
+            when(n == i, lambda: run(15 + 2 * i))
+        when((p >= 0) & (p <= 3) & (p != last), lambda: feed_out(k, p))
+        for i in range(6):
+            when(n == i, lambda: run(16 + 2 * i))
+    loop(6, layer_two)
     here = [
         pltpu.make_async_copy(k.out.at[pl.ds(0, SEQ)], k.out_hbm.at[own_rows], k.sem_in.at[0]),
-        pltpu.make_async_copy(k.gtok.at[pl.ds(0, SEQ)], k.gtok_hbm.at[own_rows], k.sem_in.at[1]),
+        pltpu.make_async_copy(k.cot.at[pl.ds(0, SEQ)], k.gtok_hbm.at[own_rows], k.sem_in.at[1]),
     ]
-    run = lambda key: [STEPS[name](net, *given) for name, *given in PLAN.get(key, ())]
-    norm_two(k, 0)
-    run("n2a")
-    norm_two(k, 1)
-    run("n2b")
+    for part in range(3):
+        feed_out(k, last, *PARTS[part])
+        norm_two(k, part)
+        run(27 + part)
     here[0].start()
     weights_sent(net)
 
     def layer_two_back(i):
         feed_back(k, (1 - i % 2) * (3 - i // 2) + (i % 2) * (i // 2))
         for n in range(4):
-            when(i == n, lambda: run("fb" + str(n)))
+            when(i == n, lambda: run(30 + n))
     loop(4, layer_two_back)
     norm_one_back(k)
-    run("n1b")
+    run(34)
 
     def backward(pr):
         attend_back(k, pr)
         for n in range(PAIRS):
-            when(pr == n, lambda: run("ab" + str(n)))
+            when(pr == n, lambda: run(35 + n))
     loop(PAIRS, backward)
     gate_back(k)
-    run("gateb")
+    run(41)
     grad_input(k)
-    grad_rows(k, 0)
-    run("gin")
-    grad_rows(k, 1)
+    for part in range(3):
+        grad_rows(k, part)
+        run(42 + part)
     here[1].start()
-    run("gin2")
     for part in (0, 1):
         grad_projections(k, part)
-        run("gp" + str(part))
+        run(45 + part)
     k.fin[...] = jnp.zeros((16, BIAS), f32)
     k.fin[0:6, :] = k.sgs[5, 0:6, :]
     k.fin[6:7, :] = k.sgs[5, pl.ds(6 + z, 1), :]
@@ -879,13 +980,17 @@
     k = K()
     for name, ref in zip(names, rest):
         setattr(k, name, ref)
-    inward = [pltpu.make_async_copy(src, k.stage.at[i], k.sem.at[2 + i]) for i, src in enumerate((ri, ro, ra))]
-    for c in inward:
+    count = iter(range(64))
+    def copy(src, dst):
+        c = pltpu.make_async_copy(src, dst, k.sem.at[next(count)])
         c.start()
-    pairs = [(out, k.rows.at[0], k.output), (gtok, k.rows.at[1], k.grad_tokens)]
-    copies = [pltpu.make_async_copy(src, via, k.sem.at[i]) for i, (src, via, _) in enumerate(pairs)]
-    for c in copies:
-        c.start()
+        return c
+    parts = [pl.ds(4 * i, 4) for i in (0, 1)]
+    size = out.shape[0] // 4
+    inward = [[copy(src.at[part], k.stage.at[i, part]) for part in parts] for i, src in enumerate((ri, ro, ra))]
+    pairs = [(src, k.rows.at[i], dst) for i, (src, dst) in enumerate(((out, k.output), (gtok, k.grad_tokens)))]
+    moves = [(src.at[at], via.at[at], dst.at[at]) for src, via, dst in pairs for at in [pl.ds(size * i, size) for i in range(4)]]
+    copies = [copy(src, via) for src, via, _ in moves]
     row = lambda r, lane, n: sg[r : r + 1, lane : lane + n].reshape(n)
     k.b_out[...], k.norm1_gain[...], k.norm1_bias[...] = row(0, 0, D), row(1, 0, D), row(2, 0, D)
     k.b_outer[...], k.norm2_gain[...], k.norm2_bias[...] = row(3, 0, D), row(4, 0, D), row(5, 0, D)
@@ -901,23 +1006,23 @@
             heads = heads + cell(11 + i, 128 * pr)
         k.gate_weight[4 * i : 4 * i + 4, :] = jnp.broadcast_to(heads[:, 0:HEAD] + heads[:, HEAD:128], (4, HEAD))
     outward = []
-    for i, c in enumerate(inward):
-        c.wait()
-        def widen(j):
-            k.wide[i, j] = k.stage[i, j].astype(f32)
-        loop(8, widen)
-        if i < 2:
-            to = [(k.wide.at[i], (k.w_inner, k.w_outer)[i])]
-        else:
-            to = [(k.wide.at[i, pl.ds(2 * j, 2)], ref) for j, ref in enumerate((k.w_query, k.w_key, k.w_value, k.w_out))]
-        for src, dst in to:
-            copy = pltpu.make_async_copy(src, dst, k.sem.at[5 + len(outward)])
-            copy.start()
-            outward.append(copy)
-    for i, (c, (_, via, dst)) in enumerate(zip(copies, pairs)):
-        c.wait()
-        outward.append(pltpu.make_async_copy(via, dst, k.sem.at[i]))
-        outward[-1].start()
+    def pass_rows(n):
+        copies[n].wait()
+        outward.append(copy(moves[n][1], moves[n][2]))
+    for i in range(3):
+        for j in (0, 1):
+            inward[i][j].wait()
+            def widen(n):
+                k.wide[i, 4 * j + n] = k.stage[i, 4 * j + n].astype(f32)
+            loop(4, widen)
+            if i < 2:
+                outward.append(copy(k.wide.at[i, parts[j]], (k.w_inner, k.w_outer)[i].at[parts[j]]))
+            else:
+                for n, ref in enumerate(((k.w_query, k.w_key), (k.w_value, k.w_out))[j]):
+                    outward.append(copy(k.wide.at[i, pl.ds(4 * j + 2 * n, 2)], ref))
+            pass_rows(2 * i + j)
+    pass_rows(6)
+    pass_rows(7)
     for c in outward:
         c.wait()
 
@@ -988,7 +1093,7 @@
         in_specs=[anywhere] * 5 + [vmem],
         out_specs=list(specs),
         out_shape=list(shapes),
-        scratch_shapes=[pltpu.VMEM((3, 8, 96, D), bf16), pltpu.VMEM((3, 8, 96, D), f32), pltpu.VMEM((2, rows, D), bf16), pltpu.SemaphoreType.DMA((11,))],
+        scratch_shapes=[pltpu.VMEM((3, 8, 96, D), bf16), pltpu.VMEM((3, 8, 96, D), f32), pltpu.VMEM((2, rows, D), bf16), pltpu.SemaphoreType.DMA((40,))],
         compiler_params=pltpu.CompilerParams(vmem_limit_bytes=VMEM_LIMIT),
     )(out, gtok, ra, ri, ro, sg)
     r = dict(zip(FINAL, results))

time: 207 us -> 202 us (0.976)
  Pallas kernels: 206 us -> 201 us
    pallas_call x1, Pallas kernels: 196 us -> 192 us  [body(): pl.pallas_call(functools.partial(kernel, names), in_specs=[spec for spec,...]
where the time goes in v4:
time: 202 us
  Pallas kernels  201 us (100%)
    pallas_call x1, Pallas kernels, body(): pl.pallas_call(functools.partial(kernel, names), in_specs=[spec for spec,...  192 us
    pallas_call x1, Pallas kernels, body(): pl.pallas_call(finish_kernel, in_specs=[anywhere] * 5 + [vmem], out_specs...  9 us

profile of v4, /device:TPU:0, one launch (start us, length us, event | category | flops | bytes accessed | tf_op | source)
XLA Modules:
  0.0 202.1 jit_solution(7757660776789554008)
XLA Ops:
  0.7 192.2 %shard_map.382 = (bf16[1984,768]{1,0:T(8,128)(2,1)}, bf16[1984,768]{1,0:T(8,128)(2,1)}, bf16[8,96,768]{2,1,0:T(8,128)(2,1)}, bf16[8,96,768]{2,1,0:T(8,128)(2,1)}...) custom-call(s32[4]{0:T(128)} %refs_0_.1, s32[1,991]{1,0:T(1,128)} %bitcast.38, bf16[3,320]{1,0:T(4,128)(2,1)} %bitcast.39, ...), custom_call_target="tpu_custom_call" | custom-call | tf_op jit(solution)/shard_map/pallas_call | solution.py:1069
  192.9 9.0 %shard_map.383 = (bf16[1984,768]{1,0:T(8,128)(2,1)}, bf16[1984,768]{1,0:T(8,128)(2,1)}, f32[2,96,768]{2,1,0:T(8,128)}, f32[2,96,768]{2,1,0:T(8,128)}, f32[2,96,7...) custom-call(bf16[1984,768]{1,0:T(8,128)(2,1)} %get-tuple-element.48., ...), custom_call_target="tpu_custom_call" | custom-call | tf_op jit(solution)/shard_map/pallas_call | solution.py:1091

commit v5 on v4

--- a/solution.py
+++ b/solution.py
@@ -334,19 +334,21 @@
     gscale = jnp.sum(ggate * first * second, axis=1, keepdims=True)
     gw = dot(dz, k.tok[...].astype(f32), precision=highest)
     pick = lambda v: jnp.sum(jnp.where(own, v, 0.0), axis=0, keepdims=True)
-    k.sg[24:25, 0:D] = pick(gw[0:16])
-    k.sg[25:26, 0:D] = pick(gw[16:32])
-    k.sg[24:25, D:] = jnp.broadcast_to(jnp.sum(jnp.sum(df, axis=0, keepdims=True), axis=1, keepdims=True), (1, 256))
-    k.sg[25:26, D:] = jnp.broadcast_to(jnp.sum(jnp.sum(ds, axis=0, keepdims=True), axis=1, keepdims=True), (1, 256))
+    k.sg[14:15, 0:D] = pick(gw[0:16])
+    k.sg[15:16, 0:D] = pick(gw[16:32])
+    k.sg[14:15, D:] = jnp.broadcast_to(jnp.sum(jnp.sum(df, axis=0, keepdims=True), axis=1, keepdims=True), (1, 256))
+    k.sg[15:16, D:] = jnp.broadcast_to(jnp.sum(jnp.sum(ds, axis=0, keepdims=True), axis=1, keepdims=True), (1, 256))
     goff = jnp.concatenate([k.goff[h] for h in range(HEADS)] + [jnp.zeros((4, BIAS), f32)], axis=0)
     rel = dot_t(goff, k.hot[...].astype(f32), precision=highest)
-    k.sg[12:24, 0:NB] = rel[0:HEADS]
-    k.sg[12:24, 512:640] = jnp.broadcast_to(gscale, (16, 128))[0:HEADS]
+    for h in range(HEADS):
+        at, i = 10 + h // 3, h % 3
+        k.sg[at : at + 1, NB * i : NB * i + NB] = rel[h : h + 1]
+        k.sg[at : at + 1, 960 + i : 961 + i] = gscale[h : h + 1]
     for t, src in ((0, k.q), (2, k.v)):
         row = jnp.sum(fold(mixed_all(src).astype(f32)), axis=0, keepdims=True)
         for p in range(4):
-            at, lane = (6 + p, D) if t == 0 else (12 + 3 * p, 640)
-            k.sg[at : at + 1, lane : lane + 192] = row[:, 192 * p : 192 * p + 192]
+            at = 6 + p if t == 0 else p
+            k.sg[at : at + 1, D : D + 192] = row[:, 192 * p : 192 * p + 192]
     k.fa[...] = dot(dz.T, weights)
 
 
@@ -385,20 +387,21 @@
     fa=((PAD, D), f32), fb=((PAD, D), f32), n1=((PAD, D), f32), inv1=((PAD, 128), f32), hid=((PAD, D), bf16),
     act=((4, PAD, D), bf16), dg=((4, PAD, D), bf16), out=((PAD, D), bf16), gb=((PAD, D), bf16),
     gs=((PAD, PAD), bf16), a=((128, BIAS), f32), ggate=((HEADS, 1, PAD), f32),
-    goff=((HEADS, 1, BIAS), f32), sg=((32, BIAS), f32),
+    goff=((HEADS, 1, BIAS), f32), sg=((16, BIAS), f32),
     wa=((4, 4, 2, 96, D), bf16), wi=((4, 8, 96, D), bf16), wo=((4, 8, 96, D), bf16),
 )
 
 
 MESH = pl.DeviceIdType.MESH
 BLOCKS = (0, 1, 2)
+WIDE = (2,)
 SEMS = dict(
-    wz=(3, 2, 3), w1=(3, 2, 3), w2=(3, 2, 3, 2), w3=(3, 2, 3), sm=(3,), rows=(2, 2, 9), r1=(3, 4), r2=(3, 4, 2), r3=(3, 4),
+    wz=(3, 2, 3, 2), w1=(3, 2, 3), w2=(3, 2, 3, 2), w3=(3, 2, 3), sm=(3,), rows=(2, 2, 9), r1=(3, 4), r2=(3, 4, 2), r3=(3, 4),
     r4=(3, 2, 3), a1=(3,), a2=(3, 2), a3=(3,), sg=(6,),
 )
 COMM_SCRATCH = dict(
     rb1a=((4, 2, 2, 96, D), bf16), rb1=((2, 4, 4, 96, D), bf16), rb2=((3, 4, 2, 96, D), bf16),
-    rb3=((3, 4, 96, D), bf16), rb4=((3, 2, 3, 96, D), bf16), sgr=((5, 32, BIAS), f32), sgs=((6, 32, BIAS), f32), fin=((16, BIAS), f32),
+    rb3=((3, 4, 96, D), bf16), rb4=((3, 2, 3, 96, D), bf16), sgr=((5, 16, BIAS), f32), sgs=((6, 16, BIAS), f32), fin=((16, BIAS), f32),
 )
 
 
@@ -455,9 +458,9 @@
     def plane(self, way, j):
         return self.z - 1 - j if way == 0 else self.z + 1 + j
 
-    def wz(self, b, way, j):
-        ref = self.chunk(b, self.plane(way, j - 1), self.e)
-        return self.copy("wz", (b, way, j), ref, ref, (self.dp, self.z + 1 if way == 0 else self.z - 1))
+    def wz(self, b, way, j, i=0):
+        ref = self.chunk(b, self.plane(way, j - 1), (self.e, self.e1)[i])
+        return self.copy("wz", (b, way, j, i), ref, ref, (self.dp, self.z + 1 if way == 0 else self.z - 1))
 
     def w1(self, b, way, j):
         ref = self.chunk(b, self.plane(way, j), self.e)
@@ -522,7 +525,7 @@
         return self.copy("a3", (b,), ref, ref, self.core)
 
     def sg(self, i):
-        k, half = self.k, pl.ds(16 * self.c, 16)
+        k, half = self.k, pl.ds(8 * self.c, 8)
         if i < 3:
             return self.copy("sg", (i,), k.sgs.at[i], k.sgr.at[i], (self.core, self.x, self.y)[i])
         if i < 5:
@@ -552,21 +555,25 @@
 
 def weight_own(net, b):
     for way in (0, 1):
-        when(net.sends(way, 0), lambda: net.wz(b, way, 0).start())
+        for i in range(1 + (b in WIDE)):
+            when(net.sends(way, 0), lambda: net.wz(b, way, 0, i).start())
 
 
 def weight_one(net, b, way, j):
     def step():
-        net.wz(b, way, j).wait_recv()
-        if j < 2:
-            when(net.sends(way, j + 1), lambda: net.wz(b, way, j + 1).start())
-        net.w1(b, way, j).start()
+        for i in range(1 + (b in WIDE)):
+            net.wz(b, way, j, i).wait_recv()
+            if j < 2:
+                when(net.sends(way, j + 1), lambda: net.wz(b, way, j + 1, i).start())
+        if b not in WIDE:
+            net.w1(b, way, j).start()
     when(net.receives(way, j), step)
 
 
 def weight_two(net, b, way, j):
     def step():
-        net.w1(b, way, j).wait_recv()
+        if b not in WIDE:
+            net.w1(b, way, j).wait_recv()
         net.w2(b, way, j, 0).start()
         net.w2(b, way, j, 1).start()
     when(net.receives(way, j), step)
@@ -588,13 +595,17 @@
     for b in BLOCKS:
         for way in (0, 1):
             for j in range(3):
-                def step():
-                    net.w1(b, way, j).wait_send()
+                def along():
+                    for i in range(1 + (b in WIDE)):
+                        net.wz(b, way, j, i).wait_send()
+                def inside():
+                    if b not in WIDE:
+                        net.w1(b, way, j).wait_send()
                     net.w2(b, way, j, 0).wait_send()
                     net.w2(b, way, j, 1).wait_send()
                     net.w3(b, way, j).wait_send()
-                when(net.sends(way, j), lambda: net.wz(b, way, j).wait_send())
-                when(net.receives(way, j), step)
+                when(net.sends(way, j), along)
+                when(net.receives(way, j), inside)
 
 
 def rows_own(net, a, part):
@@ -704,7 +715,7 @@
 
 
 def small_sum(net, i):
-    k, half = net.k, pl.ds(16 * net.c, 16)
+    k, half = net.k, pl.ds(8 * net.c, 8)
     if i == 0:
         k.sgs[0] = k.sg[...]
     else:
@@ -719,73 +730,70 @@
 
 PLAN = (
     (
-        (weight_own, 0), (weight_own, 2), (weight_one, 0, 0, 0), (weight_one, 0, 1, 0), (weight_own, 1),
-        (weight_two, 0, 0, 0),
-    ),
-    (
-        (weight_one, 0, 1, 1), (weight_one, 0, 0, 1), (weight_two, 0, 1, 0), (weight_core, 0, 0, 0),
-        (weight_two, 0, 1, 1), (weight_one, 1, 0, 0), (weight_one, 0, 1, 2), (weight_one, 0, 0, 2),
-        (weight_two, 0, 0, 1), (weight_one, 1, 1, 0), (weight_two, 0, 0, 2), (weight_one, 2, 0, 0),
-        (weight_core, 0, 1, 0),
-    ),
-    (
-        (weight_one, 2, 0, 1), (weight_core, 0, 0, 1), (weight_there, 0, 0, 0), (weight_core, 0, 1, 1),
-        (weight_two, 0, 1, 2), (weight_core, 0, 0, 2), (weight_one, 1, 1, 1), (weight_one, 1, 1, 2),
-        (weight_one, 2, 1, 0), (weight_one, 1, 0, 1), (weight_two, 1, 0, 0), (weight_core, 0, 1, 2),
-    ),
-    (
-        (weight_there, 0, 1, 0),
-    ),
-    (
-        (weight_one, 2, 0, 2), (weight_two, 1, 1, 1), (weight_two, 2, 0, 0), (weight_there, 0, 0, 1),
-        (weight_two, 1, 1, 2), (weight_there, 0, 0, 2), (weight_one, 2, 1, 1), (weight_there, 0, 1, 1),
-        (weight_there, 0, 1, 2),
-    ),
-    (),
-    (),
-    (
-        (weight_core, 1, 0, 0), (weight_two, 2, 1, 0), (weight_two, 1, 1, 0), (weight_two, 2, 0, 2),
-        (weight_core, 1, 1, 1), (weight_one, 1, 0, 2), (weight_two, 1, 0, 1), (weight_two, 2, 0, 1),
-    ),
-    (),
-    (
-        (weight_core, 1, 1, 2),
-    ),
-    (),
-    (
-        (weight_core, 2, 0, 2), (weight_two, 1, 0, 2), (weight_core, 2, 0, 0), (weight_one, 2, 1, 2),
-        (weight_core, 2, 1, 0), (weight_two, 2, 1, 1),
-    ),
-    (
-        (weight_there, 2, 0, 2), (weight_there, 1, 0, 0), (weight_core, 1, 1, 0), (weight_two, 2, 1, 2),
-        (weight_core, 1, 0, 1), (weight_there, 1, 1, 2),
-    ),
-    (
-        (weight_there, 2, 0, 0), (weight_core, 2, 1, 1),
-    ),
-    (
-        (weight_there, 2, 1, 0), (weight_there, 1, 1, 1), (weight_core, 2, 0, 1),
-    ),
-    (
-        (weight_there, 1, 1, 0), (weight_core, 1, 0, 2),
-    ),
-    (),
-    (),
-    (
-        (weight_there, 1, 0, 1),
-    ),
-    (
-        (weight_there, 2, 1, 1), (weight_there, 2, 0, 1),
-    ),
-    (
-        (weight_core, 2, 1, 2),
-    ),
-    (),
-    (
-        (weight_there, 1, 0, 2),
-    ),
-    (),
-    (),
+        (weight_own, 0), (weight_own, 1),
+    ),
+    (),
+    (
+        (weight_one, 0, 1, 0), (weight_one, 0, 0, 0), (weight_one, 1, 0, 0), (weight_two, 0, 1, 0),
+        (weight_one, 0, 1, 1), (weight_one, 0, 0, 1), (weight_one, 1, 1, 0), (weight_two, 0, 0, 0), (weight_own, 2),
+        (weight_core, 0, 1, 0), (weight_one, 0, 1, 2), (weight_two, 0, 1, 1), (weight_two, 0, 0, 1),
+        (weight_one, 0, 0, 2), (weight_two, 1, 0, 0), (weight_two, 0, 1, 2),
+    ),
+    (
+        (weight_core, 0, 0, 0), (weight_two, 0, 0, 2), (weight_one, 1, 0, 1), (weight_there, 0, 1, 0),
+    ),
+    (
+        (weight_one, 1, 1, 1), (weight_two, 1, 1, 0), (weight_core, 0, 0, 1), (weight_core, 0, 1, 1),
+        (weight_one, 2, 0, 0), (weight_one, 2, 1, 0), (weight_core, 0, 1, 2), (weight_there, 0, 1, 1),
+        (weight_one, 1, 0, 2), (weight_core, 0, 0, 2), (weight_there, 0, 0, 1), (weight_two, 2, 1, 0),
+        (weight_there, 0, 0, 0), (weight_there, 0, 1, 2), (weight_core, 1, 0, 0), (weight_one, 1, 1, 2),
+        (weight_two, 2, 0, 0), (weight_two, 1, 0, 2), (weight_two, 1, 0, 1), (weight_there, 0, 0, 2),
+    ),
+    (
+        (weight_two, 1, 1, 1),
+    ),
+    (
+        (weight_core, 1, 1, 0),
+    ),
+    (
+        (weight_one, 2, 1, 1), (weight_two, 2, 1, 1), (weight_one, 2, 0, 1), (weight_two, 1, 1, 2),
+    ),
+    (
+        (weight_core, 1, 0, 2), (weight_core, 2, 1, 0), (weight_two, 2, 0, 1),
+    ),
+    (),
+    (),
+    (
+        (weight_one, 2, 1, 2), (weight_two, 2, 1, 2), (weight_core, 1, 0, 1), (weight_one, 2, 0, 2),
+        (weight_two, 2, 0, 2), (weight_core, 2, 0, 0), (weight_there, 1, 0, 2), (weight_core, 1, 1, 1),
+    ),
+    (
+        (weight_there, 1, 0, 1), (weight_core, 2, 0, 1), (weight_core, 2, 1, 1),
+    ),
+    (),
+    (
+        (weight_core, 2, 0, 2), (weight_there, 1, 0, 0), (weight_there, 1, 1, 0), (weight_there, 2, 1, 0),
+    ),
+    (
+        (weight_core, 2, 1, 2), (weight_there, 1, 1, 1), (weight_there, 2, 0, 0),
+    ),
+    (
+        (weight_core, 1, 1, 2), (weight_there, 2, 0, 1),
+    ),
+    (),
+    (),
+    (
+        (weight_there, 2, 0, 2),
+    ),
+    (
+        (weight_there, 2, 1, 1),
+    ),
+    (),
+    (),
+    (),
+    (
+        (weight_there, 1, 1, 2),
+    ),
     (
         (weight_there, 2, 1, 2),
     ),
@@ -798,58 +806,59 @@
     ),
     (),
     (
-        (halves_out, 2, 3), (rows_own, 0, 2), (halves_out, 1, 3), (rows_next, 0, 0, 1),
-    ),
-    (
-        (halves_out, 1, 0), (rows_next, 0, 1, 1), (halves_out, 2, 0), (halves, 2, 3),
-    ),
-    (
-        (halves_out, 2, 2), (rows_next, 0, 0, 2), (halves_out, 1, 2), (halves, 1, 0), (halves, 1, 3),
-        (rows_next, 0, 1, 2),
-    ),
-    (
-        (rows_next, 0, 1, 3), (halves_out, 2, 1), (rows_next, 0, 1, 4), (halves_out, 1, 1), (rows_next, 0, 0, 3),
-        (rows_next, 0, 0, 4), (halves, 2, 0), (halves, 1, 2),
-    ),
-    (),
-    (
-        (quarters, 2, 0), (quarters, 2, 3),
-    ),
-    (),
-    (
-        (halves, 2, 1), (rows_next, 0, 1, 5),
-    ),
-    (),
-    (
-        (rows_next, 0, 1, 6), (rows_next, 0, 0, 5),
-    ),
-    (),
-    (),
-    (
-        (rows_own, 1, 0), (quarters, 1, 2), (small_sum, 0), (eighths, 2, 3), (halves, 2, 2),
-    ),
-    (
-        (rows_next, 0, 1, 7), (rows_own, 1, 1),
-    ),
-    (
-        (rows_own, 1, 2), (halves, 1, 1),
-    ),
-    (),
-    (
-        (halves_out, 0, 2), (quarters, 1, 0), (halves_out, 0, 3), (halves_out, 0, 0), (quarters, 1, 3),
-        (eighths, 2, 0), (rows_next, 0, 1, 8), (rows_next, 1, 1, 1), (quarters, 1, 1), (eighths, 1, 2),
-        (quarters, 2, 1), (halves, 0, 3), (rows_next, 1, 0, 1), (rows_next, 1, 1, 2), (eighths, 1, 0), (halves, 0, 2),
-        (eighths, 2, 1), (rows_next, 1, 0, 2), (quarters, 0, 3), (rows_next, 1, 0, 3), (halves, 0, 0),
-        (eighths, 1, 3), (halves_out, 0, 1), (rows_next, 1, 0, 4), (small_sum, 1), (eighths, 1, 1), (quarters, 2, 2),
-        (quarters, 0, 2), (chain, 2, 0), (eighths, 0, 3), (chain, 1, 2), (halves, 0, 1), (chain, 1, 0),
-        (rows_next, 0, 0, 6), (rows_next, 1, 1, 3), (chain, 1, 3), (quarters, 0, 0), (rows_next, 0, 1, 9),
-        (small_sum, 2), (chain, 1, 1), (chain, 2, 3), (chain, 2, 1), (eighths, 2, 2), (rows_next, 1, 1, 4),
-        (eighths, 0, 2), (quarters, 0, 1), (rows_next, 0, 0, 7), (chain, 0, 3), (chain, 2, 2), (rows_next, 1, 1, 5),
-        (chain, 0, 2), (eighths, 0, 0), (rows_next, 1, 0, 5), (over_z, 1), (chain, 0, 0), (eighths, 0, 1),
-        (over_z, 2), (around, 1), (chain, 0, 1), (small_sum, 3), (rows_next, 0, 0, 8), (around, 2), (over_z, 0),
-        (small_sum, 4), (to_core, 1), (rows_next, 1, 1, 6), (rows_next, 1, 1, 7), (around, 0), (rows_next, 0, 0, 9),
-        (rows_next, 1, 0, 6), (rows_next, 1, 1, 8), (to_core, 2), (rows_next, 1, 0, 7), (small_sum, 5), (to_core, 0),
-        (small_sum, 6), (rows_next, 1, 1, 9), (rows_next, 1, 0, 8), (rows_next, 1, 0, 9),
+        (rows_own, 0, 2), (halves_out, 2, 3), (halves_out, 1, 3),
+    ),
+    (
+        (halves_out, 2, 0), (rows_next, 0, 1, 1), (rows_next, 0, 0, 1), (halves_out, 1, 0), (halves, 2, 3),
+    ),
+    (
+        (halves_out, 1, 2), (halves_out, 2, 2), (rows_next, 0, 1, 2), (halves, 1, 3), (halves, 2, 0),
+        (rows_next, 0, 0, 2),
+    ),
+    (
+        (rows_next, 0, 0, 3), (halves_out, 1, 1), (halves, 1, 0), (halves, 2, 2), (rows_next, 0, 1, 3),
+    ),
+    (
+        (rows_next, 0, 1, 4), (halves, 1, 2), (rows_next, 0, 1, 5),
+    ),
+    (),
+    (
+        (rows_next, 0, 0, 4),
+    ),
+    (
+        (halves, 1, 1), (rows_next, 0, 1, 6),
+    ),
+    (
+        (rows_next, 0, 0, 5),
+    ),
+    (),
+    (),
+    (),
+    (
+        (rows_own, 1, 0), (quarters, 2, 0), (small_sum, 0),
+    ),
+    (
+        (rows_next, 0, 0, 6), (quarters, 1, 0), (halves_out, 2, 1), (rows_own, 1, 1), (quarters, 2, 3),
+    ),
+    (),
+    (
+        (halves_out, 0, 0), (quarters, 1, 3), (quarters, 1, 1), (halves_out, 0, 1),
+    ),
+    (
+        (halves_out, 0, 2), (rows_own, 1, 2), (quarters, 1, 2), (halves, 0, 0), (rows_next, 1, 0, 1), (eighths, 1, 0),
+        (halves, 2, 1), (rows_next, 1, 1, 1), (rows_next, 1, 1, 2), (halves_out, 0, 3), (rows_next, 0, 0, 7),
+        (quarters, 0, 0), (eighths, 2, 3), (eighths, 2, 0), (eighths, 1, 3), (halves, 0, 1), (quarters, 2, 2),
+        (quarters, 2, 1), (eighths, 1, 1), (small_sum, 1), (eighths, 0, 0), (rows_next, 1, 0, 2), (halves, 0, 3),
+        (eighths, 1, 2), (rows_next, 1, 0, 3), (rows_next, 0, 1, 7), (quarters, 0, 1), (chain, 2, 0),
+        (rows_next, 1, 0, 4), (halves, 0, 2), (chain, 1, 0), (chain, 1, 2), (eighths, 2, 1), (eighths, 2, 2),
+        (small_sum, 2), (chain, 0, 0), (chain, 1, 1), (chain, 2, 1), (chain, 1, 3), (quarters, 0, 3), (eighths, 0, 1),
+        (rows_next, 1, 1, 3), (rows_next, 1, 1, 4), (quarters, 0, 2), (over_z, 1), (chain, 2, 3), (small_sum, 3),
+        (chain, 0, 1), (rows_next, 0, 0, 8), (eighths, 0, 3), (eighths, 0, 2), (chain, 2, 2), (rows_next, 1, 1, 5),
+        (over_z, 2), (around, 1), (chain, 0, 3), (rows_next, 1, 0, 5), (rows_next, 1, 0, 6), (around, 2),
+        (small_sum, 4), (chain, 0, 2), (over_z, 0), (rows_next, 1, 1, 6), (rows_next, 1, 1, 7), (rows_next, 0, 1, 8),
+        (to_core, 1), (rows_next, 0, 1, 9), (to_core, 2), (around, 0), (rows_next, 1, 1, 8), (rows_next, 0, 0, 9),
+        (small_sum, 5), (to_core, 0), (small_sum, 6), (rows_next, 1, 0, 7), (rows_next, 1, 1, 9),
+        (rows_next, 1, 0, 8), (rows_next, 1, 0, 9),
     ),
 )
 
@@ -873,7 +882,7 @@
     net.greet()
     k.tok[SEQ:PAD] = jnp.zeros((PAD - SEQ, D), bf16)
     k.cot[SEQ:PAD] = jnp.zeros((PAD - SEQ, D), bf16)
-    k.sg[...] = jnp.zeros((32, BIAS), f32)
+    k.sg[...] = jnp.zeros((16, BIAS), f32)
     k.factor[...] = jnp.zeros((16, PAD), f32)
     k.fb[...] = jnp.zeros((PAD, D), f32)
     for c in local[0:6]:
@@ -956,10 +965,9 @@
         run(45 + part)
     k.fin[...] = jnp.zeros((16, BIAS), f32)
     k.fin[0:6, :] = k.sgs[5, 0:6, :]
-    k.fin[6:7, :] = k.sgs[5, pl.ds(6 + z, 1), :]
-    for i in range(3):
-        k.fin[8 + i : 9 + i, :] = k.sgs[5, pl.ds(12 + 3 * z + i, 1), :]
-    k.fin[11:13, :] = k.sgs[5, 24:26, :]
+    for at, start in ((6, 6), (7, 10), (8, 0)):
+        k.fin[at : at + 1, :] = k.sgs[5, pl.ds(start + z, 1), :]
+    k.fin[9:11, :] = k.sgs[5, 14:16, :]
     finish = pltpu.make_async_copy(k.fin, k.sg_hbm, k.sem_in.at[2])
     finish.start()
     for b in (2, 1, 0):
@@ -994,16 +1002,17 @@
     row = lambda r, lane, n: sg[r : r + 1, lane : lane + n].reshape(n)
     k.b_out[...], k.norm1_gain[...], k.norm1_bias[...] = row(0, 0, D), row(1, 0, D), row(2, 0, D)
     k.b_outer[...], k.norm2_gain[...], k.norm2_bias[...] = row(3, 0, D), row(4, 0, D), row(5, 0, D)
-    k.b_inner[...], k.b_query[...], k.b_value[...] = row(6, 0, D), row(6, D, 192), row(8, 640, 192)
-    k.rel_table[...] = sg[8:11, 0:NB]
+    k.b_inner[...], k.b_query[...], k.b_value[...] = row(6, 0, D), row(6, D, 192), row(8, D, 192)
+    for i in range(3):
+        k.rel_table[i : i + 1, :] = sg[7:8, NB * i : NB * i + NB]
     lane = lax.broadcasted_iota(jnp.int32, (1, 128), 1)
     cell = lambda r, at: sg[r : r + 1, at : at + 128]
-    k.gate_scale[...] = jnp.where(lane == 0, cell(8, 512), jnp.where(lane == 1, cell(9, 512), cell(10, 512)))[:, 0:3]
-    k.gate_bias[...] = jnp.where(lane < 4, cell(11, D), cell(12, D))[:, 0:8]
+    k.gate_scale[...] = sg[7:8, 960:963]
+    k.gate_bias[...] = jnp.where(lane < 4, cell(9, D), cell(10, D))[:, 0:8]
     for i in (0, 1):
-        heads = cell(11 + i, 0)
+        heads = cell(9 + i, 0)
         for pr in range(1, PAIRS):
-            heads = heads + cell(11 + i, 128 * pr)
+            heads = heads + cell(9 + i, 128 * pr)
         k.gate_weight[4 * i : 4 * i + 4, :] = jnp.broadcast_to(heads[:, 0:HEAD] + heads[:, HEAD:128], (4, HEAD))
     outward = []
     def pass_rows(n):

time: 202 us -> 192 us (0.950)
  Pallas kernels: 201 us -> 190 us
    pallas_call x1, Pallas kernels: 192 us -> 181 us  [body(): pl.pallas_call(functools.partial(kernel, names), in_specs=[spec for spec,...]
where the time goes in v5:
time: 192 us; the launch traced here: 191 us
  Pallas kernels  190 us (99%)
    pallas_call x1, Pallas kernels, body(): pl.pallas_call(functools.partial(kernel, names), in_specs=[spec for spec,...  181 us
    pallas_call x1, Pallas kernels, body(): pl.pallas_call(finish_kernel, in_specs=[anywhere] * 5 + [vmem], out_specs...  9 us

profile of v5, /device:TPU:0, one launch (start us, length us, event | category | flops | bytes accessed | tf_op | source)
XLA Modules:
  0.0 191.0 jit_solution(5236296392963853947)
XLA Ops:
  0.7 181.1 %shard_map.382 = (bf16[1984,768]{1,0:T(8,128)(2,1)}, bf16[1984,768]{1,0:T(8,128)(2,1)}, bf16[8,96,768]{2,1,0:T(8,128)(2,1)}, bf16[8,96,768]{2,1,0:T(8,128)(2,1)}...) custom-call(s32[4]{0:T(128)} %refs_0_.1, s32[1,991]{1,0:T(1,128)} %bitcast.38, bf16[3,320]{1,0:T(4,128)(2,1)} %bitcast.39, ...), custom_call_target="tpu_custom_call" | custom-call | tf_op jit(solution)/shard_map/pallas_call | solution.py:1078
  181.8 9.0 %shard_map.383 = (bf16[1984,768]{1,0:T(8,128)(2,1)}, bf16[1984,768]{1,0:T(8,128)(2,1)}, f32[2,96,768]{2,1,0:T(8,128)}, f32[2,96,768]{2,1,0:T(8,128)}, f32[2,96,7...) custom-call(bf16[1984,768]{1,0:T(8,128)(2,1)} %get-tuple-element.48., ...), custom_call_target="tpu_custom_call" | custom-call | tf_op jit(solution)/shard_map/pallas_call | solution.py:1100
